TPU v7x, 512 devices: a whole 4x8x8 slice. The times are simulated.
512 devices in a mesh: lat: 8 (over x, y_lo), lon: 16 (over z, core), ch: 4 (over y_hi).
Axes of the slice: x: 4, y: 8 (y_hi: 4, y_lo: 2; y = y_hi * 2 + y_lo), z: 8, core: 2. Of those that a mesh axis runs over, the one named last changes fastest.
Arguments:
- features: bfloat16 [1, 56, 384, 1024], P(None, 'lat', 'lon', 'ch'), may hold values from -6 to 6
- kernel_one: bfloat16 [3, 3, 4, 256, 1024], P(None, None, 'ch', 'lon'), may hold values from -0.0625 to 0.0625
- bias_one: float32 [1024], P('ch'), may hold values from -3 to 3
- kernel_two: bfloat16 [3, 3, 4, 256, 1024], P(None, None, 'ch', 'lon'), may hold values from -0.0625 to 0.0625
- bias_two: float32 [1024], P('ch'), may hold values from -3 to 3
Outputs:
- outputs: bfloat16 [1, 56, 384, 1024], P(None, 'lat', 'lon', 'ch')
All inputs are finite; a program needn't handle non-finite values.
Results may differ from a plain program's by a relative error of at most 0.01.
Values may be sent and summed in bfloat16 or wider, within the bound.
No kernel may reach another device: no remote copies, remote signals or barrier semaphores. Data moves between devices by JAX's collectives and lax.ppermute only.
A program may use at most 64 MiB of HBM per device.

v0:
```python
import jax
import jax.numpy as jnp
from jax import lax
from jax.sharding import PartitionSpec as P

skip_scale = 0.7071067811865476


def extended(array, sides, width, wrap):
    for axis, dim in sides:
        peers, length = (lax.axis_size(axis), array.shape[dim])
        up = [(i, (i + 1) % peers) for i in range(peers if wrap else peers - 1)]
        down = [(j, i) for i, j in up]
        last = lax.slice_in_dim(array, length - width, length, axis=dim)
        leading = lax.slice_in_dim(array, 0, width, axis=dim)
        before = lax.ppermute(last, axis, up)
        after = lax.ppermute(leading, axis, down)
        array = jnp.concatenate([before, array, after], axis=dim)
    return array


def shifted(block, axis, distance):
    devices = range(lax.axis_size(axis))
    route = [((i - distance) % len(devices), i) for i in devices]
    return lax.ppermute(block, axis, route)


def apply_taps(padded, kernel):
    count_items = padded.shape[0]
    height = padded.shape[1] - 2
    breadth = padded.shape[2] - 2
    channels = padded.shape[3]
    accumulated = jnp.zeros((count_items * height * breadth, kernel.shape[3]), jnp.float32)
    for row_off in range(3):
        for col_off in range(3):
            window = padded[:, row_off : row_off + height, col_off : col_off + breadth].reshape(
                -1, channels
            )
            accumulated = accumulated + jnp.dot(
                window, kernel[row_off, col_off], preferred_element_type=jnp.float32
            )
    return accumulated.reshape(count_items, height, breadth, kernel.shape[3])


def fold_pad(source):
    north_south = extended(source, (("lat", 1),), 1, False)
    pole_pair = jnp.concatenate([source[:, :1], source[:, -1:]], axis=1)
    pole_pair = shifted(pole_pair, "lon", lax.axis_size("lon") // 2)
    band_idx = lax.axis_index("lat")
    first_row = jnp.where(band_idx == 0, pole_pair[:, :1], north_south[:, :1])
    last_row = jnp.where(
        band_idx == lax.axis_size("lat") - 1, pole_pair[:, 1:], north_south[:, -1:]
    )
    banded = jnp.concatenate([first_row, north_south[:, 1:-1], last_row], axis=1)
    return extended(banded, (("lon", 2),), 1, True)


def conv_sum(activation, kernel, bias_vec):
    padded = fold_pad(activation)
    out_width = kernel.shape[4]
    piece = lax.all_gather(kernel, "lon", axis=3, tiled=True)
    count_rows = piece.shape[3]
    partial_value = apply_taps(padded, piece.reshape(3, 3, count_rows, out_width)).astype(
        jnp.bfloat16
    )
    partial_value = lax.optimization_barrier(partial_value).astype(jnp.float32)
    width_group = activation.shape[3]
    summed = lax.psum(partial_value.astype(jnp.bfloat16), "ch").astype(jnp.float32)
    summed = lax.dynamic_slice_in_dim(summed, lax.axis_index("ch") * width_group, width_group, 3)
    return summed + bias_vec


def body(features, kernel_one, bias_one, kernel_two, bias_two):
    act_zero = jax.nn.silu(features.astype(jnp.float32)).astype(jnp.bfloat16)
    hidden = conv_sum(act_zero, kernel_one, bias_one)
    act_one = jax.nn.silu(hidden).astype(jnp.bfloat16)
    second = conv_sum(act_one, kernel_two, bias_two)
    return ((features.astype(jnp.float32) + second) * skip_scale).astype(jnp.bfloat16)


def solution(mesh):
    placed = (
        P(None, "lat", "lon", "ch"),
        P(None, None, "ch", "lon", None),
        P("ch"),
        P(None, None, "ch", "lon", None),
        P("ch"),
    )
    return jax.shard_map(
        body, mesh=mesh, in_specs=placed, out_specs=P(None, "lat", "lon", "ch"), check_vma=False
    )
```

profile of v0, /device:TPU:2, one launch (start us, length us, event | category | flops | bytes accessed | tf_op | source)
XLA Modules:
  0.0 239.8 jit_solution(6033416910952092760)
XLA Ops:
  6.5 0.7 all-gather.3.cloned.1.call-update
  7.3 0.0 all-reduce.3.cloned.1.call-start
  7.3 0.9 fusion.7
  8.3 10.9 %collective-permute-start = (bf16[1,2,24,256]{3,2,1,0:T(8,128)(2,1)S(1)}, bf16[1,2,24,256]{3,2,1,0:T(8,128)(2,1)S(1)}, u32[]{:S(2)}, u32[]{:S(2)}) collective-permute-start(bf16[1,2,24,256]{3,2,1,0:T(8,128)(2,1)S(1)} %pad_maximum_fusion.6), channel_id=1, source_target_pairs={{32,0},{36,4},{40,8},{44,12},{48,16},{52,20},{56,24},{60,28},{0,32... | collective-permute-start | bytes 73736 | tf_op jit(solution)/shard_map/ppermute | solution.py:25
  19.2 3.5 %collective-permute-start.1 = (bf16[1,1,24,256]{3,2,1,0:T(8,128)(2,1)S(1)}, bf16[1,1,24,256]{3,2,1,0:T(8,128)(2,1)S(1)}, u32[]{:S(2)}, u32[]{:S(2)}) collective-permute-start(bf16[1,1,24,256]{3,2,1,0:T(8,128)(2,1)S(1)} %get-tuple-element.32), channel_id=1, source_target_pairs={{0,64},{64,128},{128,192},{192,256},{256,320},{320,384},{384,448},... | collective-permute-start | bytes 36872 | tf_op jit(solution)/shard_map/ppermute | solution.py:16
  22.7 3.3 %collective-permute-start.2 = (bf16[1,1,24,256]{3,2,1,0:T(8,128)(2,1)S(1)}, bf16[1,1,24,256]{3,2,1,0:T(8,128)(2,1)S(1)}, u32[]{:S(2)}, u32[]{:S(2)}) collective-permute-start(bf16[1,1,24,256]{3,2,1,0:T(8,128)(2,1)S(1)} %get-tuple-element.31), channel_id=1, source_target_pairs={{64,0},{128,64},{192,128},{256,192},{320,256},{384,320},{448,384},... | collective-permute-start | bytes 36872 | tf_op jit(solution)/shard_map/ppermute | solution.py:17
  26.0 2.3 collective-permute-done.2
  28.3 0.0 collective-permute-start.3
  28.4 2.9 %collective-permute-start.4 = (bf16[1,9,1,256]{3,2,1,0:T(2,128)(2,1)S(1)}, bf16[1,9,1,256]{3,2,1,0:T(2,128)(2,1)S(1)}, u32[]{:S(2)}, u32[]{:S(2)}) collective-permute-start(bf16[1,9,1,256]{3,2,1,0:T(2,128)(2,1)S(1)} %get-tuple-element.23), channel_id=1, source_target_pairs={{4,0},{8,4},{12,8},{16,12},{20,16},{24,20},{28,24},{32,28},{36,32}... | collective-permute-start | bytes 13832 | tf_op jit(solution)/shard_map/ppermute | solution.py:17
  31.3 1.4 collective-permute-done.3
  32.7 0.1 pad_maximum_fusion
  32.8 27.4 %all-gather.3.cloned.1.call-done = bf16[3,3,1,256,1024]{4,3,2,1,0:T(8,128)(2,1)} async-done(((bf16[3,3,1,16,1024]{4,3,2,1,0:T(8,128)(2,1)}), bf16[3,3,1,256,1024]{4,3,2,1,0:T(8,128)(2,1)}) %all-gather.3.cloned.1.call-update) | async-done | bytes 4718608 | tf_op jit(solution)/shard_map/all_gather | solution.py:61
  60.2 1.4 fusion.3
  61.6 1.4 convolution_add_fusion.15
  63.1 1.3 convolution_add_fusion.14
  64.4 0.3 convolution_add_fusion.13
  64.6 0.0 copy-start.3
  64.7 0.3 convolution_add_fusion.12
  64.9 0.3 convolution_add_fusion.11
  65.2 0.3 convolution_add_fusion.10
  65.5 0.3 convolution_add_fusion.9
  65.7 1.0 fusion
  66.7 0.0 all-reduce.3.cloned.1.call-update
  66.8 0.0 all-gather.5.cloned.1.call-start
  66.8 0.7 all-gather.5.cloned.1.call-update
  67.5 0.0 all-reduce.5.cloned.1.call-start
  67.6 55.4 %all-reduce.3.cloned.1.call-done = bf16[1,7,24,1024]{3,2,1,0:T(8,128)(2,1)} async-done(((bf16[1,7,24,1024]{3,2,1,0:T(8,128)(2,1)}), bf16[1,7,24,1024]{3,2,1,0:T(8,128)(2,1)}) %all-reduce.3.cloned.1.call-update) | async-done | bytes 344080 | tf_op jit(solution)/shard_map/psum | solution.py:68
  122.9 0.9 multiply_convert_fusion
  123.9 8.0 %collective-permute-start.5 = (bf16[1,2,24,256]{3,2,1,0:T(8,128)(2,1)S(1)}, bf16[1,2,24,256]{3,2,1,0:T(8,128)(2,1)S(1)}, u32[]{:S(2)}, u32[]{:S(2)}) collective-permute-start(bf16[1,2,24,256]{3,2,1,0:T(8,128)(2,1)S(1)} %pad_maximum_fusion.7), channel_id=1, source_target_pairs={{32,0},{36,4},{40,8},{44,12},{48,16},{52,20},{56,24},{60,28},{0,32... | collective-permute-start | bytes 73736 | tf_op jit(solution)/shard_map/ppermute | solution.py:25
  131.9 2.8 %collective-permute-start.6 = (bf16[1,1,24,256]{3,2,1,0:T(8,128)(2,1)S(1)}, bf16[1,1,24,256]{3,2,1,0:T(8,128)(2,1)S(1)}, u32[]{:S(2)}, u32[]{:S(2)}) collective-permute-start(bf16[1,1,24,256]{3,2,1,0:T(8,128)(2,1)S(1)} %get-tuple-element.28), channel_id=1, source_target_pairs={{0,64},{64,128},{128,192},{192,256},{256,320},{320,384},{384,448},... | collective-permute-start | bytes 36872 | tf_op jit(solution)/shard_map/ppermute | solution.py:16
  134.7 3.9 %collective-permute-start.7 = (bf16[1,1,24,256]{3,2,1,0:T(8,128)(2,1)S(1)}, bf16[1,1,24,256]{3,2,1,0:T(8,128)(2,1)S(1)}, u32[]{:S(2)}, u32[]{:S(2)}) collective-permute-start(bf16[1,1,24,256]{3,2,1,0:T(8,128)(2,1)S(1)} %get-tuple-element.27), channel_id=1, source_target_pairs={{64,0},{128,64},{192,128},{256,192},{320,256},{384,320},{448,384},... | collective-permute-start | bytes 36872 | tf_op jit(solution)/shard_map/ppermute | solution.py:17
  138.7 1.7 collective-permute-done.7
  140.4 0.0 collective-permute-start.8
  140.4 2.9 %collective-permute-start.9 = (bf16[1,9,1,256]{3,2,1,0:T(2,128)(2,1)S(1)}, bf16[1,9,1,256]{3,2,1,0:T(2,128)(2,1)S(1)}, u32[]{:S(2)}, u32[]{:S(2)}) collective-permute-start(bf16[1,9,1,256]{3,2,1,0:T(2,128)(2,1)S(1)} %get-tuple-element.19), channel_id=1, source_target_pairs={{4,0},{8,4},{12,8},{16,12},{20,16},{24,20},{28,24},{32,28},{36,32}... | collective-permute-start | bytes 13832 | tf_op jit(solution)/shard_map/ppermute | solution.py:17
  143.4 26.7 %all-gather.5.cloned.1.call-done = bf16[3,3,1,256,1024]{4,3,2,1,0:T(8,128)(2,1)} async-done(((bf16[3,3,1,16,1024]{4,3,2,1,0:T(8,128)(2,1)}), bf16[3,3,1,256,1024]{4,3,2,1,0:T(8,128)(2,1)}) %all-gather.5.cloned.1.call-update) | async-done | bytes 4718608 | tf_op jit(solution)/shard_map/all_gather | solution.py:61
  170.1 1.4 fusion.2
  171.5 0.1 pad_maximum_fusion.1
  171.7 1.3 convolution_add_fusion.7
  173.0 0.3 convolution_add_fusion.6
  173.3 0.3 convolution_add_fusion.5
  173.5 0.3 convolution_add_fusion.4
  173.8 0.3 convolution_add_fusion.3
  174.1 0.3 convolution_add_fusion.2
  174.3 0.3 convolution_add_fusion.1
  174.6 1.0 fusion.1
  175.6 0.0 all-reduce.5.cloned.1.call-update
  175.6 56.1 %all-reduce.5.cloned.1.call-done = bf16[1,7,24,1024]{3,2,1,0:T(8,128)(2,1)} async-done(((bf16[1,7,24,1024]{3,2,1,0:T(8,128)(2,1)}), bf16[1,7,24,1024]{3,2,1,0:T(8,128)(2,1)}) %all-reduce.5.cloned.1.call-update) | async-done | bytes 344080 | tf_op jit(solution)/shard_map/psum | solution.py:68
  231.7 1.6 fusion.9
  (30 shorter events, 0.2 us)
Async XLA Ops:
  6.5 53.7 %all-gather.3.cloned.1.call-start = ((), (), s32[]{:S(2)}) async-start(), calls=%async_computation | async-start | bytes 5013504 | tf_op jit(solution)/shard_map/all_gather | solution.py:61
  7.3 115.7 %all-reduce.3.cloned.1.call-start = ((), (), s32[]{:S(2)}) async-start(), calls=%async_computation.1 | async-start | bytes 688128 | tf_op jit(solution)/shard_map/psum | solution.py:68
  8.3 20.0 %collective-permute-start = (bf16[1,2,24,256]{3,2,1,0:T(8,128)(2,1)S(1)}, bf16[1,2,24,256]{3,2,1,0:T(8,128)(2,1)S(1)}, u32[]{:S(2)}, u32[]{:S(2)}) collective-permute-start(bf16[1,2,24,256]{3,2,1,0:T(8,128)(2,1)S(1)} %pad_maximum_fusion.6), channel_id=1, source_target_pairs={{32,0},{36,4},{40,8},{44,12},{48,16},{52,20},{56,24},{60,28},{0,32... | collective-permute-start | bytes 73736 | tf_op jit(solution)/shard_map/ppermute | solution.py:25
  19.2 6.8 %collective-permute-start.1 = (bf16[1,1,24,256]{3,2,1,0:T(8,128)(2,1)S(1)}, bf16[1,1,24,256]{3,2,1,0:T(8,128)(2,1)S(1)}, u32[]{:S(2)}, u32[]{:S(2)}) collective-permute-start(bf16[1,1,24,256]{3,2,1,0:T(8,128)(2,1)S(1)} %get-tuple-element.32), channel_id=1, source_target_pairs={{0,64},{64,128},{128,192},{192,256},{256,320},{320,384},{384,448},... | collective-permute-start | bytes 36872 | tf_op jit(solution)/shard_map/ppermute | solution.py:16
  22.7 5.6 %collective-permute-start.2 = (bf16[1,1,24,256]{3,2,1,0:T(8,128)(2,1)S(1)}, bf16[1,1,24,256]{3,2,1,0:T(8,128)(2,1)S(1)}, u32[]{:S(2)}, u32[]{:S(2)}) collective-permute-start(bf16[1,1,24,256]{3,2,1,0:T(8,128)(2,1)S(1)} %get-tuple-element.31), channel_id=1, source_target_pairs={{64,0},{128,64},{192,128},{256,192},{320,256},{384,320},{448,384},... | collective-permute-start | bytes 36872 | tf_op jit(solution)/shard_map/ppermute | solution.py:17
  28.3 4.3 %collective-permute-start.3 = (bf16[1,9,1,256]{3,2,1,0:T(2,128)(2,1)S(1)}, bf16[1,9,1,256]{3,2,1,0:T(2,128)(2,1)S(1)}, u32[]{:S(2)}, u32[]{:S(2)}) collective-permute-start(bf16[1,9,1,256]{3,2,1,0:T(2,128)(2,1)S(1)} %get-tuple-element.24), channel_id=1, source_target_pairs={{0,4},{4,8},{8,12},{12,16},{16,20},{20,24},{24,28},{28,32},{32,36}... | collective-permute-start | bytes 13832 | tf_op jit(solution)/shard_map/ppermute | solution.py:16
  28.4 4.3 %collective-permute-start.4 = (bf16[1,9,1,256]{3,2,1,0:T(2,128)(2,1)S(1)}, bf16[1,9,1,256]{3,2,1,0:T(2,128)(2,1)S(1)}, u32[]{:S(2)}, u32[]{:S(2)}) collective-permute-start(bf16[1,9,1,256]{3,2,1,0:T(2,128)(2,1)S(1)} %get-tuple-element.23), channel_id=1, source_target_pairs={{4,0},{8,4},{12,8},{16,12},{20,16},{24,20},{28,24},{32,28},{36,32}... | collective-permute-start | bytes 13832 | tf_op jit(solution)/shard_map/ppermute | solution.py:17
  60.2 4.2 %copy-start.1 = (bf16[3,3,1,256,1024]{4,3,2,1,0:T(8,128)(2,1)S(1)}, bf16[3,3,1,256,1024]{4,3,2,1,0:T(8,128)(2,1)}, u32[]{:S(2)}) copy-start(bf16[3,3,1,256,1024]{4,3,2,1,0:T(8,128)(2,1)} %all-gather.3.cloned.1.call-done) | copy-start | bytes 14155780
  64.6 58.3 %copy-start.3 = (f32[256]{0:T(256)S(1)}, f32[256]{0:T(256)}, u32[]{:S(2)}) copy-start(f32[256]{0:T(256)} %param.7) | copy-start | bytes 3076
  66.8 103.3 %all-gather.5.cloned.1.call-start = ((), (), s32[]{:S(2)}) async-start(), calls=%async_computation.2 | async-start | bytes 5013504 | tf_op jit(solution)/shard_map/all_gather | solution.py:61
  67.5 164.2 %all-reduce.5.cloned.1.call-start = ((), (), s32[]{:S(2)}) async-start(), calls=%async_computation.3 | async-start | bytes 688128 | tf_op jit(solution)/shard_map/psum | solution.py:68
  123.9 16.4 %collective-permute-start.5 = (bf16[1,2,24,256]{3,2,1,0:T(8,128)(2,1)S(1)}, bf16[1,2,24,256]{3,2,1,0:T(8,128)(2,1)S(1)}, u32[]{:S(2)}, u32[]{:S(2)}) collective-permute-start(bf16[1,2,24,256]{3,2,1,0:T(8,128)(2,1)S(1)} %pad_maximum_fusion.7), channel_id=1, source_target_pairs={{32,0},{36,4},{40,8},{44,12},{48,16},{52,20},{56,24},{60,28},{0,32... | collective-permute-start | bytes 73736 | tf_op jit(solution)/shard_map/ppermute | solution.py:25
  131.9 6.8 %collective-permute-start.6 = (bf16[1,1,24,256]{3,2,1,0:T(8,128)(2,1)S(1)}, bf16[1,1,24,256]{3,2,1,0:T(8,128)(2,1)S(1)}, u32[]{:S(2)}, u32[]{:S(2)}) collective-permute-start(bf16[1,1,24,256]{3,2,1,0:T(8,128)(2,1)S(1)} %get-tuple-element.28), channel_id=1, source_target_pairs={{0,64},{64,128},{128,192},{192,256},{256,320},{320,384},{384,448},... | collective-permute-start | bytes 36872 | tf_op jit(solution)/shard_map/ppermute | solution.py:16
  134.7 5.6 %collective-permute-start.7 = (bf16[1,1,24,256]{3,2,1,0:T(8,128)(2,1)S(1)}, bf16[1,1,24,256]{3,2,1,0:T(8,128)(2,1)S(1)}, u32[]{:S(2)}, u32[]{:S(2)}) collective-permute-start(bf16[1,1,24,256]{3,2,1,0:T(8,128)(2,1)S(1)} %get-tuple-element.27), channel_id=1, source_target_pairs={{64,0},{128,64},{192,128},{256,192},{320,256},{384,320},{448,384},... | collective-permute-start | bytes 36872 | tf_op jit(solution)/shard_map/ppermute | solution.py:17
  140.4 31.2 %collective-permute-start.8 = (bf16[1,9,1,256]{3,2,1,0:T(2,128)(2,1)S(1)}, bf16[1,9,1,256]{3,2,1,0:T(2,128)(2,1)S(1)}, u32[]{:S(2)}, u32[]{:S(2)}) collective-permute-start(bf16[1,9,1,256]{3,2,1,0:T(2,128)(2,1)S(1)} %get-tuple-element.20), channel_id=1, source_target_pairs={{0,4},{4,8},{8,12},{12,16},{16,20},{20,24},{24,28},{28,32},{32,36}... | collective-permute-start | bytes 13832 | tf_op jit(solution)/shard_map/ppermute | solution.py:16
  140.4 31.1 %collective-permute-start.9 = (bf16[1,9,1,256]{3,2,1,0:T(2,128)(2,1)S(1)}, bf16[1,9,1,256]{3,2,1,0:T(2,128)(2,1)S(1)}, u32[]{:S(2)}, u32[]{:S(2)}) collective-permute-start(bf16[1,9,1,256]{3,2,1,0:T(2,128)(2,1)S(1)} %get-tuple-element.19), channel_id=1, source_target_pairs={{4,0},{8,4},{12,8},{16,12},{20,16},{24,20},{28,24},{32,28},{36,32}... | collective-permute-start | bytes 13832 | tf_op jit(solution)/shard_map/ppermute | solution.py:17
  170.1 2.9 %copy-start = (bf16[3,3,1,256,1024]{4,3,2,1,0:T(8,128)(2,1)S(1)}, bf16[3,3,1,256,1024]{4,3,2,1,0:T(8,128)(2,1)}, u32[]{:S(2)}) copy-start(bf16[3,3,1,256,1024]{4,3,2,1,0:T(8,128)(2,1)} %all-gather.5.cloned.1.call-done) | copy-start | bytes 14155780
  173.5 58.2 %copy-start.2 = (bf16[1,7,24,256]{3,2,1,0:T(8,128)(2,1)S(1)}, bf16[1,7,24,256]{3,2,1,0:T(8,128)(2,1)}, u32[]{:S(2)}) copy-start(bf16[1,7,24,256]{3,2,1,0:T(8,128)(2,1)} %param.5) | copy-start | bytes 258052
  173.5 58.2 %copy-start.4 = (f32[256]{0:T(256)S(1)}, f32[256]{0:T(256)}, u32[]{:S(2)}) copy-start(f32[256]{0:T(256)} %param.9) | copy-start | bytes 3076
Sparse Core Ops, SparseCore 0:
  9.5 50.6 all-gather.2
  66.9 55.9 all-reduce.2
  125.1 44.9 all-gather.4
  175.8 55.9 all-reduce.4
where the time goes:
time: 240 us
  waiting for transfers between devices  172 us (72%)
  starting transfers between devices  38.5 us (16%)
  between operations  13.5 us (6%)
  matrix products  11.7 us (5%)
  other arithmetic  3.66 us (2%)
    psum x2, waiting for transfers between devices, conv_sum(): lax.psum(partial_value.astype(jnp.bfloat16), 'ch').astype(jnp.float32)  111 us
    all_gather x2, waiting for transfers between devices, conv_sum(): piece = lax.all_gather(kernel, 'lon', axis=3, tiled=True)  54.1 us
    ppermute x2, starting transfers between devices, shifted(): return lax.ppermute(block, axis, route)  18.9 us
    ppermute x4, starting transfers between devices, extended(): after = lax.ppermute(leading, axis, down)  13.1 us
    dot_general x18, matrix products, apply_taps(): jnp.dot(window, kernel[row_off, col_off], preferred_element_type=jnp.floa...  11.7 us
    ppermute x4, starting transfers between devices, extended(): before = lax.ppermute(last, axis, up)  6.34 us
  transfers between devices with their start and end apart: 14, of which 7 were waited for; matrix products, arithmetic and copies ran while one was open for 1% of the time, Pallas kernels for 0%

commit v1 on v0

v1 whole, which is shorter than its diff:
```python
import jax
import jax.numpy as jnp
from jax import lax
from jax.sharding import Mesh, PartitionSpec as P

skip_scale = 0.7071067811865476
AXES = ("x", "ylo", "z", "core", "ch")
LAT, LON, POLE = ("x", "ylo"), ("z", "core"), ("x", "ylo", "z", "core")


def silu(v):
    return jax.nn.silu(v.astype(jnp.float32)).astype(jnp.bfloat16)


def half_of(kernel, ylo):
    taps, rows, groups = 9, kernel.shape[3], 4
    flat = kernel.reshape(taps, rows, kernel.shape[4])
    width = kernel.shape[4] // groups
    low = [flat[:, :, g * width : g * width + width // 2] for g in range(groups)]
    high = [flat[:, :, g * width + width // 2 : (g + 1) * width] for g in range(groups)]
    return jnp.where(ylo == 0, jnp.concatenate(low, 2), jnp.concatenate(high, 2))


def lon_halo(block, width, lon):
    up = [(i, (i + 1) % lon) for i in range(lon)]
    down = [(j, i) for i, j in up]
    before = lax.ppermute(block[:, -width:], LON, up)
    after = lax.ppermute(block[:, :width], LON, down)
    return jnp.concatenate([before, block, after], axis=1)


def lat_pairs(lat, lon):
    pairs = []
    for i in range(lat):
        for j in range(lon):
            k = i - 1 if i % 2 == 0 else i + 1
            to = (k, j) if 0 <= k < lat else (i, (j + lon // 2) % lon)
            pairs.append((i * lon + j, to[0] * lon + to[1]))
    return pairs


def region(block, lat, lon):
    x, ylo = lax.axis_index("x"), lax.axis_index("ylo")
    wide = lon_halo(block, 2, lon)
    sent = jnp.where(ylo == 0, wide[:2], wide[-2:])
    came = lax.ppermute(sent, POLE, lat_pairs(lat, lon))
    at_pole = jnp.logical_or((x == 0) & (ylo == 0), (x == lat // 2 - 1) & (ylo == 1))
    came = jnp.where(at_pole, came[::-1], came)
    nine = jnp.where(
        ylo == 0, jnp.concatenate([came, wide]), jnp.concatenate([wide, came])
    )
    other = lax.ppermute(nine, "ylo", [(0, 1), (1, 0)])
    return jnp.concatenate([jnp.where(ylo == 0, nine, other), jnp.where(ylo == 0, other, nine)])


def conv(rows_of, columns, kernel):
    windows = [rows_of(a)[:, e : e + columns] for a in range(3) for e in range(3)]
    stacked = jnp.concatenate(windows, axis=2)
    flat = stacked.reshape(-1, stacked.shape[2])
    return jnp.dot(flat, kernel, preferred_element_type=jnp.float32).astype(jnp.bfloat16)


def body(features, kernel_one, bias_one, kernel_two, bias_two):
    lat = lax.axis_size("x") * lax.axis_size("ylo")
    lon = lax.axis_size("z") * lax.axis_size("core")
    x, ylo = lax.axis_index("x"), lax.axis_index("ylo")
    own = features[0]
    height, breadth, width = own.shape

    both = jnp.stack([half_of(kernel_one, ylo), half_of(kernel_two, ylo)])
    both = lax.all_gather(both, LON, axis=2, tiled=True)
    both = both.reshape(2, 9 * width, both.shape[3])

    ext = region(silu(own), lat, lon)
    top, bottom = x == 0, x == lax.axis_size("x") - 1
    last = ext.shape[0] - 1

    def rows_of(a):
        first = jnp.where(top, ext[2 - a : 3 - a], ext[a : a + 1])
        final = jnp.where(bottom, ext[last - a : last - a + 1], ext[last - 2 + a : last - 1 + a])
        return jnp.concatenate([first, ext[a + 1 : last - 2 + a], final])

    partial_one = conv(rows_of, breadth + 2, both[0])
    cells = partial_one.shape[0]
    partial_one = partial_one.reshape(cells, 4, width // 2).transpose(1, 0, 2)
    parts = lax.all_to_all(partial_one, "ch", 0, 0)
    hidden = parts.astype(jnp.float32).sum(0)
    hidden = hidden + jnp.where(ylo == 0, bias_one[: width // 2], bias_one[width // 2 :])
    mine = silu(hidden)
    other = lax.ppermute(mine, "ylo", [(0, 1), (1, 0)])
    act = jnp.concatenate(
        [jnp.where(ylo == 0, mine, other), jnp.where(ylo == 0, other, mine)], axis=1
    )
    act = act.reshape(2 * height + 2, breadth + 2, width)

    partial_two = conv(lambda a: act[a : a + 2 * height], breadth, both[1])
    partial_two = partial_two.reshape(2, height * breadth, 4, width // 2)
    partial_two = partial_two.transpose(0, 2, 1, 3).reshape(8, height * breadth, width // 2)
    parts = lax.all_to_all(partial_two, ("ylo", "ch"), 0, 0)
    second = parts.astype(jnp.float32).reshape(2, 4, height * breadth, width // 2).sum(1)
    second = jnp.concatenate([second[0], second[1]], axis=1) + bias_two
    second = second.reshape(height, breadth, width)
    return ((own.astype(jnp.float32) + second) * skip_scale).astype(jnp.bfloat16)[None]


def solution(mesh):
    lat, lon, ch = (mesh.shape[name] for name in ("lat", "lon", "ch"))
    fine = Mesh(mesh.devices.reshape(lat // 2, 2, lon // 2, 2, ch), AXES)
    field = P(None, LAT, LON, "ch")
    kernel = P(None, None, "ch", LON, None)
    return jax.shard_map(
        body,
        mesh=fine,
        in_specs=(field, kernel, P("ch"), kernel, P("ch")),
        out_specs=field,
        check_vma=False,
    )
```

time: 240 us -> 119 us (0.50)
  waiting for transfers between devices: 172 us -> 49.7 us
  blocking collectives: 0 us -> 16.4 us
  starting transfers between devices: 38.5 us -> 25 us
  matrix products: 11.7 us -> 2.11 us
  local copies, waits for them, and re-layouts: 0.13 us -> 9.12 us
    psum x2 -> x0, waiting for transfers between devices: 111 us -> none  [conv_sum(): lax.psum(partial_value.astype(jnp.bfloat16), 'ch').astype(jnp.float32)]
    all_gather x2 -> x1, waiting for transfers between devices: 54.1 us -> 24.3 us  [body(): both = lax.all_gather(both, LON, axis=2, tiled=True)]
    ppermute x10 -> x5, starting transfers between devices: 38.3 us -> 18.3 us  [the longest x1 8.49 us: lon_halo(): after = lax.ppermute(block[:, :width], LON, down)]
    all_to_all x0 -> x1, blocking collectives: none -> 16.4 us  [body(): parts = lax.all_to_all(partial_two, ('ylo', 'ch'), 0, 0)]
    all_to_all x0 -> x1, waiting for transfers between devices: none -> 13.5 us  [body(): parts = lax.all_to_all(partial_one, 'ch', 0, 0)]
    dot_general x18 -> x2, matrix products: 11.7 us -> 2.11 us  [conv(): jnp.dot(flat, kernel, preferred_element_type=jnp.float32)]
    all_to_all x0 -> x1, starting transfers between devices: none -> 6.73 us  [body(): parts = lax.all_to_all(partial_one, 'ch', 0, 0)]
    ppermute x10 -> x5, waiting for transfers between devices: 5.34 us -> 11.9 us  [the longest x1 3.77 us: body(): other = lax.ppermute(mine, 'ylo', [(0, 1), (1, 0)])]
  transfers between devices with their start and end apart: 14 -> 7, of which waited for: 7 -> 7; matrix products, arithmetic and copies ran while one was open for 1% -> 3% of each run, Pallas kernels for 0% -> 0%
where the time goes in v1:
time: 119 us; the launch traced here: 118 us
  waiting for transfers between devices  49.7 us (42%)
  starting transfers between devices  25 us (21%)
  blocking collectives  16.4 us (14%)
  between operations  13.8 us (12%)
  local copies, waits for them, and re-layouts  9.12 us (8%)
  other arithmetic  2.23 us (2%)
  matrix products  2.11 us (2%)
    all_gather x1, waiting for transfers between devices, body(): both = lax.all_gather(both, LON, axis=2, tiled=True)  24.3 us
    all_to_all x1, blocking collectives, body(): parts = lax.all_to_all(partial_two, ('ylo', 'ch'), 0, 0)  16.4 us
    all_to_all x1, waiting for transfers between devices, body(): parts = lax.all_to_all(partial_one, 'ch', 0, 0)  13.5 us
    ppermute x1, starting transfers between devices, lon_halo(): after = lax.ppermute(block[:, :width], LON, down)  8.49 us
    all_to_all x1, starting transfers between devices, body(): parts = lax.all_to_all(partial_one, 'ch', 0, 0)  6.73 us
    ppermute x1, waiting for transfers between devices, body(): other = lax.ppermute(mine, 'ylo', [(0, 1), (1, 0)])  3.77 us
    ppermute x1, waiting for transfers between devices, region(): other = lax.ppermute(nine, 'ylo', [(0, 1), (1, 0)])  3.54 us
    ppermute x1, starting transfers between devices, region(): other = lax.ppermute(nine, 'ylo', [(0, 1), (1, 0)])  3.48 us
  transfers between devices with their start and end apart: 7, of which 7 were waited for; matrix products, arithmetic and copies ran while one was open for 3% of the time, Pallas kernels for 0%

profile of v1, /device:TPU:2, one launch (start us, length us, event | category | flops | bytes accessed | tf_op | source)
XLA Modules:
  0.0 118.4 jit_solution(5470090524509661130)
XLA Ops:
  6.5 1.0 slice_bitcast_fusion.11
  7.5 0.9 slice_bitcast_fusion.3
  8.4 0.1 maximum_select_fusion.1
  8.6 0.7 pad_maximum_fusion
  9.3 0.0 all-gather.2.cloned.1.call-update
  9.4 0.1 fusion.16
  9.4 0.0 collective-permute-start
  9.5 8.5 %collective-permute-start.1 = (bf16[7,2,256]{2,1,0:T(2,128)(2,1)S(1)}, bf16[7,2,256]{2,1,0:T(2,128)(2,1)S(1)}, u32[]{:S(2)}, u32[]{:S(2)}) collective-permute-start(bf16[7,2,256]{2,1,0:T(2,128)(2,1)S(1)} %get-tuple-element.41), channel_id=1, source_target_pairs={{4,0},{8,4},{12,8},{16,12},{20,16},{24,20},{28,24},{32,28},{36,32}... | collective-permute-start | bytes 21512 | tf_op jit(solution)/shard_map/ppermute | solution.py:28
  18.0 1.3 %collective-permute-done = bf16[7,2,256]{2,1,0:T(2,128)(2,1)S(1)} collective-permute-done((bf16[7,2,256]{2,1,0:T(2,128)(2,1)S(1)}, bf16[7,2,256]{2,1,0:T(2,128)(2,1)S(1)}, u32[]{:S(2)}, u32[]{:S(2)}) %collective-permute-start) | collective-permute-done | bytes 7200 | tf_op jit(solution)/shard_map/ppermute | solution.py:27
  19.3 0.1 collective-permute-done.1
  19.3 3.5 %collective-permute-start.2 = (bf16[2,28,256]{2,1,0:T(8,128)(2,1)S(1)}, bf16[2,28,256]{2,1,0:T(8,128)(2,1)S(1)}, u32[]{:S(2)}, u32[]{:S(2)}) collective-permute-start(bf16[2,28,256]{2,1,0:T(8,128)(2,1)S(1)} %fusion.19), channel_id=1, source_target_pairs={{0,32},{4,36},{8,40},{12,44},{16,48},{20,52},{24,56},{28,60},{32,0... | collective-permute-start | bytes 86024 | tf_op jit(solution)/shard_map/ppermute | solution.py:46
  22.8 3.2 %collective-permute-done.2 = bf16[2,28,256]{2,1,0:T(8,128)(2,1)S(1)} collective-permute-done((bf16[2,28,256]{2,1,0:T(8,128)(2,1)S(1)}, bf16[2,28,256]{2,1,0:T(8,128)(2,1)S(1)}, u32[]{:S(2)}, u32[]{:S(2)}) %collective-permute-start.2) | collective-permute-done | bytes 28704 | tf_op jit(solution)/shard_map/ppermute | solution.py:46
  26.1 0.1 maximum_select_fusion
  26.1 3.5 %collective-permute-start.3 = (bf16[9,28,256]{2,1,0:T(8,128)(2,1)S(1)}, bf16[9,28,256]{2,1,0:T(8,128)(2,1)S(1)}, u32[]{:S(2)}, u32[]{:S(2)}) collective-permute-start(bf16[9,28,256]{2,1,0:T(8,128)(2,1)S(1)} %maximum_select_fusion), channel_id=1, source_target_pairs={{0,64},{64,0},{1,65},{65,1},{2,66},{66,2},{3,67},{67,3},{4,68},{68... | collective-permute-start | bytes 387080 | tf_op jit(solution)/shard_map/ppermute | solution.py:52
  29.6 3.5 %collective-permute-done.3 = bf16[9,28,256]{2,1,0:T(8,128)(2,1)S(1)} collective-permute-done((bf16[9,28,256]{2,1,0:T(8,128)(2,1)S(1)}, bf16[9,28,256]{2,1,0:T(8,128)(2,1)S(1)}, u32[]{:S(2)}, u32[]{:S(2)}) %collective-permute-start.3) | collective-permute-done | bytes 129056 | tf_op jit(solution)/shard_map/ppermute | solution.py:52
  33.3 0.1 fusion.6
  33.4 0.1 slice_dynamic-update-slice_fusion.7
  33.5 0.1 slice_dynamic-update-slice_fusion.6
  33.6 0.1 slice_dynamic-update-slice_fusion.4
  33.7 0.1 slice_dynamic-update-slice_fusion.3
  33.8 0.1 slice_dynamic-update-slice_fusion.1
  33.9 0.1 slice_dynamic-update-slice_fusion
  34.0 2.1 %reshape.295 = bf16[416,2304]{1,0:T(8,128)(2,1)} reshape(bf16[16,26,2304]{2,1,0:T(8,128)(2,1)S(1)} %slice_dynamic-update-slice_fusion) | data formatting | bytes 3833856 | tf_op jit(solution)/shard_map/reshape | solution.py:59
  36.1 24.3 %all-gather.2.cloned.1.call-done = bf16[2,9,256,512]{3,2,1,0:T(8,128)(2,1)} async-done(((bf16[2,9,16,512]{3,2,1,0:T(8,128)(2,1)}), bf16[2,9,256,512]{3,2,1,0:T(8,128)(2,1)}) %all-gather.2.cloned.1.call-update) | async-done | bytes 4718608 | tf_op jit(solution)/shard_map/all_gather | solution.py:71
  60.3 3.0 %fusion.20 = (bf16[1,9,256,512]{3,2,1,0:T(8,128)(2,1)S(1)}, bf16[1,9,256,512]{3,2,1,0:T(8,128)(2,1)S(1)}) fusion(bf16[2,9,256,512]{3,2,1,0:T(8,128)(2,1)} %all-gather.2.cloned.1.call-done), kind=kLoop, calls=%fused_computation.92 | loop fusion | bytes 9437184 | tf_op jit(solution)/shard_map/slice | solution.py:96
  63.4 1.1 fusion
  64.5 0.8 copy.11
  65.3 6.7 %all-to-all-start = ((bf16[4,416,128]{2,1,0:T(8,128)(2,1)}), bf16[4,416,128]{2,1,0:T(8,128)(2,1)S(1)}, u32[]{:S(2)}, u32[]{:S(2)}) async-start(bf16[4,416,128]{2,1,0:T(8,128)(2,1)} %bitcast.72), calls=%async_computation | async-start | bytes 851968 | tf_op jit(solution)/shard_map/all_to_all | solution.py:86
  72.1 13.5 %all-to-all-done = bf16[4,416,128]{2,1,0:T(8,128)(2,1)S(1)} async-done(((bf16[4,416,128]{2,1,0:T(8,128)(2,1)}), bf16[4,416,128]{2,1,0:T(8,128)(2,1)S(1)}, u32[]{:S(2)}, u32[]{:S(2)}) %all-to-all-start) | async-done | bytes 426016 | tf_op jit(solution)/shard_map/all_to_all | solution.py:86
  85.6 0.1 convert_reduce_fusion
  85.7 0.1 multiply_convert_fusion
  85.8 2.8 %collective-permute-start.4 = (bf16[416,128]{1,0:T(8,128)(2,1)S(1)}, bf16[416,128]{1,0:T(8,128)(2,1)S(1)}, u32[]{:S(2)}, u32[]{:S(2)}) collective-permute-start(bf16[416,128]{1,0:T(8,128)(2,1)S(1)} %multiply_convert_fusion), channel_id=1, source_target_pairs={{0,64},{64,0},{1,65},{65,1},{2,66},{66,2},{3,67},{67,3},{4,68},{68... | collective-permute-start | bytes 319496 | tf_op jit(solution)/shard_map/ppermute | solution.py:90
  88.6 3.8 %collective-permute-done.4 = bf16[416,128]{1,0:T(8,128)(2,1)S(1)} collective-permute-done((bf16[416,128]{1,0:T(8,128)(2,1)S(1)}, bf16[416,128]{1,0:T(8,128)(2,1)S(1)}, u32[]{:S(2)}, u32[]{:S(2)}) %collective-permute-start.4) | collective-permute-done | bytes 106528 | tf_op jit(solution)/shard_map/ppermute | solution.py:90
  92.4 0.1 broadcast_select_fusion.2
  92.5 0.1 pad_maximum_fusion.3
  92.6 0.1 slice.273
  92.6 0.1 slice.263
  92.7 0.1 slice.268
  92.8 0.1 slice_dynamic-update-slice_fusion.16
  92.8 0.1 slice_dynamic-update-slice_fusion.15
  92.9 0.1 slice_dynamic-update-slice_fusion.13
  93.0 0.1 slice_dynamic-update-slice_fusion.12
  93.1 0.1 slice_dynamic-update-slice_fusion.10
  93.2 0.1 slice_dynamic-update-slice_fusion.9
  93.3 1.0 convolution_convert_fusion.1
  94.2 0.1 reshape.300
  94.4 16.4 %all_to_all.10 = bf16[8,168,128]{2,1,0:T(8,128)(2,1)S(1)} all-to-all(bf16[8,168,128]{2,1,0:T(8,128)(2,1)S(1)} %bitcast.75), channel_id=1, replica_groups=mesh['x'=4,'ylo'=2,'z'=8,'core'=2,'ch'=4] {'ylo','ch'}, dimensions={0} | all-to-all | bytes 688128 | tf_op jit(solution)/shard_map/all_to_all | solution.py:99
  110.9 0.7 fusion.18
  (27 shorter events, 0.4 us)
Async XLA Ops:
  6.5 2.8 %copy-start.1 = (bf16[1,7,24,256]{3,2,1,0:T(8,128)(2,1)S(1)}, bf16[1,7,24,256]{3,2,1,0:T(8,128)(2,1)}, u32[]{:S(2)}) copy-start(bf16[1,7,24,256]{3,2,1,0:T(8,128)(2,1)} %param.5) | copy-start | bytes 258052
  6.5 53.8 %all-gather.2.cloned.1.call-start = ((), (), s32[]{:S(2)}) async-start(), calls=%async_computation.2 | async-start | bytes 5013504 | tf_op jit(solution)/shard_map/all_gather | solution.py:71
  9.4 9.8 %collective-permute-start = (bf16[7,2,256]{2,1,0:T(2,128)(2,1)S(1)}, bf16[7,2,256]{2,1,0:T(2,128)(2,1)S(1)}, u32[]{:S(2)}, u32[]{:S(2)}) collective-permute-start(bf16[7,2,256]{2,1,0:T(2,128)(2,1)S(1)} %get-tuple-element.40), channel_id=1, source_target_pairs={{0,4},{4,8},{8,12},{12,16},{16,20},{20,24},{24,28},{28,32},{32,36}... | collective-permute-start | bytes 21512 | tf_op jit(solution)/shard_map/ppermute | solution.py:27
  9.5 9.8 %collective-permute-start.1 = (bf16[7,2,256]{2,1,0:T(2,128)(2,1)S(1)}, bf16[7,2,256]{2,1,0:T(2,128)(2,1)S(1)}, u32[]{:S(2)}, u32[]{:S(2)}) collective-permute-start(bf16[7,2,256]{2,1,0:T(2,128)(2,1)S(1)} %get-tuple-element.41), channel_id=1, source_target_pairs={{4,0},{8,4},{12,8},{16,12},{20,16},{24,20},{28,24},{32,28},{36,32}... | collective-permute-start | bytes 21512 | tf_op jit(solution)/shard_map/ppermute | solution.py:28
  19.3 6.7 %collective-permute-start.2 = (bf16[2,28,256]{2,1,0:T(8,128)(2,1)S(1)}, bf16[2,28,256]{2,1,0:T(8,128)(2,1)S(1)}, u32[]{:S(2)}, u32[]{:S(2)}) collective-permute-start(bf16[2,28,256]{2,1,0:T(8,128)(2,1)S(1)} %fusion.19), channel_id=1, source_target_pairs={{0,32},{4,36},{8,40},{12,44},{16,48},{20,52},{24,56},{28,60},{32,0... | collective-permute-start | bytes 86024 | tf_op jit(solution)/shard_map/ppermute | solution.py:46
  26.1 7.0 %collective-permute-start.3 = (bf16[9,28,256]{2,1,0:T(8,128)(2,1)S(1)}, bf16[9,28,256]{2,1,0:T(8,128)(2,1)S(1)}, u32[]{:S(2)}, u32[]{:S(2)}) collective-permute-start(bf16[9,28,256]{2,1,0:T(8,128)(2,1)S(1)} %maximum_select_fusion), channel_id=1, source_target_pairs={{0,64},{64,0},{1,65},{65,1},{2,66},{66,2},{3,67},{67,3},{4,68},{68... | collective-permute-start | bytes 387080 | tf_op jit(solution)/shard_map/ppermute | solution.py:52
  60.3 3.0 %copy-start = (bf16[416,2304]{1,0:T(8,128)(2,1)S(1)}, bf16[416,2304]{1,0:T(8,128)(2,1)}, u32[]{:S(2)}) copy-start(bf16[416,2304]{1,0:T(8,128)(2,1)} %reshape.295) | copy-start | bytes 5750788
  63.3 8.7 %copy-start.3 = (f32[256]{0:T(256)S(1)}, f32[256]{0:T(256)}, u32[]{:S(2)}) copy-start(f32[256]{0:T(256)} %param.7) | copy-start | bytes 3076
  65.3 20.3 %all-to-all-start = ((bf16[4,416,128]{2,1,0:T(8,128)(2,1)}), bf16[4,416,128]{2,1,0:T(8,128)(2,1)S(1)}, u32[]{:S(2)}, u32[]{:S(2)}) async-start(bf16[4,416,128]{2,1,0:T(8,128)(2,1)} %bitcast.72), calls=%async_computation | async-start | bytes 851968 | tf_op jit(solution)/shard_map/all_to_all | solution.py:86
  85.8 6.6 %collective-permute-start.4 = (bf16[416,128]{1,0:T(8,128)(2,1)S(1)}, bf16[416,128]{1,0:T(8,128)(2,1)S(1)}, u32[]{:S(2)}, u32[]{:S(2)}) collective-permute-start(bf16[416,128]{1,0:T(8,128)(2,1)S(1)} %multiply_convert_fusion), channel_id=1, source_target_pairs={{0,64},{64,0},{1,65},{65,1},{2,66},{66,2},{3,67},{67,3},{4,68},{68... | collective-permute-start | bytes 319496 | tf_op jit(solution)/shard_map/ppermute | solution.py:90
  94.2 16.6 %copy-start.2 = (f32[256]{0:T(256)S(1)}, f32[256]{0:T(256)}, u32[]{:S(2)}) copy-start(f32[256]{0:T(256)} %param.9) | copy-start | bytes 3076
Sparse Core Ops, SparseCore 0:
  9.5 50.7 all-gather.1

commit v2 on v1

--- a/solution.py
+++ b/solution.py
@@ -67,9 +67,10 @@
     own = features[0]
     height, breadth, width = own.shape
 
-    both = jnp.stack([half_of(kernel_one, ylo), half_of(kernel_two, ylo)])
-    both = lax.all_gather(both, LON, axis=2, tiled=True)
-    both = both.reshape(2, 9 * width, both.shape[3])
+    both = [
+        lax.all_gather(half_of(kernel, ylo), LON, axis=1, tiled=True).reshape(9 * width, -1)
+        for kernel in (kernel_one, kernel_two)
+    ]
 
     ext = region(silu(own), lat, lon)
     top, bottom = x == 0, x == lax.axis_size("x") - 1

time: 119 us -> 132 us (1.11)
  the two profiles are of different devices: /device:TPU:2 before, /device:TPU:4 now
where the time goes in v2:
time: 132 us
  waiting for transfers between devices  57.3 us (43%)
  starting transfers between devices  24.7 us (19%)
  blocking collectives  20.1 us (15%)
  between operations  13.8 us (10%)
  local copies, waits for them, and re-layouts  6.11 us (5%)
  matrix products  6.02 us (5%)
  other arithmetic  3.67 us (3%)
    all_gather x2, waiting for transfers between devices, body(): lax.all_gather(half_of(kernel, ylo), LON, axis=1, tiled=True)  32.9 us
    all_to_all x1, blocking collectives, body(): parts = lax.all_to_all(partial_two, ('ylo', 'ch'), 0, 0)  20.1 us
    all_to_all x1, waiting for transfers between devices, body(): parts = lax.all_to_all(partial_one, 'ch', 0, 0)  13.5 us
    ppermute x1, starting transfers between devices, lon_halo(): after = lax.ppermute(block[:, :width], LON, down)  8.49 us
    all_to_all x1, starting transfers between devices, body(): parts = lax.all_to_all(partial_one, 'ch', 0, 0)  6.73 us
    dot_general x2, matrix products, conv(): jnp.dot(flat, kernel, preferred_element_type=jnp.float32)  6.02 us
    ppermute x1, waiting for transfers between devices, body(): other = lax.ppermute(mine, 'ylo', [(0, 1), (1, 0)])  3.81 us
    ppermute x1, waiting for transfers between devices, region(): came = lax.ppermute(sent, POLE, lat_pairs(lat, lon))  3.51 us
  transfers between devices with their start and end apart: 8, of which 8 were waited for; matrix products, arithmetic and copies ran while one was open for 8% of the time, Pallas kernels for 0%

profile of v2, /device:TPU:4, one launch (start us, length us, event | category | flops | bytes accessed | tf_op | source)
XLA Modules:
  0.0 131.7 jit_solution(2053105544258129663)
XLA Ops:
  6.5 0.9 fusion.21
  7.5 0.7 maximum_select_fusion.1
  8.2 0.0 all-gather.5.cloned.1.call-start
  8.3 0.9 fusion.16
  9.2 0.0 collective-permute-start
  9.3 8.5 %collective-permute-start.1 = (bf16[7,2,256]{2,1,0:T(2,128)(2,1)S(1)}, bf16[7,2,256]{2,1,0:T(2,128)(2,1)S(1)}, u32[]{:S(2)}, u32[]{:S(2)}) collective-permute-start(bf16[7,2,256]{2,1,0:T(2,128)(2,1)S(1)} %get-tuple-element.39), channel_id=1, source_target_pairs={{4,0},{8,4},{12,8},{16,12},{20,16},{24,20},{28,24},{32,28},{36,32}... | collective-permute-start | bytes 21512 | tf_op jit(solution)/shard_map/ppermute | solution.py:28
  17.8 1.3 collective-permute-done
  19.1 0.1 collective-permute-done.1
  19.1 3.5 %collective-permute-start.2 = (bf16[2,28,256]{2,1,0:T(8,128)(2,1)S(1)}, bf16[2,28,256]{2,1,0:T(8,128)(2,1)S(1)}, u32[]{:S(2)}, u32[]{:S(2)}) collective-permute-start(bf16[2,28,256]{2,1,0:T(8,128)(2,1)S(1)} %fusion.19), channel_id=1, source_target_pairs={{0,32},{4,36},{8,40},{12,44},{16,48},{20,52},{24,56},{28,60},{32,0... | collective-permute-start | bytes 86024 | tf_op jit(solution)/shard_map/ppermute | solution.py:46
  22.6 3.5 %collective-permute-done.2 = bf16[2,28,256]{2,1,0:T(8,128)(2,1)S(1)} collective-permute-done((bf16[2,28,256]{2,1,0:T(8,128)(2,1)S(1)}, bf16[2,28,256]{2,1,0:T(8,128)(2,1)S(1)}, u32[]{:S(2)}, u32[]{:S(2)}) %collective-permute-start.2) | collective-permute-done | bytes 28704 | tf_op jit(solution)/shard_map/ppermute | solution.py:46
  26.2 0.1 maximum_select_fusion
  26.2 3.2 %collective-permute-start.3 = (bf16[9,28,256]{2,1,0:T(8,128)(2,1)S(1)}, bf16[9,28,256]{2,1,0:T(8,128)(2,1)S(1)}, u32[]{:S(2)}, u32[]{:S(2)}) collective-permute-start(bf16[9,28,256]{2,1,0:T(8,128)(2,1)S(1)} %maximum_select_fusion), channel_id=1, source_target_pairs={{0,64},{64,0},{1,65},{65,1},{2,66},{66,2},{3,67},{67,3},{4,68},{68... | collective-permute-start | bytes 387080 | tf_op jit(solution)/shard_map/ppermute | solution.py:52
  29.4 0.9 fusion.20
  30.4 0.7 maximum_select_fusion.2
  31.1 2.2 %collective-permute-done.3 = bf16[9,28,256]{2,1,0:T(8,128)(2,1)S(1)} collective-permute-done((bf16[9,28,256]{2,1,0:T(8,128)(2,1)S(1)}, bf16[9,28,256]{2,1,0:T(8,128)(2,1)S(1)}, u32[]{:S(2)}, u32[]{:S(2)}) %collective-permute-start.3) | collective-permute-done | bytes 129056 | tf_op jit(solution)/shard_map/ppermute | solution.py:52
  33.4 0.1 fusion.6
  33.5 0.1 slice_dynamic-update-slice_fusion.7
  33.5 0.1 slice_dynamic-update-slice_fusion.6
  33.7 0.1 slice_dynamic-update-slice_fusion.4
  33.8 0.1 slice_dynamic-update-slice_fusion.3
  33.9 0.1 slice_dynamic-update-slice_fusion.1
  34.0 0.1 slice_dynamic-update-slice_fusion
  34.1 2.1 %reshape.82 = bf16[416,2304]{1,0:T(8,128)(2,1)} reshape(bf16[16,26,2304]{2,1,0:T(8,128)(2,1)S(1)} %slice_dynamic-update-slice_fusion) | data formatting | bytes 3833856 | tf_op jit(solution)/shard_map/reshape | solution.py:59
  36.2 21.4 %all-gather.3.cloned.1.call-done = bf16[9,256,512]{2,1,0:T(8,128)(2,1)} async-done(((bf16[9,16,512]{2,1,0:T(8,128)(2,1)}), bf16[9,256,512]{2,1,0:T(8,128)(2,1)}) %all-gather.3.cloned.1.call-update) | async-done | bytes 2359312 | tf_op jit(solution)/shard_map/all_gather | solution.py:71
  57.6 3.4 %fusion = bf16[52,4,8,128]{3,2,1,0:T(8,128)(2,1)S(1)} fusion(bf16[416,2304]{1,0:T(8,128)(2,1)} %reshape.82, bf16[2304,512]{1,0:T(8,128)(2,1)} %bitcast.47), kind=kOutput, calls=%fused_computation.2 | convolution fusion | flops 981680128 | bytes 4702208 | tf_op jit(solution)/shard_map/dot_general | solution.py:60
  61.0 0.8 copy.11
  61.9 6.7 %all-to-all-start = ((bf16[4,416,128]{2,1,0:T(8,128)(2,1)}), bf16[4,416,128]{2,1,0:T(8,128)(2,1)S(1)}, u32[]{:S(2)}, u32[]{:S(2)}) async-start(bf16[4,416,128]{2,1,0:T(8,128)(2,1)} %bitcast.40), calls=%async_computation | async-start | bytes 851968 | tf_op jit(solution)/shard_map/all_to_all | solution.py:87
  68.6 13.5 %all-to-all-done = bf16[4,416,128]{2,1,0:T(8,128)(2,1)S(1)} async-done(((bf16[4,416,128]{2,1,0:T(8,128)(2,1)}), bf16[4,416,128]{2,1,0:T(8,128)(2,1)S(1)}, u32[]{:S(2)}, u32[]{:S(2)}) %all-to-all-start) | async-done | bytes 426016 | tf_op jit(solution)/shard_map/all_to_all | solution.py:87
  82.1 0.1 convert_reduce_fusion
  82.2 0.1 multiply_convert_fusion
  82.3 2.8 %collective-permute-start.4 = (bf16[416,128]{1,0:T(8,128)(2,1)S(1)}, bf16[416,128]{1,0:T(8,128)(2,1)S(1)}, u32[]{:S(2)}, u32[]{:S(2)}) collective-permute-start(bf16[416,128]{1,0:T(8,128)(2,1)S(1)} %multiply_convert_fusion), channel_id=1, source_target_pairs={{0,64},{64,0},{1,65},{65,1},{2,66},{66,2},{3,67},{67,3},{4,68},{68... | collective-permute-start | bytes 319496 | tf_op jit(solution)/shard_map/ppermute | solution.py:91
  85.1 3.8 %collective-permute-done.4 = bf16[416,128]{1,0:T(8,128)(2,1)S(1)} collective-permute-done((bf16[416,128]{1,0:T(8,128)(2,1)S(1)}, bf16[416,128]{1,0:T(8,128)(2,1)S(1)}, u32[]{:S(2)}, u32[]{:S(2)}) %collective-permute-start.4) | collective-permute-done | bytes 106528 | tf_op jit(solution)/shard_map/ppermute | solution.py:91
  88.9 0.1 broadcast_select_fusion.2
  89.0 0.1 pad_maximum_fusion.2
  89.1 0.1 slice.246
  89.1 0.1 slice.251
  89.2 0.1 slice.256
  89.3 0.1 slice_dynamic-update-slice_fusion.16
  89.4 0.1 slice_dynamic-update-slice_fusion.15
  89.5 0.1 slice_dynamic-update-slice_fusion.13
  89.5 0.1 slice_dynamic-update-slice_fusion.12
  89.6 0.1 slice_dynamic-update-slice_fusion.10
  89.7 0.1 slice_dynamic-update-slice_fusion.9
  89.8 11.4 %all-gather.5.cloned.1.call-done = bf16[9,256,512]{2,1,0:T(8,128)(2,1)} async-done(((bf16[9,16,512]{2,1,0:T(8,128)(2,1)}), bf16[9,256,512]{2,1,0:T(8,128)(2,1)}) %all-gather.5.cloned.1.call-update) | async-done | bytes 2359312 | tf_op jit(solution)/shard_map/all_gather | solution.py:71
  101.2 2.6 %convolution_convert_fusion.1 = bf16[336,512]{1,0:T(8,128)(2,1)S(1)} fusion(bf16[336,2304]{1,0:T(8,128)(2,1)S(1)} %bitcast.46, bf16[2304,512]{1,0:T(8,128)(2,1)} %bitcast.48), kind=kOutput, calls=%fused_computation.1 | convolution fusion | flops 792895488 | bytes 4251648 | tf_op jit(solution)/shard_map/dot_general | solution.py:60
  103.8 0.1 reshape.89
  104.0 20.1 %all_to_all.10 = bf16[8,168,128]{2,1,0:T(8,128)(2,1)S(1)} all-to-all(bf16[8,168,128]{2,1,0:T(8,128)(2,1)S(1)} %bitcast.41), channel_id=1, replica_groups=mesh['x'=4,'ylo'=2,'z'=8,'core'=2,'ch'=4] {'ylo','ch'}, dimensions={0} | all-to-all | bytes 688128 | tf_op jit(solution)/shard_map/all_to_all | solution.py:100
  124.2 0.7 fusion.18
  (27 shorter events, 0.4 us)
Async XLA Ops:
  6.5 51.1 %all-gather.3.cloned.1.call-start = ((), (), s32[]{:S(2)}) async-start(), calls=%async_computation.2 | async-start | bytes 2506752 | tf_op jit(solution)/shard_map/all_gather | solution.py:71
  8.2 93.0 %all-gather.5.cloned.1.call-start = ((), (), s32[]{:S(2)}) async-start(), calls=%async_computation.3 | async-start | bytes 2506752 | tf_op jit(solution)/shard_map/all_gather | solution.py:71
  9.2 9.8 %collective-permute-start = (bf16[7,2,256]{2,1,0:T(2,128)(2,1)S(1)}, bf16[7,2,256]{2,1,0:T(2,128)(2,1)S(1)}, u32[]{:S(2)}, u32[]{:S(2)}) collective-permute-start(bf16[7,2,256]{2,1,0:T(2,128)(2,1)S(1)} %get-tuple-element.38), channel_id=1, source_target_pairs={{0,4},{4,8},{8,12},{12,16},{16,20},{20,24},{24,28},{28,32},{32,36}... | collective-permute-start | bytes 21512 | tf_op jit(solution)/shard_map/ppermute | solution.py:27
  9.3 9.8 %collective-permute-start.1 = (bf16[7,2,256]{2,1,0:T(2,128)(2,1)S(1)}, bf16[7,2,256]{2,1,0:T(2,128)(2,1)S(1)}, u32[]{:S(2)}, u32[]{:S(2)}) collective-permute-start(bf16[7,2,256]{2,1,0:T(2,128)(2,1)S(1)} %get-tuple-element.39), channel_id=1, source_target_pairs={{4,0},{8,4},{12,8},{16,12},{20,16},{24,20},{28,24},{32,28},{36,32}... | collective-permute-start | bytes 21512 | tf_op jit(solution)/shard_map/ppermute | solution.py:28
  19.1 7.0 %collective-permute-start.2 = (bf16[2,28,256]{2,1,0:T(8,128)(2,1)S(1)}, bf16[2,28,256]{2,1,0:T(8,128)(2,1)S(1)}, u32[]{:S(2)}, u32[]{:S(2)}) collective-permute-start(bf16[2,28,256]{2,1,0:T(8,128)(2,1)S(1)} %fusion.19), channel_id=1, source_target_pairs={{0,32},{4,36},{8,40},{12,44},{16,48},{20,52},{24,56},{28,60},{32,0... | collective-permute-start | bytes 86024 | tf_op jit(solution)/shard_map/ppermute | solution.py:46
  26.2 7.0 %collective-permute-start.3 = (bf16[9,28,256]{2,1,0:T(8,128)(2,1)S(1)}, bf16[9,28,256]{2,1,0:T(8,128)(2,1)S(1)}, u32[]{:S(2)}, u32[]{:S(2)}) collective-permute-start(bf16[9,28,256]{2,1,0:T(8,128)(2,1)S(1)} %maximum_select_fusion), channel_id=1, source_target_pairs={{0,64},{64,0},{1,65},{65,1},{2,66},{66,2},{3,67},{67,3},{4,68},{68... | collective-permute-start | bytes 387080 | tf_op jit(solution)/shard_map/ppermute | solution.py:52
  57.6 11.0 %copy-start.2 = (f32[256]{0:T(256)S(1)}, f32[256]{0:T(256)}, u32[]{:S(2)}) copy-start(f32[256]{0:T(256)} %param.7) | copy-start | bytes 3076
  61.9 20.3 %all-to-all-start = ((bf16[4,416,128]{2,1,0:T(8,128)(2,1)}), bf16[4,416,128]{2,1,0:T(8,128)(2,1)S(1)}, u32[]{:S(2)}, u32[]{:S(2)}) async-start(bf16[4,416,128]{2,1,0:T(8,128)(2,1)} %bitcast.40), calls=%async_computation | async-start | bytes 851968 | tf_op jit(solution)/shard_map/all_to_all | solution.py:87
  82.3 6.6 %collective-permute-start.4 = (bf16[416,128]{1,0:T(8,128)(2,1)S(1)}, bf16[416,128]{1,0:T(8,128)(2,1)S(1)}, u32[]{:S(2)}, u32[]{:S(2)}) collective-permute-start(bf16[416,128]{1,0:T(8,128)(2,1)S(1)} %multiply_convert_fusion), channel_id=1, source_target_pairs={{0,64},{64,0},{1,65},{65,1},{2,66},{66,2},{3,67},{67,3},{4,68},{68... | collective-permute-start | bytes 319496 | tf_op jit(solution)/shard_map/ppermute | solution.py:91
  103.8 20.4 %copy-start = (bf16[1,7,24,256]{3,2,1,0:T(8,128)(2,1)S(1)}, bf16[1,7,24,256]{3,2,1,0:T(8,128)(2,1)}, u32[]{:S(2)}) copy-start(bf16[1,7,24,256]{3,2,1,0:T(8,128)(2,1)} %param.5) | copy-start | bytes 258052
  103.8 20.4 %copy-start.1 = (f32[256]{0:T(256)S(1)}, f32[256]{0:T(256)}, u32[]{:S(2)}) copy-start(f32[256]{0:T(256)} %param.9) | copy-start | bytes 3076
Sparse Core Ops, SparseCore 0:
  9.5 48.0 all-gather.2
  59.7 41.3 all-gather.4

commit v3 on v1

--- a/solution.py
+++ b/solution.py
@@ -1,6 +1,7 @@
 import jax
 import jax.numpy as jnp
 from jax import lax
+from jax.experimental import pallas as pl
 from jax.sharding import Mesh, PartitionSpec as P
 
 skip_scale = 0.7071067811865476
@@ -53,11 +54,49 @@
     return jnp.concatenate([jnp.where(ylo == 0, nine, other), jnp.where(ylo == 0, other, nine)])
 
 
-def conv(rows_of, columns, kernel):
+def columns_of(rows_of, columns):
     windows = [rows_of(a)[:, e : e + columns] for a in range(3) for e in range(3)]
     stacked = jnp.concatenate(windows, axis=2)
-    flat = stacked.reshape(-1, stacked.shape[2])
-    return jnp.dot(flat, kernel, preferred_element_type=jnp.float32).astype(jnp.bfloat16)
+    return stacked.reshape(-1, stacked.shape[2])
+
+
+def taps_kernel(cells_ref, kernel_ref, out_ref):
+    parts, blocks, size, lanes = out_ref.shape
+    owners, _, taps, rows, _ = kernel_ref.shape
+    depth = owners * rows
+    total = None
+    for t in range(taps):
+        tap = kernel_ref[:, 0, t].reshape(depth, blocks * lanes)
+        term = jnp.dot(
+            cells_ref[:, t * depth : (t + 1) * depth], tap, preferred_element_type=jnp.float32
+        )
+        total = term if total is None else total + term
+    for p in range(parts):
+        for j in range(blocks):
+            piece = total[p * size : (p + 1) * size, j * lanes : (j + 1) * lanes]
+            out_ref[p, j] = piece.astype(out_ref.dtype)
+
+
+def conv(cells, gathered, which, parts):
+    owners, _, taps, rows, outs = gathered.shape
+    size, lanes, step = cells.shape[0] // parts, 128, 2
+    return pl.pallas_call(
+        taps_kernel,
+        grid=(outs // (lanes * step),),
+        in_specs=[
+            pl.BlockSpec(cells.shape, lambda n: (0, 0)),
+            pl.BlockSpec(
+                (owners, 1, taps, rows, lanes * step), lambda n: (0, which, 0, 0, n)
+            ),
+        ],
+        out_specs=pl.BlockSpec((parts, step, size, lanes), lambda n: (0, n, 0, 0)),
+        out_shape=jax.ShapeDtypeStruct((parts, outs // lanes, size, lanes), jnp.bfloat16),
+        cost_estimate=pl.CostEstimate(
+            flops=2 * cells.size * outs,
+            bytes_accessed=2 * (cells.size + taps * owners * rows * outs),
+            transcendentals=0,
+        ),
+    )(cells, gathered)
 
 
 def body(features, kernel_one, bias_one, kernel_two, bias_two):
@@ -68,8 +107,7 @@
     height, breadth, width = own.shape
 
     both = jnp.stack([half_of(kernel_one, ylo), half_of(kernel_two, ylo)])
-    both = lax.all_gather(both, LON, axis=2, tiled=True)
-    both = both.reshape(2, 9 * width, both.shape[3])
+    both = lax.all_gather(both, LON)
 
     ext = region(silu(own), lat, lon)
     top, bottom = x == 0, x == lax.axis_size("x") - 1
@@ -80,9 +118,7 @@
         final = jnp.where(bottom, ext[last - a : last - a + 1], ext[last - 2 + a : last - 1 + a])
         return jnp.concatenate([first, ext[a + 1 : last - 2 + a], final])
 
-    partial_one = conv(rows_of, breadth + 2, both[0])
-    cells = partial_one.shape[0]
-    partial_one = partial_one.reshape(cells, 4, width // 2).transpose(1, 0, 2)
+    partial_one = conv(columns_of(rows_of, breadth + 2), both, 0, 1)[0]
     parts = lax.all_to_all(partial_one, "ch", 0, 0)
     hidden = parts.astype(jnp.float32).sum(0)
     hidden = hidden + jnp.where(ylo == 0, bias_one[: width // 2], bias_one[width // 2 :])
@@ -93,9 +129,8 @@
     )
     act = act.reshape(2 * height + 2, breadth + 2, width)
 
-    partial_two = conv(lambda a: act[a : a + 2 * height], breadth, both[1])
-    partial_two = partial_two.reshape(2, height * breadth, 4, width // 2)
-    partial_two = partial_two.transpose(0, 2, 1, 3).reshape(8, height * breadth, width // 2)
+    cells = columns_of(lambda a: act[a : a + 2 * height], breadth)
+    partial_two = conv(cells, both, 1, 2).reshape(8, height * breadth, width // 2)
     parts = lax.all_to_all(partial_two, ("ylo", "ch"), 0, 0)
     second = parts.astype(jnp.float32).reshape(2, 4, height * breadth, width // 2).sum(1)
     second = jnp.concatenate([second[0], second[1]], axis=1) + bias_two

time: 119 us -> 122 us (1.025)
  the two profiles are of different devices: /device:TPU:2 before, /device:TPU:4 now
where the time goes in v3:
time: 122 us; the launch traced here: 121 us
  waiting for transfers between devices  50 us (41%)
  starting transfers between devices  24.7 us (20%)
  blocking collectives  16.6 us (14%)
  between operations  13.7 us (11%)
  Pallas kernels  7.6 us (6%)
  local copies, waits for them, and re-layouts  6.37 us (5%)
  other arithmetic  2.24 us (2%)
    all_gather x1, waiting for transfers between devices, body(): both = lax.all_gather(both, LON)  23.9 us
    all_to_all x1, blocking collectives, body(): parts = lax.all_to_all(partial_two, ('ylo', 'ch'), 0, 0)  16.6 us
    all_to_all x1, waiting for transfers between devices, body(): parts = lax.all_to_all(partial_one, 'ch', 0, 0)  13.6 us
    ppermute x1, starting transfers between devices, lon_halo(): after = lax.ppermute(block[:, :width], LON, down)  8.49 us
    pallas_call x2, Pallas kernels, conv(): pl.pallas_call(taps_kernel, grid=(outs // (lanes * step),), in_specs=[pl....  7.6 us
    all_to_all x1, starting transfers between devices, body(): parts = lax.all_to_all(partial_one, 'ch', 0, 0)  6.73 us
    ppermute x1, waiting for transfers between devices, region(): other = lax.ppermute(nine, 'ylo', [(0, 1), (1, 0)])  3.83 us
    ppermute x1, waiting for transfers between devices, body(): other = lax.ppermute(mine, 'ylo', [(0, 1), (1, 0)])  3.8 us
  transfers between devices with their start and end apart: 7, of which 7 were waited for; matrix products, arithmetic and copies ran while one was open for 2% of the time, Pallas kernels for 0%

profile of v3, /device:TPU:4, one launch (start us, length us, event | category | flops | bytes accessed | tf_op | source)
XLA Modules:
  0.0 121.2 jit_solution(3891627615503371492)
XLA Ops:
  6.5 0.0 all-gather.3.cloned.1.call-start
  6.5 1.0 slice_bitcast_fusion.11
  7.5 0.9 slice_bitcast_fusion.3
  8.4 0.1 maximum_select_fusion.1
  8.6 0.8 pad_maximum_fusion
  9.3 0.0 all-gather.3.cloned.1.call-update
  9.3 0.0 copy-done.1
  9.4 0.1 fusion.15
  9.4 0.0 collective-permute-start
  9.5 8.5 %collective-permute-start.1 = (bf16[7,2,256]{2,1,0:T(2,128)(2,1)S(1)}, bf16[7,2,256]{2,1,0:T(2,128)(2,1)S(1)}, u32[]{:S(2)}, u32[]{:S(2)}) collective-permute-start(bf16[7,2,256]{2,1,0:T(2,128)(2,1)S(1)} %get-tuple-element.39), channel_id=1, source_target_pairs={{4,0},{8,4},{12,8},{16,12},{20,16},{24,20},{28,24},{32,28},{36,32}... | collective-permute-start | bytes 21512 | tf_op jit(solution)/shard_map/ppermute | solution.py:29
  18.0 1.3 %collective-permute-done = bf16[7,2,256]{2,1,0:T(2,128)(2,1)S(1)} collective-permute-done((bf16[7,2,256]{2,1,0:T(2,128)(2,1)S(1)}, bf16[7,2,256]{2,1,0:T(2,128)(2,1)S(1)}, u32[]{:S(2)}, u32[]{:S(2)}) %collective-permute-start) | collective-permute-done | bytes 7200 | tf_op jit(solution)/shard_map/ppermute | solution.py:28
  19.3 0.1 collective-permute-done.1
  19.4 3.5 %collective-permute-start.2 = (bf16[2,28,256]{2,1,0:T(8,128)(2,1)S(1)}, bf16[2,28,256]{2,1,0:T(8,128)(2,1)S(1)}, u32[]{:S(2)}, u32[]{:S(2)}) collective-permute-start(bf16[2,28,256]{2,1,0:T(8,128)(2,1)S(1)} %fusion.18), channel_id=1, source_target_pairs={{0,32},{4,36},{8,40},{12,44},{16,48},{20,52},{24,56},{28,60},{32,0... | collective-permute-start | bytes 86024 | tf_op jit(solution)/shard_map/ppermute | solution.py:47
  22.8 3.5 %collective-permute-done.2 = bf16[2,28,256]{2,1,0:T(8,128)(2,1)S(1)} collective-permute-done((bf16[2,28,256]{2,1,0:T(8,128)(2,1)S(1)}, bf16[2,28,256]{2,1,0:T(8,128)(2,1)S(1)}, u32[]{:S(2)}, u32[]{:S(2)}) %collective-permute-start.2) | collective-permute-done | bytes 28704 | tf_op jit(solution)/shard_map/ppermute | solution.py:47
  26.4 0.1 maximum_select_fusion
  26.4 3.2 %collective-permute-start.3 = (bf16[9,28,256]{2,1,0:T(8,128)(2,1)S(1)}, bf16[9,28,256]{2,1,0:T(8,128)(2,1)S(1)}, u32[]{:S(2)}, u32[]{:S(2)}) collective-permute-start(bf16[9,28,256]{2,1,0:T(8,128)(2,1)S(1)} %maximum_select_fusion), channel_id=1, source_target_pairs={{0,64},{64,0},{1,65},{65,1},{2,66},{66,2},{3,67},{67,3},{4,68},{68... | collective-permute-start | bytes 387080 | tf_op jit(solution)/shard_map/ppermute | solution.py:53
  29.6 3.8 %collective-permute-done.3 = bf16[9,28,256]{2,1,0:T(8,128)(2,1)S(1)} collective-permute-done((bf16[9,28,256]{2,1,0:T(8,128)(2,1)S(1)}, bf16[9,28,256]{2,1,0:T(8,128)(2,1)S(1)}, u32[]{:S(2)}, u32[]{:S(2)}) %collective-permute-start.3) | collective-permute-done | bytes 129056 | tf_op jit(solution)/shard_map/ppermute | solution.py:53
  33.6 0.1 fusion.5
  33.7 0.1 slice_dynamic-update-slice_fusion.7
  33.8 0.1 slice_dynamic-update-slice_fusion.6
  33.9 0.1 slice_dynamic-update-slice_fusion.4
  34.0 0.1 slice_dynamic-update-slice_fusion.3
  34.1 0.1 slice_dynamic-update-slice_fusion.1
  34.2 0.1 slice_dynamic-update-slice_fusion
  34.3 2.1 %reshape.284.cells_ref = bf16[416,2304]{1,0:T(8,128)(2,1)} reshape(bf16[16,26,2304]{2,1,0:T(8,128)(2,1)S(1)} %slice_dynamic-update-slice_fusion) | data formatting | bytes 3833856 | tf_op jit(solution)/shard_map/reshape | solution.py:60
  36.4 23.9 %all-gather.3.cloned.1.call-done = bf16[32,9,16,512]{3,2,1,0:T(8,128)(2,1)} async-done(((bf16[2,9,16,512]{3,2,1,0:T(8,128)(2,1)}), bf16[32,9,16,512]{3,2,1,0:T(8,128)(2,1)}) %all-gather.3.cloned.1.call-update) | async-done | bytes 4718608 | tf_op jit(solution)/shard_map/all_gather | solution.py:110
  60.3 4.0 %shard_map.55 = bf16[1,4,416,128]{3,2,1,0:T(8,128)(2,1)} custom-call(bf16[416,2304]{1,0:T(8,128)(2,1)} %reshape.284.cells_ref, bf16[16,2,9,16,512]{4,3,2,1,0:T(8,128)(2,1)} %bitcast.59), custom_call_target="tpu_custom_call" | custom-call | flops 981467136 | bytes 4276224 | tf_op jit(solution)/shard_map/pallas_call | solution.py:83
  64.3 6.7 %all-to-all-start = ((bf16[4,416,128]{2,1,0:T(8,128)(2,1)}), bf16[4,416,128]{2,1,0:T(8,128)(2,1)S(1)}, u32[]{:S(2)}, u32[]{:S(2)}) async-start(bf16[4,416,128]{2,1,0:T(8,128)(2,1)} %bitcast.62), calls=%async_computation | async-start | bytes 851968 | tf_op jit(solution)/shard_map/all_to_all | solution.py:122
  71.0 13.6 %all-to-all-done = bf16[4,416,128]{2,1,0:T(8,128)(2,1)S(1)} async-done(((bf16[4,416,128]{2,1,0:T(8,128)(2,1)}), bf16[4,416,128]{2,1,0:T(8,128)(2,1)S(1)}, u32[]{:S(2)}, u32[]{:S(2)}) %all-to-all-start) | async-done | bytes 426016 | tf_op jit(solution)/shard_map/all_to_all | solution.py:122
  84.6 0.1 convert_reduce_fusion
  84.6 0.1 multiply_convert_fusion
  84.7 2.8 %collective-permute-start.4 = (bf16[416,128]{1,0:T(8,128)(2,1)S(1)}, bf16[416,128]{1,0:T(8,128)(2,1)S(1)}, u32[]{:S(2)}, u32[]{:S(2)}) collective-permute-start(bf16[416,128]{1,0:T(8,128)(2,1)S(1)} %multiply_convert_fusion), channel_id=1, source_target_pairs={{0,64},{64,0},{1,65},{65,1},{2,66},{66,2},{3,67},{67,3},{4,68},{68... | collective-permute-start | bytes 319496 | tf_op jit(solution)/shard_map/ppermute | solution.py:126
  87.5 3.8 %collective-permute-done.4 = bf16[416,128]{1,0:T(8,128)(2,1)S(1)} collective-permute-done((bf16[416,128]{1,0:T(8,128)(2,1)S(1)}, bf16[416,128]{1,0:T(8,128)(2,1)S(1)}, u32[]{:S(2)}, u32[]{:S(2)}) %collective-permute-start.4) | collective-permute-done | bytes 106528 | tf_op jit(solution)/shard_map/ppermute | solution.py:126
  91.3 0.1 broadcast_select_fusion.2
  91.4 0.1 pad_maximum_fusion.3
  91.5 0.1 slice.254
  91.6 0.1 slice_dynamic-update-slice_fusion.16
  91.6 0.1 slice_dynamic-update-slice_fusion.15
  91.7 0.1 slice.259
  91.8 0.1 slice_dynamic-update-slice_fusion.13
  91.9 0.1 slice_dynamic-update-slice_fusion.12
  92.0 0.1 slice.264
  92.0 0.1 slice_dynamic-update-slice_fusion.10
  92.1 0.1 slice_dynamic-update-slice_fusion.9
  92.2 1.2 copy-done
  93.4 3.6 %shard_map.56 = bf16[2,4,168,128]{3,2,1,0:T(8,128)(2,1)} custom-call(bf16[336,2304]{1,0:T(8,128)(2,1)} %bitcast.61, bf16[16,2,9,16,512]{4,3,2,1,0:T(8,128)(2,1)} %bitcast.60), custom_call_target="tpu_custom_call" | custom-call | flops 792723456 | bytes 3907584 | tf_op jit(solution)/shard_map/pallas_call | solution.py:83
  97.0 16.6 %all_to_all.10 = bf16[8,168,128]{2,1,0:T(8,128)(2,1)S(1)} all-to-all(bf16[8,168,128]{2,1,0:T(8,128)(2,1)} %bitcast.63), channel_id=1, replica_groups=mesh['x'=4,'ylo'=2,'z'=8,'core'=2,'ch'=4] {'ylo','ch'}, dimensions={0} | all-to-all | bytes 688128 | tf_op jit(solution)/shard_map/all_to_all | solution.py:134
  113.7 0.7 fusion.17
  (23 shorter events, 0.4 us)
Async XLA Ops:
  6.5 2.8 %copy-start.1 = (bf16[1,7,24,256]{3,2,1,0:T(8,128)(2,1)S(1)}, bf16[1,7,24,256]{3,2,1,0:T(8,128)(2,1)}, u32[]{:S(2)}) copy-start(bf16[1,7,24,256]{3,2,1,0:T(8,128)(2,1)} %param.5) | copy-start | bytes 258052
  6.5 53.7 %all-gather.3.cloned.1.call-start = ((), (), s32[]{:S(2)}) async-start(), calls=%async_computation.2 | async-start | bytes 5013504 | tf_op jit(solution)/shard_map/all_gather | solution.py:110
  9.4 9.8 %collective-permute-start = (bf16[7,2,256]{2,1,0:T(2,128)(2,1)S(1)}, bf16[7,2,256]{2,1,0:T(2,128)(2,1)S(1)}, u32[]{:S(2)}, u32[]{:S(2)}) collective-permute-start(bf16[7,2,256]{2,1,0:T(2,128)(2,1)S(1)} %get-tuple-element.38), channel_id=1, source_target_pairs={{0,4},{4,8},{8,12},{12,16},{16,20},{20,24},{24,28},{28,32},{32,36}... | collective-permute-start | bytes 21512 | tf_op jit(solution)/shard_map/ppermute | solution.py:28
  9.5 9.8 %collective-permute-start.1 = (bf16[7,2,256]{2,1,0:T(2,128)(2,1)S(1)}, bf16[7,2,256]{2,1,0:T(2,128)(2,1)S(1)}, u32[]{:S(2)}, u32[]{:S(2)}) collective-permute-start(bf16[7,2,256]{2,1,0:T(2,128)(2,1)S(1)} %get-tuple-element.39), channel_id=1, source_target_pairs={{4,0},{8,4},{12,8},{16,12},{20,16},{24,20},{28,24},{32,28},{36,32}... | collective-permute-start | bytes 21512 | tf_op jit(solution)/shard_map/ppermute | solution.py:29
  19.4 7.0 %collective-permute-start.2 = (bf16[2,28,256]{2,1,0:T(8,128)(2,1)S(1)}, bf16[2,28,256]{2,1,0:T(8,128)(2,1)S(1)}, u32[]{:S(2)}, u32[]{:S(2)}) collective-permute-start(bf16[2,28,256]{2,1,0:T(8,128)(2,1)S(1)} %fusion.18), channel_id=1, source_target_pairs={{0,32},{4,36},{8,40},{12,44},{16,48},{20,52},{24,56},{28,60},{32,0... | collective-permute-start | bytes 86024 | tf_op jit(solution)/shard_map/ppermute | solution.py:47
  26.4 7.0 %collective-permute-start.3 = (bf16[9,28,256]{2,1,0:T(8,128)(2,1)S(1)}, bf16[9,28,256]{2,1,0:T(8,128)(2,1)S(1)}, u32[]{:S(2)}, u32[]{:S(2)}) collective-permute-start(bf16[9,28,256]{2,1,0:T(8,128)(2,1)S(1)} %maximum_select_fusion), channel_id=1, source_target_pairs={{0,64},{64,0},{1,65},{65,1},{2,66},{66,2},{3,67},{67,3},{4,68},{68... | collective-permute-start | bytes 387080 | tf_op jit(solution)/shard_map/ppermute | solution.py:53
  60.3 10.7 %copy-start.3 = (f32[256]{0:T(256)S(1)}, f32[256]{0:T(256)}, u32[]{:S(2)}) copy-start(f32[256]{0:T(256)} %param.7) | copy-start | bytes 3076
  64.3 20.3 %all-to-all-start = ((bf16[4,416,128]{2,1,0:T(8,128)(2,1)}), bf16[4,416,128]{2,1,0:T(8,128)(2,1)S(1)}, u32[]{:S(2)}, u32[]{:S(2)}) async-start(bf16[4,416,128]{2,1,0:T(8,128)(2,1)} %bitcast.62), calls=%async_computation | async-start | bytes 851968 | tf_op jit(solution)/shard_map/all_to_all | solution.py:122
  84.7 6.6 %collective-permute-start.4 = (bf16[416,128]{1,0:T(8,128)(2,1)S(1)}, bf16[416,128]{1,0:T(8,128)(2,1)S(1)}, u32[]{:S(2)}, u32[]{:S(2)}) collective-permute-start(bf16[416,128]{1,0:T(8,128)(2,1)S(1)} %multiply_convert_fusion), channel_id=1, source_target_pairs={{0,64},{64,0},{1,65},{65,1},{2,66},{66,2},{3,67},{67,3},{4,68},{68... | collective-permute-start | bytes 319496 | tf_op jit(solution)/shard_map/ppermute | solution.py:126
  92.2 1.2 copy-start
  93.4 20.3 %copy-start.2 = (f32[256]{0:T(256)S(1)}, f32[256]{0:T(256)}, u32[]{:S(2)}) copy-start(f32[256]{0:T(256)} %param.9) | copy-start | bytes 3076
Sparse Core Ops, SparseCore 0:
  9.5 50.7 all-gather.2

commit v4 on v1

v4 whole, which is shorter than its diff:
```python
import jax
import jax.numpy as jnp
from jax import lax
from jax.sharding import Mesh, PartitionSpec as P

skip_scale = 0.7071067811865476
AXES = ("xh", "xl", "ylo", "z", "core", "ch")
LAT, LON, QUAD = ("xh", "xl", "ylo"), ("z", "core"), ("xl", "ylo")
SWAP = [(0, 1), (1, 0)]
LANES = 128
SLICE = 64


def silu(v):
    return jax.nn.silu(v.astype(jnp.float32)).astype(jnp.bfloat16)


def quarter(kernel, member, groups):
    taps, rows, outs = 9, kernel.shape[3], kernel.shape[4]
    column = lax.broadcasted_iota(jnp.int32, (outs, groups * SLICE), 1)
    wanted = column // SLICE * (outs // groups) + member * SLICE + column % SLICE
    pick = lax.broadcasted_iota(jnp.int32, wanted.shape, 0) == wanted
    flat = kernel.reshape(taps * rows, outs)
    chosen = jnp.dot(flat, pick.astype(flat.dtype), preferred_element_type=jnp.float32)
    return chosen.astype(flat.dtype).reshape(taps, rows, groups * SLICE)


def copies_of(block):
    return jnp.broadcast_to(block[None], (lax.axis_size("z"),) + block.shape)


def reduced(blocks, axis):
    me, count = lax.axis_index(axis), blocks.shape[0]
    total = lax.dynamic_index_in_dim(blocks, me, 0, keepdims=False).astype(jnp.float32)
    for d in range(1, count):
        sent = lax.dynamic_index_in_dim(blocks, lax.rem(me + d, count), 0, keepdims=False)
        came = lax.ppermute(sent, axis, [(i, (i + d) % count) for i in range(count)])
        total = total + came.astype(jnp.float32)
    return total


def from_quad(block):
    came = [block]
    for d in range(1, 4):
        came.append(lax.ppermute(block, QUAD, [(i, i ^ d) for i in range(4)]))
    return came


def lon_halo(block, width, lon):
    up = [(i, (i + 1) % lon) for i in range(lon)]
    down = [(j, i) for i, j in up]
    before = lax.ppermute(block[:, -width:], LON, up)
    after = lax.ppermute(block[:, :width], LON, down)
    return jnp.concatenate([before, block, after], axis=1)


def edge_pairs(lat, lon, far):
    pairs = []
    for i in range(lat):
        if i % 4 not in (0, 3):
            continue
        k = i - 1 if i % 4 == 0 else i + 1
        for j in range(lon):
            to = (k, j) if 0 <= k < lat else (i, (j + lon // 2) % lon)
            band = to[0] ^ 1 if far else to[0]
            pairs.append((i * lon + j, band * lon + to[1]))
    return pairs


def region(block, member, upper, lon):
    sent = jnp.where(member == 3, block[-2:], block[:2])
    near, far = (lax.ppermute(sent, LAT + LON, edge_pairs(8, lon, f)) for f in (False, True))
    past = jnp.where((member == 0) | (member == 3), near, far)
    past = jnp.where(upper == (member < 2), past[::-1], past)
    other = lax.ppermute(block, "ylo", SWAP)
    odd = member % 2 == 1
    both = [jnp.where(odd, other, block), jnp.where(odd, block, other), past]
    both = jnp.concatenate(both)
    other = lax.ppermute(both, "xl", SWAP)
    low, high = jnp.where(member < 2, both, other), jnp.where(member < 2, other, both)
    inner = 2 * block.shape[0]
    return jnp.concatenate([low[inner:], low[:inner], high])


def with_rims(ext, upper):
    first, final = ext[:3], ext[-3:]
    first = jnp.where(upper, first[::-1], first)
    final = jnp.where(upper, final, final[::-1])
    return jnp.concatenate([first, ext[1:-1], final])


def conv(cells, mine, other, core):
    low, high = jnp.where(core == 0, mine, other), jnp.where(core == 0, other, mine)
    kernel = jnp.stack([low, high], axis=1).transpose(2, 0, 1, 3, 4)
    kernel = kernel.reshape(3, 3, cells.shape[2], mine.shape[3])
    out = lax.conv_general_dilated(
        cells[None],
        kernel,
        (1, 1),
        "VALID",
        dimension_numbers=("NHWC", "HWIO", "NHWC"),
        preferred_element_type=jnp.float32,
    )
    return out[0].astype(jnp.bfloat16)


def folded(low, high):
    groups = low.shape[1] // SLICE
    cut = [slice(g * SLICE, (g + 1) * SLICE) for g in range(groups)]
    return jnp.stack([jnp.concatenate([low[:, c], high[:, c]], axis=1) for c in cut])


def body(features, kernel_one, bias_one, kernel_two, bias_two):
    lon = lax.axis_size("z") * lax.axis_size("core")
    groups = lax.axis_size("ch")
    member = lax.axis_index(QUAD).astype(jnp.int32)
    upper = lax.axis_index("xh") == 0
    core = lax.axis_index("core")
    own = features[0]
    height, breadth, width = own.shape

    first = silu(own)
    block = copies_of(quarter(kernel_one, member, groups))
    block, first = lax.optimization_barrier((block, first))
    mine = lax.all_to_all(block, "z", 0, 0)
    ext = lon_halo(region(first, member, upper, lon), 2, lon)
    other = lax.ppermute(mine, "core", SWAP)
    out = conv(with_rims(ext, upper), mine, other, core)
    out = jnp.concatenate([out[:1], out[3:-3], out[-1:]])
    half = 2 * height + 2
    partial = folded(
        out[:half].reshape(-1, out.shape[2]), out[-half:].reshape(-1, out.shape[2])
    )

    block = copies_of(quarter(kernel_two, member, groups))
    block, partial = lax.optimization_barrier((block, partial))
    mine = lax.all_to_all(block, "z", 0, 0)
    bias = lax.dynamic_slice_in_dim(bias_one, member * SLICE, SLICE, 0)
    hidden = reduced(partial, "ch") + jnp.concatenate([bias, bias])
    hidden, mine = lax.optimization_barrier((hidden, mine))
    other = lax.ppermute(mine, "core", SWAP)
    acts = from_quad(silu(hidden))
    acts = jnp.stack(acts).reshape(4, half, breadth + 2, LANES)
    acts = [lax.dynamic_index_in_dim(acts, member ^ k, 0, keepdims=False) for k in range(4)]
    acts = [jnp.concatenate([a[:-1, :, :SLICE], a[1:, :, SLICE:]]) for a in acts]
    out = conv(jnp.concatenate(acts, axis=2), mine, other, core)
    out = out.reshape(4, height * breadth, groups * SLICE)
    out = jnp.pad(out, ((0, 0), (0, (8 - height) * breadth), (0, 0)))
    partial = jnp.stack([folded(o[: 4 * breadth], o[4 * breadth :]) for o in out])
    parts = lax.all_to_all(partial.reshape(4 * groups, -1, LANES), QUAD + ("ch",), 0, 0)
    parts = parts.astype(jnp.float32).reshape(4, groups, -1, LANES).sum(1)
    first, rest = parts[:, :, :SLICE], parts[:, : (height - 4) * breadth, SLICE:]
    second = jnp.concatenate([first, rest], axis=1)
    second = jnp.concatenate([second[k] for k in range(4)], axis=1) + bias_two
    second = second.reshape(height, breadth, width)
    return ((own.astype(jnp.float32) + second) * skip_scale).astype(jnp.bfloat16)[None]


def solution(mesh):
    lat, lon, ch = (mesh.shape[name] for name in ("lat", "lon", "ch"))
    fine = Mesh(mesh.devices.reshape(lat // 4, 2, 2, lon // 2, 2, ch), AXES)
    field = P(None, LAT, LON, "ch")
    kernel = P(None, None, "ch", LON, None)
    return jax.shard_map(
        body,
        mesh=fine,
        in_specs=(field, kernel, P("ch"), kernel, P("ch")),
        out_specs=field,
        check_vma=False,
    )
```

time: 119 us -> 114 us (0.958)
  the two profiles are of different devices: /device:TPU:2 before, /device:TPU:14 now
where the time goes in v4:
time: 114 us; the launch traced here: 113 us
  starting transfers between devices  51.6 us (45%)
  waiting for transfers between devices  25.3 us (22%)
  blocking collectives  20 us (18%)
  local copies, waits for them, and re-layouts  6.53 us (6%)
  other arithmetic  5.42 us (5%)
  matrix products  3.4 us (3%)
    all_to_all x1, blocking collectives, body(): lax.all_to_all(partial.reshape(4 * groups, -1, LANES), QUAD + ('ch',), 0, 0)  20 us
    ppermute x3, starting transfers between devices, reduced(): lax.ppermute(sent, axis, [(i, (i + d) % count) for i in range(count)])  13.7 us
    ppermute x2, starting transfers between devices, region(): lax.ppermute(sent, LAT + LON, edge_pairs(8, lon, f))  12.2 us
    ppermute x3, starting transfers between devices, from_quad(): came.append(lax.ppermute(block, QUAD, [(i, i ^ d) for i in range(4)]))  9.21 us
    ppermute x3, waiting for transfers between devices, reduced(): lax.ppermute(sent, axis, [(i, (i + d) % count) for i in range(count)])  8.13 us
    all_to_all x2, starting transfers between devices, body(): mine = lax.all_to_all(block, 'z', 0, 0)  8.12 us
    ppermute x1, waiting for transfers between devices, region(): other = lax.ppermute(both, 'xl', SWAP)  6.05 us
    all_to_all x2, waiting for transfers between devices, body(): mine = lax.all_to_all(block, 'z', 0, 0)  4.76 us
  transfers between devices with their start and end apart: 16, of which 8 were waited for; matrix products, arithmetic and copies ran while one was open for 3% of the time, Pallas kernels for 0%

profile of v4, /device:TPU:14, one launch (start us, length us, event | category | flops | bytes accessed | tf_op | source)
XLA Modules:
  0.0 113.0 jit_solution(6160427930252110507)
XLA Ops:
  0.0 1.0 fusion.26
  1.0 0.3 convolution_convert_fusion
  1.4 0.9 broadcast_in_dim.26
  2.3 10.9 %collective-permute-start.1 = (bf16[2,24,256]{2,1,0:T(8,128)(2,1)S(1)}, bf16[2,24,256]{2,1,0:T(8,128)(2,1)S(1)}, u32[]{:S(2)}, u32[]{:S(2)}) collective-permute-start(bf16[2,24,256]{2,1,0:T(8,128)(2,1)S(1)} %slice_select_fusion), channel_id=1, source_target_pairs={{0,32},{4,36},{8,40},{12,44},{16,48},{20,52},{24,56},{28,60},{32,0... | collective-permute-start | bytes 73736 | tf_op jit(solution)/shard_map/ppermute | solution.py:72
  13.2 1.3 %collective-permute-start.2 = (bf16[2,24,256]{2,1,0:T(8,128)(2,1)S(1)}, bf16[2,24,256]{2,1,0:T(8,128)(2,1)S(1)}, u32[]{:S(2)}, u32[]{:S(2)}) collective-permute-start(bf16[2,24,256]{2,1,0:T(8,128)(2,1)S(1)} %slice_select_fusion), channel_id=1, source_target_pairs={{0,96},{4,100},{8,104},{12,108},{16,112},{20,116},{24,120},{28,124... | collective-permute-start | bytes 73736 | tf_op jit(solution)/shard_map/ppermute | solution.py:72
  14.5 1.9 %collective-permute-start = (bf16[7,24,256]{2,1,0:T(8,128)(2,1)S(1)}, bf16[7,24,256]{2,1,0:T(8,128)(2,1)S(1)}, u32[]{:S(2)}, u32[]{:S(2)}) collective-permute-start(bf16[7,24,256]{2,1,0:T(8,128)(2,1)S(1)} %fusion.26), channel_id=1, source_target_pairs={{0,64},{64,0},{1,65},{65,1},{2,66},{66,2},{3,67},{67,3},{4,68},{68... | collective-permute-start | bytes 258056 | tf_op jit(solution)/shard_map/ppermute | solution.py:75
  16.4 4.6 %all-to-all-start = ((bf16[8,9,16,256]{3,2,1,0:T(8,128)(2,1)}), bf16[8,9,16,256]{3,2,1,0:T(8,128)(2,1)S(1)}, u32[]{:S(2)}, u32[]{:S(2)}) async-start(bf16[8,9,16,256]{3,2,1,0:T(8,128)(2,1)} %broadcast_in_dim.26), calls=%async_computation | async-start | bytes 1179648 | tf_op jit(solution)/shard_map/all_to_all | solution.py:125
  21.1 1.9 %collective-permute-start.3 = (bf16[16,24,256]{2,1,0:T(8,128)(2,1)S(1)}, bf16[16,24,256]{2,1,0:T(8,128)(2,1)S(1)}, u32[]{:S(2)}, u32[]{:S(2)}) collective-permute-start(bf16[16,24,256]{2,1,0:T(8,128)(2,1)S(1)} %pad_maximum_fusion.5), channel_id=1, source_target_pairs={{0,128},{128,0},{1,129},{129,1},{2,130},{130,2},{3,131},{131,3},{4... | collective-permute-start | bytes 589832 | tf_op jit(solution)/shard_map/ppermute | solution.py:79
  23.0 6.0 %collective-permute-done.3 = bf16[16,24,256]{2,1,0:T(8,128)(2,1)S(1)} collective-permute-done((bf16[16,24,256]{2,1,0:T(8,128)(2,1)S(1)}, bf16[16,24,256]{2,1,0:T(8,128)(2,1)S(1)}, u32[]{:S(2)}, u32[]{:S(2)}) %collective-permute-start.3) | collective-permute-done | bytes 196640 | tf_op jit(solution)/shard_map/ppermute | solution.py:79
  29.2 0.6 collective-permute-start.5
  29.9 0.3 convolution_convert_fusion.1
  30.2 1.3 %collective-permute-done.5 = bf16[32,2,256]{2,1,0:T(2,128)(2,1)S(1)} collective-permute-done((bf16[32,2,256]{2,1,0:T(2,128)(2,1)S(1)}, bf16[32,2,256]{2,1,0:T(2,128)(2,1)S(1)}, u32[]{:S(2)}, u32[]{:S(2)}) %collective-permute-start.5) | collective-permute-done | bytes 32800 | tf_op jit(solution)/shard_map/ppermute | solution.py:53
  31.5 3.2 %collective-permute-done.4 = bf16[32,2,256]{2,1,0:T(2,128)(2,1)S(1)} collective-permute-done((bf16[32,2,256]{2,1,0:T(2,128)(2,1)S(1)}, bf16[32,2,256]{2,1,0:T(2,128)(2,1)S(1)}, u32[]{:S(2)}, u32[]{:S(2)}) %collective-permute-start.4) | collective-permute-done | bytes 32800 | tf_op jit(solution)/shard_map/ppermute | solution.py:52
  34.7 0.3 pad_maximum_fusion
  35.0 4.8 %all-to-all-done = bf16[8,9,16,256]{3,2,1,0:T(8,128)(2,1)S(1)} async-done(((bf16[8,9,16,256]{3,2,1,0:T(8,128)(2,1)}), bf16[8,9,16,256]{3,2,1,0:T(8,128)(2,1)S(1)}, u32[]{:S(2)}, u32[]{:S(2)}) %all-to-all-start) | async-done | bytes 589856 | tf_op jit(solution)/shard_map/all_to_all | solution.py:125
  39.7 1.9 %collective-permute-start.6 = (bf16[8,9,16,256]{3,2,1,0:T(8,128)(2,1)S(1)}, bf16[8,9,16,256]{3,2,1,0:T(8,128)(2,1)S(1)}, u32[]{:S(2)}, u32[]{:S(2)}) collective-permute-start(bf16[8,9,16,256]{3,2,1,0:T(8,128)(2,1)S(1)} %all-to-all-done), channel_id=1, source_target_pairs={{0,4},{4,0},{1,5},{5,1},{2,6},{6,2},{3,7},{7,3},{8,12},{12,8},{9,1... | collective-permute-start | bytes 1769480 | tf_op jit(solution)/shard_map/ppermute | solution.py:127
  41.9 0.1 reshape.143
  42.3 1.4 %collective-permute-done.6 = bf16[8,9,16,256]{3,2,1,0:T(8,128)(2,1)S(1)} collective-permute-done((bf16[8,9,16,256]{3,2,1,0:T(8,128)(2,1)S(1)}, bf16[8,9,16,256]{3,2,1,0:T(8,128)(2,1)S(1)}, u32[]{:S(2)}, u32[]{:S(2)}) %collective-permute-start.6) | collective-permute-done | bytes 589856 | tf_op jit(solution)/shard_map/ppermute | solution.py:127
  43.7 0.1 maximum_bitcast_fusion
  43.8 0.2 copy.20
  44.0 0.5 copy-done.6
  44.5 1.5 %fusion.2 = bf16[34,8,4,256]{3,1,2,0:T(8,128)(2,1)S(1)} fusion(bf16[3,3,256,256]{3,2,1,0:T(8,128)(2,1)S(1)} %bitcast.161, bf16[36,1,7,2,256]{4,2,3,0,1:T(8,128)(2,1)S(1)} %slice.374, bf16[36,1,8,4,256]{4,2,3,0,1:T(8,128)(2,1)S(1)} %copy.19, pred[8,4]{0,1:T(4,128)(4,1)S(1)} %copy-done.6), kind=kOutput, calls=%fused_computation.5 | convolution fusion | flops 1286668288 | bytes 2584608 | tf_op jit(solution)/shard_map/conv_general_dilated | solution.py:96
  46.0 0.2 copy.22
  46.2 0.1 reshape.149
  46.6 0.1 fusion.46
  46.8 0.1 fusion.45
  47.5 0.9 broadcast_in_dim.24
  48.3 3.5 %all-to-all-start.1 = ((bf16[8,9,16,256]{3,2,1,0:T(8,128)(2,1)}), bf16[8,9,16,256]{3,2,1,0:T(8,128)(2,1)S(1)}, u32[]{:S(2)}, u32[]{:S(2)}) async-start(bf16[8,9,16,256]{3,2,1,0:T(8,128)(2,1)} %broadcast_in_dim.24), calls=%async_computation.1 | async-start | bytes 1179648 | tf_op jit(solution)/shard_map/all_to_all | solution.py:137
  52.0 5.4 %collective-permute-start.9 = (bf16[416,128]{1,0:T(8,128)(2,1)S(1)}, bf16[416,128]{1,0:T(8,128)(2,1)S(1)}, u32[]{:S(2)}, u32[]{:S(2)}) collective-permute-start(bf16[416,128]{1,0:T(8,128)(2,1)S(1)} %get-tuple-element.32), channel_id=1, source_target_pairs={{0,3},{1,0},{2,1},{3,2},{4,7},{5,4},{6,5},{7,6},{8,11},{9,8},{10,9... | collective-permute-start | bytes 319496 | tf_op jit(solution)/shard_map/ppermute | solution.py:37
  57.4 4.6 %collective-permute-start.8 = (bf16[416,128]{1,0:T(8,128)(2,1)S(1)}, bf16[416,128]{1,0:T(8,128)(2,1)S(1)}, u32[]{:S(2)}, u32[]{:S(2)}) collective-permute-start(bf16[416,128]{1,0:T(8,128)(2,1)S(1)} %get-tuple-element.33), channel_id=1, source_target_pairs={{0,2},{1,3},{2,0},{3,1},{4,6},{5,7},{6,4},{7,5},{8,10},{9,11},{10,... | collective-permute-start | bytes 319496 | tf_op jit(solution)/shard_map/ppermute | solution.py:37
  62.0 3.8 %collective-permute-start.7 = (bf16[416,128]{1,0:T(8,128)(2,1)S(1)}, bf16[416,128]{1,0:T(8,128)(2,1)S(1)}, u32[]{:S(2)}, u32[]{:S(2)}) collective-permute-start(bf16[416,128]{1,0:T(8,128)(2,1)S(1)} %get-tuple-element.31), channel_id=1, source_target_pairs={{0,1},{1,2},{2,3},{3,0},{4,5},{5,6},{6,7},{7,4},{8,9},{9,10},{10,1... | collective-permute-start | bytes 319496 | tf_op jit(solution)/shard_map/ppermute | solution.py:37
  65.9 4.8 %collective-permute-done.8 = bf16[416,128]{1,0:T(8,128)(2,1)S(1)} collective-permute-done((bf16[416,128]{1,0:T(8,128)(2,1)S(1)}, bf16[416,128]{1,0:T(8,128)(2,1)S(1)}, u32[]{:S(2)}, u32[]{:S(2)}) %collective-permute-start.8) | collective-permute-done | bytes 106528 | tf_op jit(solution)/shard_map/ppermute | solution.py:37
  70.7 3.3 %collective-permute-done.7 = bf16[416,128]{1,0:T(8,128)(2,1)S(1)} collective-permute-done((bf16[416,128]{1,0:T(8,128)(2,1)S(1)}, bf16[416,128]{1,0:T(8,128)(2,1)S(1)}, u32[]{:S(2)}, u32[]{:S(2)}) %collective-permute-start.7) | collective-permute-done | bytes 106528 | tf_op jit(solution)/shard_map/ppermute | solution.py:37
  74.2 1.9 %collective-permute-start.10 = (bf16[416,128]{1,0:T(8,128)(2,1)S(1)}, bf16[416,128]{1,0:T(8,128)(2,1)S(1)}, u32[]{:S(2)}, u32[]{:S(2)}) collective-permute-start(bf16[416,128]{1,0:T(8,128)(2,1)S(1)} %multiply_convert_fusion), channel_id=1, source_target_pairs={{0,64},{64,0},{128,192},{192,128},{1,65},{65,1},{129,193},{193,129... | collective-permute-start | bytes 319496 | tf_op jit(solution)/shard_map/ppermute | solution.py:45
  76.1 1.9 %collective-permute-start.11 = (bf16[416,128]{1,0:T(8,128)(2,1)S(1)}, bf16[416,128]{1,0:T(8,128)(2,1)S(1)}, u32[]{:S(2)}, u32[]{:S(2)}) collective-permute-start(bf16[416,128]{1,0:T(8,128)(2,1)S(1)} %multiply_convert_fusion), channel_id=1, source_target_pairs={{0,128},{64,192},{128,0},{192,64},{1,129},{65,193},{129,1},{193,65... | collective-permute-start | bytes 319496 | tf_op jit(solution)/shard_map/ppermute | solution.py:45
  78.0 5.4 %collective-permute-start.12 = (bf16[416,128]{1,0:T(8,128)(2,1)S(1)}, bf16[416,128]{1,0:T(8,128)(2,1)S(1)}, u32[]{:S(2)}, u32[]{:S(2)}) collective-permute-start(bf16[416,128]{1,0:T(8,128)(2,1)S(1)} %multiply_convert_fusion), channel_id=1, source_target_pairs={{0,192},{64,128},{128,64},{192,0},{1,193},{65,129},{129,65},{193,1... | collective-permute-start | bytes 319496 | tf_op jit(solution)/shard_map/ppermute | solution.py:45
  83.4 1.9 %collective-permute-start.13 = (bf16[8,9,16,256]{3,2,1,0:T(8,128)(2,1)S(1)}, bf16[8,9,16,256]{3,2,1,0:T(8,128)(2,1)S(1)}, u32[]{:S(2)}, u32[]{:S(2)}) collective-permute-start(bf16[8,9,16,256]{3,2,1,0:T(8,128)(2,1)S(1)} %all-to-all-done.1), channel_id=1, source_target_pairs={{0,4},{4,0},{1,5},{5,1},{2,6},{6,2},{3,7},{7,3},{8,12},{12,8},{9,1... | collective-permute-start | bytes 1769480 | tf_op jit(solution)/shard_map/ppermute | solution.py:141
  85.5 0.6 collective-permute-done.12
  86.7 0.3 maximum_bitcast_fusion.3
  87.1 0.1 reshape.154
  87.4 0.1 maximum_bitcast_fusion.1
  87.6 0.2 copy.26
  87.7 0.5 copy-done.5
  88.2 1.2 %fusion.3 = bf16[28,8,4,256]{3,1,2,0:T(8,128)(2,1)S(1)} fusion(bf16[3,3,256,256]{3,2,1,0:T(8,128)(2,1)S(1)} %bitcast.162, bf16[30,1,7,2,256]{4,2,3,0,1:T(8,128)(2,1)S(1)} %slice.397, bf16[30,1,8,4,256]{4,2,3,0,1:T(8,128)(2,1)S(1)} %copy.25, pred[8,4]{0,1:T(4,128)(4,1)S(1)} %copy-done.5), kind=kOutput, calls=%fused_computation.7 | convolution fusion | flops 1059635200 | bytes 2344992 | tf_op jit(solution)/shard_map/conv_general_dilated | solution.py:96
  89.5 0.2 copy.27
  89.7 0.1 reshape.158
  92.1 20.0 %all_to_all.15 = bf16[16,96,128]{2,1,0:T(8,128)(2,1)S(1)} all-to-all(bf16[16,96,128]{2,1,0:T(8,128)(2,1)S(1)} %bitcast.159), channel_id=1, replica_groups=mesh['xh'=2,'xl'=2,'ylo'=2,'z'=8,'core'=2,'ch'=4] {'xl','ylo','ch'}, dimensions={0} | all-to-all | bytes 786432 | tf_op jit(solution)/shard_map/all_to_all | solution.py:150
  112.3 0.8 fusion.28
  (115 shorter events, 5.2 us)
Async XLA Ops:
  0.0 1.0 copy-start
  2.3 18.7 %collective-permute-start.1 = (bf16[2,24,256]{2,1,0:T(8,128)(2,1)S(1)}, bf16[2,24,256]{2,1,0:T(8,128)(2,1)S(1)}, u32[]{:S(2)}, u32[]{:S(2)}) collective-permute-start(bf16[2,24,256]{2,1,0:T(8,128)(2,1)S(1)} %slice_select_fusion), channel_id=1, source_target_pairs={{0,32},{4,36},{8,40},{12,44},{16,48},{20,52},{24,56},{28,60},{32,0... | collective-permute-start | bytes 73736 | tf_op jit(solution)/shard_map/ppermute | solution.py:72
  13.2 7.8 %collective-permute-start.2 = (bf16[2,24,256]{2,1,0:T(8,128)(2,1)S(1)}, bf16[2,24,256]{2,1,0:T(8,128)(2,1)S(1)}, u32[]{:S(2)}, u32[]{:S(2)}) collective-permute-start(bf16[2,24,256]{2,1,0:T(8,128)(2,1)S(1)} %slice_select_fusion), channel_id=1, source_target_pairs={{0,96},{4,100},{8,104},{12,108},{16,112},{20,116},{24,120},{28,124... | collective-permute-start | bytes 73736 | tf_op jit(solution)/shard_map/ppermute | solution.py:72
  14.5 6.6 %collective-permute-start = (bf16[7,24,256]{2,1,0:T(8,128)(2,1)S(1)}, bf16[7,24,256]{2,1,0:T(8,128)(2,1)S(1)}, u32[]{:S(2)}, u32[]{:S(2)}) collective-permute-start(bf16[7,24,256]{2,1,0:T(8,128)(2,1)S(1)} %fusion.26), channel_id=1, source_target_pairs={{0,64},{64,0},{1,65},{65,1},{2,66},{66,2},{3,67},{67,3},{4,68},{68... | collective-permute-start | bytes 258056 | tf_op jit(solution)/shard_map/ppermute | solution.py:75
  16.4 23.3 %all-to-all-start = ((bf16[8,9,16,256]{3,2,1,0:T(8,128)(2,1)}), bf16[8,9,16,256]{3,2,1,0:T(8,128)(2,1)S(1)}, u32[]{:S(2)}, u32[]{:S(2)}) async-start(bf16[8,9,16,256]{3,2,1,0:T(8,128)(2,1)} %broadcast_in_dim.26), calls=%async_computation | async-start | bytes 1179648 | tf_op jit(solution)/shard_map/all_to_all | solution.py:125
  21.0 8.8 %copy-start.3 = (bf16[3,3,1,16,1024]{4,3,2,1,0:T(8,128)(2,1)S(1)}, bf16[3,3,1,16,1024]{4,3,2,1,0:T(8,128)(2,1)}, u32[]{:S(2)}) copy-start(bf16[3,3,1,16,1024]{4,3,2,1,0:T(8,128)(2,1)} %param.8) | copy-start | bytes 884740
  21.1 8.0 %collective-permute-start.3 = (bf16[16,24,256]{2,1,0:T(8,128)(2,1)S(1)}, bf16[16,24,256]{2,1,0:T(8,128)(2,1)S(1)}, u32[]{:S(2)}, u32[]{:S(2)}) collective-permute-start(bf16[16,24,256]{2,1,0:T(8,128)(2,1)S(1)} %pad_maximum_fusion.5), channel_id=1, source_target_pairs={{0,128},{128,0},{1,129},{129,1},{2,130},{130,2},{3,131},{131,3},{4... | collective-permute-start | bytes 589832 | tf_op jit(solution)/shard_map/ppermute | solution.py:79
  29.2 2.3 %collective-permute-start.5 = (bf16[32,2,256]{2,1,0:T(2,128)(2,1)S(1)}, bf16[32,2,256]{2,1,0:T(2,128)(2,1)S(1)}, u32[]{:S(2)}, u32[]{:S(2)}) collective-permute-start(bf16[32,2,256]{2,1,0:T(2,128)(2,1)S(1)} %get-tuple-element.35), channel_id=1, source_target_pairs={{4,0},{8,4},{12,8},{16,12},{20,16},{24,20},{28,24},{32,28},{36,32}... | collective-permute-start | bytes 98312 | tf_op jit(solution)/shard_map/ppermute | solution.py:53
  29.9 4.8 %collective-permute-start.4 = (bf16[32,2,256]{2,1,0:T(2,128)(2,1)S(1)}, bf16[32,2,256]{2,1,0:T(2,128)(2,1)S(1)}, u32[]{:S(2)}, u32[]{:S(2)}) collective-permute-start(bf16[32,2,256]{2,1,0:T(2,128)(2,1)S(1)} %get-tuple-element.34), channel_id=1, source_target_pairs={{0,4},{4,8},{8,12},{12,16},{16,20},{20,24},{24,28},{28,32},{32,36}... | collective-permute-start | bytes 98312 | tf_op jit(solution)/shard_map/ppermute | solution.py:52
  39.7 3.9 %collective-permute-start.6 = (bf16[8,9,16,256]{3,2,1,0:T(8,128)(2,1)S(1)}, bf16[8,9,16,256]{3,2,1,0:T(8,128)(2,1)S(1)}, u32[]{:S(2)}, u32[]{:S(2)}) collective-permute-start(bf16[8,9,16,256]{3,2,1,0:T(8,128)(2,1)S(1)} %all-to-all-done), channel_id=1, source_target_pairs={{0,4},{4,0},{1,5},{5,1},{2,6},{6,2},{3,7},{7,3},{8,12},{12,8},{9,1... | collective-permute-start | bytes 1769480 | tf_op jit(solution)/shard_map/ppermute | solution.py:127
  43.8 0.7 copy-start.6
  47.5 4.4 %copy-start.4 = (f32[256]{0:T(256)S(1)}, f32[256]{0:T(256)}, u32[]{:S(2)}) copy-start(f32[256]{0:T(256)} %param.7) | copy-start | bytes 3076
  48.3 25.7 %all-to-all-start.1 = ((bf16[8,9,16,256]{3,2,1,0:T(8,128)(2,1)}), bf16[8,9,16,256]{3,2,1,0:T(8,128)(2,1)S(1)}, u32[]{:S(2)}, u32[]{:S(2)}) async-start(bf16[8,9,16,256]{3,2,1,0:T(8,128)(2,1)} %broadcast_in_dim.24), calls=%async_computation.1 | async-start | bytes 1179648 | tf_op jit(solution)/shard_map/all_to_all | solution.py:137
  52.0 13.8 %collective-permute-start.9 = (bf16[416,128]{1,0:T(8,128)(2,1)S(1)}, bf16[416,128]{1,0:T(8,128)(2,1)S(1)}, u32[]{:S(2)}, u32[]{:S(2)}) collective-permute-start(bf16[416,128]{1,0:T(8,128)(2,1)S(1)} %get-tuple-element.32), channel_id=1, source_target_pairs={{0,3},{1,0},{2,1},{3,2},{4,7},{5,4},{6,5},{7,6},{8,11},{9,8},{10,9... | collective-permute-start | bytes 319496 | tf_op jit(solution)/shard_map/ppermute | solution.py:37
  57.4 13.2 %collective-permute-start.8 = (bf16[416,128]{1,0:T(8,128)(2,1)S(1)}, bf16[416,128]{1,0:T(8,128)(2,1)S(1)}, u32[]{:S(2)}, u32[]{:S(2)}) collective-permute-start(bf16[416,128]{1,0:T(8,128)(2,1)S(1)} %get-tuple-element.33), channel_id=1, source_target_pairs={{0,2},{1,3},{2,0},{3,1},{4,6},{5,7},{6,4},{7,5},{8,10},{9,11},{10,... | collective-permute-start | bytes 319496 | tf_op jit(solution)/shard_map/ppermute | solution.py:37
  62.0 12.0 %collective-permute-start.7 = (bf16[416,128]{1,0:T(8,128)(2,1)S(1)}, bf16[416,128]{1,0:T(8,128)(2,1)S(1)}, u32[]{:S(2)}, u32[]{:S(2)}) collective-permute-start(bf16[416,128]{1,0:T(8,128)(2,1)S(1)} %get-tuple-element.31), channel_id=1, source_target_pairs={{0,1},{1,2},{2,3},{3,0},{4,5},{5,6},{6,7},{7,4},{8,9},{9,10},{10,1... | collective-permute-start | bytes 319496 | tf_op jit(solution)/shard_map/ppermute | solution.py:37
  74.2 11.2 %collective-permute-start.10 = (bf16[416,128]{1,0:T(8,128)(2,1)S(1)}, bf16[416,128]{1,0:T(8,128)(2,1)S(1)}, u32[]{:S(2)}, u32[]{:S(2)}) collective-permute-start(bf16[416,128]{1,0:T(8,128)(2,1)S(1)} %multiply_convert_fusion), channel_id=1, source_target_pairs={{0,64},{64,0},{128,192},{192,128},{1,65},{65,1},{129,193},{193,129... | collective-permute-start | bytes 319496 | tf_op jit(solution)/shard_map/ppermute | solution.py:45
  76.1 9.3 %collective-permute-start.11 = (bf16[416,128]{1,0:T(8,128)(2,1)S(1)}, bf16[416,128]{1,0:T(8,128)(2,1)S(1)}, u32[]{:S(2)}, u32[]{:S(2)}) collective-permute-start(bf16[416,128]{1,0:T(8,128)(2,1)S(1)} %multiply_convert_fusion), channel_id=1, source_target_pairs={{0,128},{64,192},{128,0},{192,64},{1,129},{65,193},{129,1},{193,65... | collective-permute-start | bytes 319496 | tf_op jit(solution)/shard_map/ppermute | solution.py:45
  78.0 8.0 %collective-permute-start.12 = (bf16[416,128]{1,0:T(8,128)(2,1)S(1)}, bf16[416,128]{1,0:T(8,128)(2,1)S(1)}, u32[]{:S(2)}, u32[]{:S(2)}) collective-permute-start(bf16[416,128]{1,0:T(8,128)(2,1)S(1)} %multiply_convert_fusion), channel_id=1, source_target_pairs={{0,192},{64,128},{128,64},{192,0},{1,193},{65,129},{129,65},{193,1... | collective-permute-start | bytes 319496 | tf_op jit(solution)/shard_map/ppermute | solution.py:45
  83.4 3.9 %collective-permute-start.13 = (bf16[8,9,16,256]{3,2,1,0:T(8,128)(2,1)S(1)}, bf16[8,9,16,256]{3,2,1,0:T(8,128)(2,1)S(1)}, u32[]{:S(2)}, u32[]{:S(2)}) collective-permute-start(bf16[8,9,16,256]{3,2,1,0:T(8,128)(2,1)S(1)} %all-to-all-done.1), channel_id=1, source_target_pairs={{0,4},{4,0},{1,5},{5,1},{2,6},{6,2},{3,7},{7,3},{8,12},{12,8},{9,1... | collective-permute-start | bytes 1769480 | tf_op jit(solution)/shard_map/ppermute | solution.py:141
  87.6 0.7 copy-start.5
  92.1 20.2 %copy-start.1 = (bf16[1,7,24,256]{3,2,1,0:T(8,128)(2,1)S(1)}, bf16[1,7,24,256]{3,2,1,0:T(8,128)(2,1)}, u32[]{:S(2)}) copy-start(bf16[1,7,24,256]{3,2,1,0:T(8,128)(2,1)} %param.5) | copy-start | bytes 258052
  92.1 20.2 %copy-start.2 = (f32[256]{0:T(256)S(1)}, f32[256]{0:T(256)}, u32[]{:S(2)}) copy-start(f32[256]{0:T(256)} %param.9) | copy-start | bytes 3076

commit v5 on v4

--- a/solution.py
+++ b/solution.py
@@ -39,11 +39,14 @@
     return total
 
 
-def from_quad(block):
-    came = [block]
-    for d in range(1, 4):
-        came.append(lax.ppermute(block, QUAD, [(i, i ^ d) for i in range(4)]))
-    return came
+def from_quad(block, member):
+    blocks = block[None]
+    for axis, later in (("ylo", member % 2 == 1), ("xl", member >= 2)):
+        other = lax.ppermute(blocks, axis, SWAP)
+        blocks = jnp.concatenate(
+            [jnp.where(later, other, blocks), jnp.where(later, blocks, other)]
+        )
+    return blocks
 
 
 def lon_halo(block, width, lon):
@@ -104,10 +107,22 @@
     return out[0].astype(jnp.bfloat16)
 
 
-def folded(low, high):
-    groups = low.shape[1] // SLICE
-    cut = [slice(g * SLICE, (g + 1) * SLICE) for g in range(groups)]
-    return jnp.stack([jnp.concatenate([low[:, c], high[:, c]], axis=1) for c in cut])
+def folded(cells, size):
+    short = 2 * size - cells.shape[-2]
+    low, high = cells[..., :size, :], cells[..., size:, :]
+    high = jnp.pad(high, [(0, 0)] * (cells.ndim - 2) + [(0, short), (0, 0)])
+    cut = [slice(g * SLICE, (g + 1) * SLICE) for g in range(cells.shape[-1] // SLICE)]
+    return jnp.stack([jnp.concatenate([low[..., c], high[..., c]], -1) for c in cut], -3)
+
+
+def unfolded(blocks, count):
+    size = blocks.shape[-2]
+    low, high = blocks[..., :SLICE], blocks[..., : count - size, SLICE:]
+    return jnp.concatenate([low, high], -2)
+
+
+def half_of(count):
+    return -(-count // 16) * 8
 
 
 def body(features, kernel_one, bias_one, kernel_two, bias_two):
@@ -123,34 +138,30 @@
     block = copies_of(quarter(kernel_one, member, groups))
     block, first = lax.optimization_barrier((block, first))
     mine = lax.all_to_all(block, "z", 0, 0)
-    ext = lon_halo(region(first, member, upper, lon), 2, lon)
+    ext = region(first, member, upper, lon)
+    block, ext = lax.optimization_barrier((copies_of(quarter(kernel_two, member, groups)), ext))
+    ext = lon_halo(ext, 2, lon)
     other = lax.ppermute(mine, "core", SWAP)
     out = conv(with_rims(ext, upper), mine, other, core)
     out = jnp.concatenate([out[:1], out[3:-3], out[-1:]])
-    half = 2 * height + 2
-    partial = folded(
-        out[:half].reshape(-1, out.shape[2]), out[-half:].reshape(-1, out.shape[2])
-    )
+    rows, columns = out.shape[0], out.shape[1]
+    count = rows * columns
+    partial = folded(out.reshape(count, -1), half_of(count))
 
-    block = copies_of(quarter(kernel_two, member, groups))
     block, partial = lax.optimization_barrier((block, partial))
     mine = lax.all_to_all(block, "z", 0, 0)
     bias = lax.dynamic_slice_in_dim(bias_one, member * SLICE, SLICE, 0)
     hidden = reduced(partial, "ch") + jnp.concatenate([bias, bias])
     hidden, mine = lax.optimization_barrier((hidden, mine))
     other = lax.ppermute(mine, "core", SWAP)
-    acts = from_quad(silu(hidden))
-    acts = jnp.stack(acts).reshape(4, half, breadth + 2, LANES)
-    acts = [lax.dynamic_index_in_dim(acts, member ^ k, 0, keepdims=False) for k in range(4)]
-    acts = [jnp.concatenate([a[:-1, :, :SLICE], a[1:, :, SLICE:]]) for a in acts]
-    out = conv(jnp.concatenate(acts, axis=2), mine, other, core)
-    out = out.reshape(4, height * breadth, groups * SLICE)
-    out = jnp.pad(out, ((0, 0), (0, (8 - height) * breadth), (0, 0)))
-    partial = jnp.stack([folded(o[: 4 * breadth], o[4 * breadth :]) for o in out])
+    acts = unfolded(from_quad(silu(hidden), member), count)
+    acts = jnp.concatenate([acts[k] for k in range(4)], axis=1)
+    out = conv(acts.reshape(rows, columns, -1), mine, other, core)
+    count = height * breadth
+    partial = folded(out.reshape(4, count, -1), half_of(count))
     parts = lax.all_to_all(partial.reshape(4 * groups, -1, LANES), QUAD + ("ch",), 0, 0)
     parts = parts.astype(jnp.float32).reshape(4, groups, -1, LANES).sum(1)
-    first, rest = parts[:, :, :SLICE], parts[:, : (height - 4) * breadth, SLICE:]
-    second = jnp.concatenate([first, rest], axis=1)
+    second = unfolded(parts, count)
     second = jnp.concatenate([second[k] for k in range(4)], axis=1) + bias_two
     second = second.reshape(height, breadth, width)
     return ((own.astype(jnp.float32) + second) * skip_scale).astype(jnp.bfloat16)[None]

time: 114 us -> 111 us (0.974)
  waiting for transfers between devices: 25.3 us -> 31.8 us
  starting transfers between devices: 51.6 us -> 46.3 us
  blocking collectives: 20 us -> 17.5 us
    ppermute x3 -> x2, waiting for transfers between devices: 0.56 us -> 8.35 us  [from_quad(): other = lax.ppermute(blocks, axis, SWAP)]
    ppermute x3 -> x2, starting transfers between devices: 9.21 us -> 3.84 us  [from_quad(): other = lax.ppermute(blocks, axis, SWAP)]
    ppermute x1, waiting for transfers between devices: 1.26 us -> 4.1 us  [lon_halo(): after = lax.ppermute(block[:, :width], LON, down)]
    ppermute x1, waiting for transfers between devices: 3.18 us -> 0.57 us  [lon_halo(): before = lax.ppermute(block[:, -width:], LON, up)]
    all_to_all x1, blocking collectives: 20 us -> 17.5 us  [body(): lax.all_to_all(partial.reshape(4 * groups, -1, LANES), QUAD + ('ch',), 0, 0)]
  transfers between devices with their start and end apart: 16 -> 15, of which waited for: 8 -> 9; matrix products, arithmetic and copies ran while one was open for 3% -> 3% of each run, Pallas kernels for 0% -> 0%
where the time goes in v5:
time: 111 us
  starting transfers between devices  46.3 us (42%)
  waiting for transfers between devices  31.8 us (29%)
  blocking collectives  17.5 us (16%)
  local copies, waits for them, and re-layouts  5.81 us (5%)
  other arithmetic  4.85 us (4%)
  matrix products  3.4 us (3%)
    all_to_all x1, blocking collectives, body(): lax.all_to_all(partial.reshape(4 * groups, -1, LANES), QUAD + ('ch',), 0, 0)  17.5 us
    ppermute x3, starting transfers between devices, reduced(): lax.ppermute(sent, axis, [(i, (i + d) % count) for i in range(count)])  13.7 us
    ppermute x2, starting transfers between devices, region(): lax.ppermute(sent, LAT + LON, edge_pairs(8, lon, f))  12.3 us
    ppermute x2, waiting for transfers between devices, from_quad(): other = lax.ppermute(blocks, axis, SWAP)  8.35 us
    all_to_all x2, starting transfers between devices, body(): mine = lax.all_to_all(block, 'z', 0, 0)  8.13 us
    ppermute x3, waiting for transfers between devices, reduced(): lax.ppermute(sent, axis, [(i, (i + d) % count) for i in range(count)])  7.72 us
    ppermute x1, waiting for transfers between devices, region(): other = lax.ppermute(both, 'xl', SWAP)  5.69 us
    ppermute x1, waiting for transfers between devices, lon_halo(): after = lax.ppermute(block[:, :width], LON, down)  4.1 us
  transfers between devices with their start and end apart: 15, of which 9 were waited for; matrix products, arithmetic and copies ran while one was open for 3% of the time, Pallas kernels for 0%

profile of v5, /device:TPU:14, one launch (start us, length us, event | category | flops | bytes accessed | tf_op | source)
XLA Modules:
  0.0 110.5 jit_solution(3530511628403060163)
XLA Ops:
  0.0 1.0 fusion.27
  1.0 0.3 convolution_convert_fusion
  1.4 0.9 broadcast_in_dim.26
  2.3 11.0 %collective-permute-start.1 = (bf16[2,24,256]{2,1,0:T(8,128)(2,1)S(1)}, bf16[2,24,256]{2,1,0:T(8,128)(2,1)S(1)}, u32[]{:S(2)}, u32[]{:S(2)}) collective-permute-start(bf16[2,24,256]{2,1,0:T(8,128)(2,1)S(1)} %slice_select_fusion), channel_id=1, source_target_pairs={{0,32},{4,36},{8,40},{12,44},{16,48},{20,52},{24,56},{28,60},{32,0... | collective-permute-start | bytes 73736 | tf_op jit(solution)/shard_map/ppermute | solution.py:75
  13.3 1.3 %collective-permute-start.2 = (bf16[2,24,256]{2,1,0:T(8,128)(2,1)S(1)}, bf16[2,24,256]{2,1,0:T(8,128)(2,1)S(1)}, u32[]{:S(2)}, u32[]{:S(2)}) collective-permute-start(bf16[2,24,256]{2,1,0:T(8,128)(2,1)S(1)} %slice_select_fusion), channel_id=1, source_target_pairs={{0,96},{4,100},{8,104},{12,108},{16,112},{20,116},{24,120},{28,124... | collective-permute-start | bytes 73736 | tf_op jit(solution)/shard_map/ppermute | solution.py:75
  14.6 1.9 %collective-permute-start = (bf16[7,24,256]{2,1,0:T(8,128)(2,1)S(1)}, bf16[7,24,256]{2,1,0:T(8,128)(2,1)S(1)}, u32[]{:S(2)}, u32[]{:S(2)}) collective-permute-start(bf16[7,24,256]{2,1,0:T(8,128)(2,1)S(1)} %fusion.27), channel_id=1, source_target_pairs={{0,64},{64,0},{1,65},{65,1},{2,66},{66,2},{3,67},{67,3},{4,68},{68... | collective-permute-start | bytes 258056 | tf_op jit(solution)/shard_map/ppermute | solution.py:78
  16.6 4.6 %all-to-all-start = ((bf16[8,9,16,256]{3,2,1,0:T(8,128)(2,1)}), bf16[8,9,16,256]{3,2,1,0:T(8,128)(2,1)S(1)}, u32[]{:S(2)}, u32[]{:S(2)}) async-start(bf16[8,9,16,256]{3,2,1,0:T(8,128)(2,1)} %broadcast_in_dim.26), calls=%async_computation | async-start | bytes 1179648 | tf_op jit(solution)/shard_map/all_to_all | solution.py:140
  21.3 1.9 %collective-permute-start.3 = (bf16[16,24,256]{2,1,0:T(8,128)(2,1)S(1)}, bf16[16,24,256]{2,1,0:T(8,128)(2,1)S(1)}, u32[]{:S(2)}, u32[]{:S(2)}) collective-permute-start(bf16[16,24,256]{2,1,0:T(8,128)(2,1)S(1)} %pad_maximum_fusion.7), channel_id=1, source_target_pairs={{0,128},{128,0},{1,129},{129,1},{2,130},{130,2},{3,131},{131,3},{4... | collective-permute-start | bytes 589832 | tf_op jit(solution)/shard_map/ppermute | solution.py:82
  23.2 0.3 convolution_convert_fusion.1
  23.6 5.7 %collective-permute-done.3 = bf16[16,24,256]{2,1,0:T(8,128)(2,1)S(1)} collective-permute-done((bf16[16,24,256]{2,1,0:T(8,128)(2,1)S(1)}, bf16[16,24,256]{2,1,0:T(8,128)(2,1)S(1)}, u32[]{:S(2)}, u32[]{:S(2)}) %collective-permute-start.3) | collective-permute-done | bytes 196640 | tf_op jit(solution)/shard_map/ppermute | solution.py:82
  29.4 0.9 broadcast_in_dim.24
  30.3 0.6 collective-permute-start.5
  31.0 4.1 %collective-permute-done.5 = bf16[32,2,256]{2,1,0:T(2,128)(2,1)S(1)} collective-permute-done((bf16[32,2,256]{2,1,0:T(2,128)(2,1)S(1)}, bf16[32,2,256]{2,1,0:T(2,128)(2,1)S(1)}, u32[]{:S(2)}, u32[]{:S(2)}) %collective-permute-start.5) | collective-permute-done | bytes 32800 | tf_op jit(solution)/shard_map/ppermute | solution.py:56
  35.1 0.6 collective-permute-done.4
  35.6 0.3 pad_maximum_fusion.1
  35.9 4.0 %all-to-all-done = bf16[8,9,16,256]{3,2,1,0:T(8,128)(2,1)S(1)} async-done(((bf16[8,9,16,256]{3,2,1,0:T(8,128)(2,1)}), bf16[8,9,16,256]{3,2,1,0:T(8,128)(2,1)S(1)}, u32[]{:S(2)}, u32[]{:S(2)}) %all-to-all-start) | async-done | bytes 589856 | tf_op jit(solution)/shard_map/all_to_all | solution.py:140
  39.9 1.9 %collective-permute-start.6 = (bf16[8,9,16,256]{3,2,1,0:T(8,128)(2,1)S(1)}, bf16[8,9,16,256]{3,2,1,0:T(8,128)(2,1)S(1)}, u32[]{:S(2)}, u32[]{:S(2)}) collective-permute-start(bf16[8,9,16,256]{3,2,1,0:T(8,128)(2,1)S(1)} %all-to-all-done), channel_id=1, source_target_pairs={{0,4},{4,0},{1,5},{5,1},{2,6},{6,2},{3,7},{7,3},{8,12},{12,8},{9,1... | collective-permute-start | bytes 1769480 | tf_op jit(solution)/shard_map/ppermute | solution.py:144
  42.1 0.1 reshape.130
  42.5 1.4 %collective-permute-done.6 = bf16[8,9,16,256]{3,2,1,0:T(8,128)(2,1)S(1)} collective-permute-done((bf16[8,9,16,256]{3,2,1,0:T(8,128)(2,1)S(1)}, bf16[8,9,16,256]{3,2,1,0:T(8,128)(2,1)S(1)}, u32[]{:S(2)}, u32[]{:S(2)}) %collective-permute-start.6) | collective-permute-done | bytes 589856 | tf_op jit(solution)/shard_map/ppermute | solution.py:144
  44.0 0.2 copy.23
  44.2 0.5 copy-done.6
  44.7 1.5 %fusion.2 = bf16[34,8,4,256]{3,1,2,0:T(8,128)(2,1)S(1)} fusion(bf16[3,3,256,256]{3,2,1,0:T(8,128)(2,1)S(1)} %bitcast.116, bf16[36,1,7,2,256]{4,2,3,0,1:T(8,128)(2,1)S(1)} %slice.202, bf16[36,1,8,4,256]{4,2,3,0,1:T(8,128)(2,1)S(1)} %copy.22, pred[8,4]{0,1:T(4,128)(4,1)S(1)} %copy-done.6), kind=kOutput, calls=%fused_computation.5 | convolution fusion | flops 1286668288 | bytes 2584608 | tf_op jit(solution)/shard_map/conv_general_dilated | solution.py:99
  46.3 0.2 copy.25
  46.8 0.1 reshape.123
  46.9 0.1 fusion.44
  47.0 0.1 pad_slice_fusion.13
  47.7 3.5 %all-to-all-start.1 = ((bf16[8,9,16,256]{3,2,1,0:T(8,128)(2,1)}), bf16[8,9,16,256]{3,2,1,0:T(8,128)(2,1)S(1)}, u32[]{:S(2)}, u32[]{:S(2)}) async-start(bf16[8,9,16,256]{3,2,1,0:T(8,128)(2,1)} %broadcast_in_dim.24), calls=%async_computation.1 | async-start | bytes 1179648 | tf_op jit(solution)/shard_map/all_to_all | solution.py:152
  51.4 5.4 %collective-permute-start.9 = (bf16[392,128]{1,0:T(8,128)(2,1)S(1)}, bf16[392,128]{1,0:T(8,128)(2,1)S(1)}, u32[]{:S(2)}, u32[]{:S(2)}) collective-permute-start(bf16[392,128]{1,0:T(8,128)(2,1)S(1)} %get-tuple-element.36), channel_id=1, source_target_pairs={{0,3},{1,0},{2,1},{3,2},{4,7},{5,4},{6,5},{7,6},{8,11},{9,8},{10,9... | collective-permute-start | bytes 301064 | tf_op jit(solution)/shard_map/ppermute | solution.py:37
  56.8 4.6 %collective-permute-start.8 = (bf16[392,128]{1,0:T(8,128)(2,1)S(1)}, bf16[392,128]{1,0:T(8,128)(2,1)S(1)}, u32[]{:S(2)}, u32[]{:S(2)}) collective-permute-start(bf16[392,128]{1,0:T(8,128)(2,1)S(1)} %get-tuple-element.37), channel_id=1, source_target_pairs={{0,2},{1,3},{2,0},{3,1},{4,6},{5,7},{6,4},{7,5},{8,10},{9,11},{10,... | collective-permute-start | bytes 301064 | tf_op jit(solution)/shard_map/ppermute | solution.py:37
  61.4 3.7 %collective-permute-start.7 = (bf16[392,128]{1,0:T(8,128)(2,1)S(1)}, bf16[392,128]{1,0:T(8,128)(2,1)S(1)}, u32[]{:S(2)}, u32[]{:S(2)}) collective-permute-start(bf16[392,128]{1,0:T(8,128)(2,1)S(1)} %get-tuple-element.35), channel_id=1, source_target_pairs={{0,1},{1,2},{2,3},{3,0},{4,5},{5,6},{6,7},{7,4},{8,9},{9,10},{10,1... | collective-permute-start | bytes 301064 | tf_op jit(solution)/shard_map/ppermute | solution.py:37
  65.2 4.2 %collective-permute-done.8 = bf16[392,128]{1,0:T(8,128)(2,1)S(1)} collective-permute-done((bf16[392,128]{1,0:T(8,128)(2,1)S(1)}, bf16[392,128]{1,0:T(8,128)(2,1)S(1)}, u32[]{:S(2)}, u32[]{:S(2)}) %collective-permute-start.8) | collective-permute-done | bytes 100384 | tf_op jit(solution)/shard_map/ppermute | solution.py:37
  69.3 3.6 %collective-permute-done.7 = bf16[392,128]{1,0:T(8,128)(2,1)S(1)} collective-permute-done((bf16[392,128]{1,0:T(8,128)(2,1)S(1)}, bf16[392,128]{1,0:T(8,128)(2,1)S(1)}, u32[]{:S(2)}, u32[]{:S(2)}) %collective-permute-start.7) | collective-permute-done | bytes 100384 | tf_op jit(solution)/shard_map/ppermute | solution.py:37
  73.1 1.9 %collective-permute-start.10 = (bf16[1,392,128]{2,1,0:T(8,128)(2,1)S(1)}, bf16[1,392,128]{2,1,0:T(8,128)(2,1)S(1)}, u32[]{:S(2)}, u32[]{:S(2)}) collective-permute-start(bf16[1,392,128]{2,1,0:T(8,128)(2,1)S(1)} %fusion.30), channel_id=1, source_target_pairs={{0,64},{64,0},{1,65},{65,1},{2,66},{66,2},{3,67},{67,3},{4,68},{68... | collective-permute-start | bytes 301064 | tf_op jit(solution)/shard_map/ppermute | solution.py:45
  75.0 4.6 %collective-permute-done.10 = bf16[1,392,128]{2,1,0:T(8,128)(2,1)S(1)} collective-permute-done((bf16[1,392,128]{2,1,0:T(8,128)(2,1)S(1)}, bf16[1,392,128]{2,1,0:T(8,128)(2,1)S(1)}, u32[]{:S(2)}, u32[]{:S(2)}) %collective-permute-start.10) | collective-permute-done | bytes 100384 | tf_op jit(solution)/shard_map/ppermute | solution.py:45
  79.7 1.9 %collective-permute-start.11 = (bf16[2,392,128]{2,1,0:T(8,128)(2,1)S(1)}, bf16[2,392,128]{2,1,0:T(8,128)(2,1)S(1)}, u32[]{:S(2)}, u32[]{:S(2)}) collective-permute-start(bf16[2,392,128]{2,1,0:T(8,128)(2,1)S(1)} %pad_maximum_fusion.6), channel_id=1, source_target_pairs={{0,128},{128,0},{1,129},{129,1},{2,130},{130,2},{3,131},{131,3},{4... | collective-permute-start | bytes 602120 | tf_op jit(solution)/shard_map/ppermute | solution.py:45
  81.6 1.9 %collective-permute-start.12 = (bf16[8,9,16,256]{3,2,1,0:T(8,128)(2,1)S(1)}, bf16[8,9,16,256]{3,2,1,0:T(8,128)(2,1)S(1)}, u32[]{:S(2)}, u32[]{:S(2)}) collective-permute-start(bf16[8,9,16,256]{3,2,1,0:T(8,128)(2,1)S(1)} %all-to-all-done.1), channel_id=1, source_target_pairs={{0,4},{4,0},{1,5},{5,1},{2,6},{6,2},{3,7},{7,3},{8,12},{12,8},{9,1... | collective-permute-start | bytes 1769480 | tf_op jit(solution)/shard_map/ppermute | solution.py:156
  83.6 3.7 %collective-permute-done.11 = bf16[2,392,128]{2,1,0:T(8,128)(2,1)S(1)} collective-permute-done((bf16[2,392,128]{2,1,0:T(8,128)(2,1)S(1)}, bf16[2,392,128]{2,1,0:T(8,128)(2,1)S(1)}, u32[]{:S(2)}, u32[]{:S(2)}) %collective-permute-start.11) | collective-permute-done | bytes 200736 | tf_op jit(solution)/shard_map/ppermute | solution.py:45
  87.4 0.2 fusion.10
  88.0 0.3 maximum_bitcast_fusion.3
  88.4 0.1 reshape.141
  88.6 0.2 select_bitcast_fusion.1
  88.9 0.2 copy.29
  89.1 0.5 copy-done.5
  89.6 1.2 %fusion.3 = bf16[28,8,4,256]{3,1,2,0:T(8,128)(2,1)S(1)} fusion(bf16[3,3,256,256]{3,2,1,0:T(8,128)(2,1)S(1)} %bitcast.117, bf16[30,1,7,2,256]{4,2,3,0,1:T(8,128)(2,1)S(1)} %slice.220, bf16[30,1,8,4,256]{4,2,3,0,1:T(8,128)(2,1)S(1)} %copy.28, pred[8,4]{0,1:T(4,128)(4,1)S(1)} %copy-done.5), kind=kOutput, calls=%fused_computation.7 | convolution fusion | flops 1059635200 | bytes 2344992 | tf_op jit(solution)/shard_map/conv_general_dilated | solution.py:99
  90.8 0.2 copy.30
  91.2 0.1 fusion.46
  92.0 17.5 %all_to_all.15 = bf16[16,88,128]{2,1,0:T(8,128)(2,1)S(1)} all-to-all(bf16[16,88,128]{2,1,0:T(8,128)(2,1)S(1)} %bitcast.115), channel_id=1, replica_groups=mesh['xh'=2,'xl'=2,'ylo'=2,'z'=8,'core'=2,'ch'=4] {'xl','ylo','ch'}, dimensions={0} | all-to-all | bytes 720896 | tf_op jit(solution)/shard_map/all_to_all | solution.py:162
  109.7 0.8 fusion.29
  (89 shorter events, 3.7 us)
Async XLA Ops:
  0.0 1.0 copy-start
  2.3 20.9 %copy-start.3 = (bf16[3,3,1,16,1024]{4,3,2,1,0:T(8,128)(2,1)S(1)}, bf16[3,3,1,16,1024]{4,3,2,1,0:T(8,128)(2,1)}, u32[]{:S(2)}) copy-start(bf16[3,3,1,16,1024]{4,3,2,1,0:T(8,128)(2,1)} %param.8) | copy-start | bytes 884740
  2.3 18.9 %collective-permute-start.1 = (bf16[2,24,256]{2,1,0:T(8,128)(2,1)S(1)}, bf16[2,24,256]{2,1,0:T(8,128)(2,1)S(1)}, u32[]{:S(2)}, u32[]{:S(2)}) collective-permute-start(bf16[2,24,256]{2,1,0:T(8,128)(2,1)S(1)} %slice_select_fusion), channel_id=1, source_target_pairs={{0,32},{4,36},{8,40},{12,44},{16,48},{20,52},{24,56},{28,60},{32,0... | collective-permute-start | bytes 73736 | tf_op jit(solution)/shard_map/ppermute | solution.py:75
  13.3 7.8 %collective-permute-start.2 = (bf16[2,24,256]{2,1,0:T(8,128)(2,1)S(1)}, bf16[2,24,256]{2,1,0:T(8,128)(2,1)S(1)}, u32[]{:S(2)}, u32[]{:S(2)}) collective-permute-start(bf16[2,24,256]{2,1,0:T(8,128)(2,1)S(1)} %slice_select_fusion), channel_id=1, source_target_pairs={{0,96},{4,100},{8,104},{12,108},{16,112},{20,116},{24,120},{28,124... | collective-permute-start | bytes 73736 | tf_op jit(solution)/shard_map/ppermute | solution.py:75
  14.6 6.6 %collective-permute-start = (bf16[7,24,256]{2,1,0:T(8,128)(2,1)S(1)}, bf16[7,24,256]{2,1,0:T(8,128)(2,1)S(1)}, u32[]{:S(2)}, u32[]{:S(2)}) collective-permute-start(bf16[7,24,256]{2,1,0:T(8,128)(2,1)S(1)} %fusion.27), channel_id=1, source_target_pairs={{0,64},{64,0},{1,65},{65,1},{2,66},{66,2},{3,67},{67,3},{4,68},{68... | collective-permute-start | bytes 258056 | tf_op jit(solution)/shard_map/ppermute | solution.py:78
  16.6 23.3 %all-to-all-start = ((bf16[8,9,16,256]{3,2,1,0:T(8,128)(2,1)}), bf16[8,9,16,256]{3,2,1,0:T(8,128)(2,1)S(1)}, u32[]{:S(2)}, u32[]{:S(2)}) async-start(bf16[8,9,16,256]{3,2,1,0:T(8,128)(2,1)} %broadcast_in_dim.26), calls=%async_computation | async-start | bytes 1179648 | tf_op jit(solution)/shard_map/all_to_all | solution.py:140
  21.3 8.0 %collective-permute-start.3 = (bf16[16,24,256]{2,1,0:T(8,128)(2,1)S(1)}, bf16[16,24,256]{2,1,0:T(8,128)(2,1)S(1)}, u32[]{:S(2)}, u32[]{:S(2)}) collective-permute-start(bf16[16,24,256]{2,1,0:T(8,128)(2,1)S(1)} %pad_maximum_fusion.7), channel_id=1, source_target_pairs={{0,128},{128,0},{1,129},{129,1},{2,130},{130,2},{3,131},{131,3},{4... | collective-permute-start | bytes 589832 | tf_op jit(solution)/shard_map/ppermute | solution.py:82
  30.3 4.7 %collective-permute-start.5 = (bf16[32,2,256]{2,1,0:T(2,128)(2,1)S(1)}, bf16[32,2,256]{2,1,0:T(2,128)(2,1)S(1)}, u32[]{:S(2)}, u32[]{:S(2)}) collective-permute-start(bf16[32,2,256]{2,1,0:T(2,128)(2,1)S(1)} %get-tuple-element.43), channel_id=1, source_target_pairs={{4,0},{8,4},{12,8},{16,12},{20,16},{24,20},{28,24},{32,28},{36,32}... | collective-permute-start | bytes 98312 | tf_op jit(solution)/shard_map/ppermute | solution.py:56
  31.0 4.7 %collective-permute-start.4 = (bf16[32,2,256]{2,1,0:T(2,128)(2,1)S(1)}, bf16[32,2,256]{2,1,0:T(2,128)(2,1)S(1)}, u32[]{:S(2)}, u32[]{:S(2)}) collective-permute-start(bf16[32,2,256]{2,1,0:T(2,128)(2,1)S(1)} %get-tuple-element.42), channel_id=1, source_target_pairs={{0,4},{4,8},{8,12},{12,16},{16,20},{20,24},{24,28},{28,32},{32,36}... | collective-permute-start | bytes 98312 | tf_op jit(solution)/shard_map/ppermute | solution.py:55
  39.9 3.9 %collective-permute-start.6 = (bf16[8,9,16,256]{3,2,1,0:T(8,128)(2,1)S(1)}, bf16[8,9,16,256]{3,2,1,0:T(8,128)(2,1)S(1)}, u32[]{:S(2)}, u32[]{:S(2)}) collective-permute-start(bf16[8,9,16,256]{3,2,1,0:T(8,128)(2,1)S(1)} %all-to-all-done), channel_id=1, source_target_pairs={{0,4},{4,0},{1,5},{5,1},{2,6},{6,2},{3,7},{7,3},{8,12},{12,8},{9,1... | collective-permute-start | bytes 1769480 | tf_op jit(solution)/shard_map/ppermute | solution.py:144
  44.0 0.7 copy-start.6
  47.5 3.8 %copy-start.4 = (f32[256]{0:T(256)S(1)}, f32[256]{0:T(256)}, u32[]{:S(2)}) copy-start(f32[256]{0:T(256)} %param.7) | copy-start | bytes 3076
  47.7 25.3 %all-to-all-start.1 = ((bf16[8,9,16,256]{3,2,1,0:T(8,128)(2,1)}), bf16[8,9,16,256]{3,2,1,0:T(8,128)(2,1)S(1)}, u32[]{:S(2)}, u32[]{:S(2)}) async-start(bf16[8,9,16,256]{3,2,1,0:T(8,128)(2,1)} %broadcast_in_dim.24), calls=%async_computation.1 | async-start | bytes 1179648 | tf_op jit(solution)/shard_map/all_to_all | solution.py:152
  51.4 13.8 %collective-permute-start.9 = (bf16[392,128]{1,0:T(8,128)(2,1)S(1)}, bf16[392,128]{1,0:T(8,128)(2,1)S(1)}, u32[]{:S(2)}, u32[]{:S(2)}) collective-permute-start(bf16[392,128]{1,0:T(8,128)(2,1)S(1)} %get-tuple-element.36), channel_id=1, source_target_pairs={{0,3},{1,0},{2,1},{3,2},{4,7},{5,4},{6,5},{7,6},{8,11},{9,8},{10,9... | collective-permute-start | bytes 301064 | tf_op jit(solution)/shard_map/ppermute | solution.py:37
  56.8 12.6 %collective-permute-start.8 = (bf16[392,128]{1,0:T(8,128)(2,1)S(1)}, bf16[392,128]{1,0:T(8,128)(2,1)S(1)}, u32[]{:S(2)}, u32[]{:S(2)}) collective-permute-start(bf16[392,128]{1,0:T(8,128)(2,1)S(1)} %get-tuple-element.37), channel_id=1, source_target_pairs={{0,2},{1,3},{2,0},{3,1},{4,6},{5,7},{6,4},{7,5},{8,10},{9,11},{10,... | collective-permute-start | bytes 301064 | tf_op jit(solution)/shard_map/ppermute | solution.py:37
  61.4 11.6 %collective-permute-start.7 = (bf16[392,128]{1,0:T(8,128)(2,1)S(1)}, bf16[392,128]{1,0:T(8,128)(2,1)S(1)}, u32[]{:S(2)}, u32[]{:S(2)}) collective-permute-start(bf16[392,128]{1,0:T(8,128)(2,1)S(1)} %get-tuple-element.35), channel_id=1, source_target_pairs={{0,1},{1,2},{2,3},{3,0},{4,5},{5,6},{6,7},{7,4},{8,9},{9,10},{10,1... | collective-permute-start | bytes 301064 | tf_op jit(solution)/shard_map/ppermute | solution.py:37
  73.1 6.5 %collective-permute-start.10 = (bf16[1,392,128]{2,1,0:T(8,128)(2,1)S(1)}, bf16[1,392,128]{2,1,0:T(8,128)(2,1)S(1)}, u32[]{:S(2)}, u32[]{:S(2)}) collective-permute-start(bf16[1,392,128]{2,1,0:T(8,128)(2,1)S(1)} %fusion.30), channel_id=1, source_target_pairs={{0,64},{64,0},{1,65},{65,1},{2,66},{66,2},{3,67},{67,3},{4,68},{68... | collective-permute-start | bytes 301064 | tf_op jit(solution)/shard_map/ppermute | solution.py:45
  79.7 7.6 %collective-permute-start.11 = (bf16[2,392,128]{2,1,0:T(8,128)(2,1)S(1)}, bf16[2,392,128]{2,1,0:T(8,128)(2,1)S(1)}, u32[]{:S(2)}, u32[]{:S(2)}) collective-permute-start(bf16[2,392,128]{2,1,0:T(8,128)(2,1)S(1)} %pad_maximum_fusion.6), channel_id=1, source_target_pairs={{0,128},{128,0},{1,129},{129,1},{2,130},{130,2},{3,131},{131,3},{4... | collective-permute-start | bytes 602120 | tf_op jit(solution)/shard_map/ppermute | solution.py:45
  81.6 7.0 %collective-permute-start.12 = (bf16[8,9,16,256]{3,2,1,0:T(8,128)(2,1)S(1)}, bf16[8,9,16,256]{3,2,1,0:T(8,128)(2,1)S(1)}, u32[]{:S(2)}, u32[]{:S(2)}) collective-permute-start(bf16[8,9,16,256]{3,2,1,0:T(8,128)(2,1)S(1)} %all-to-all-done.1), channel_id=1, source_target_pairs={{0,4},{4,0},{1,5},{5,1},{2,6},{6,2},{3,7},{7,3},{8,12},{12,8},{9,1... | collective-permute-start | bytes 1769480 | tf_op jit(solution)/shard_map/ppermute | solution.py:156
  88.9 0.7 copy-start.5
  91.9 17.8 %copy-start.1 = (bf16[1,7,24,256]{3,2,1,0:T(8,128)(2,1)S(1)}, bf16[1,7,24,256]{3,2,1,0:T(8,128)(2,1)}, u32[]{:S(2)}) copy-start(bf16[1,7,24,256]{3,2,1,0:T(8,128)(2,1)} %param.5) | copy-start | bytes 258052
  92.0 17.8 %copy-start.2 = (f32[256]{0:T(256)S(1)}, f32[256]{0:T(256)}, u32[]{:S(2)}) copy-start(f32[256]{0:T(256)} %param.9) | copy-start | bytes 3076

commit v6 on v5

--- a/solution.py
+++ b/solution.py
@@ -37,16 +37,6 @@
         came = lax.ppermute(sent, axis, [(i, (i + d) % count) for i in range(count)])
         total = total + came.astype(jnp.float32)
     return total
-
-
-def from_quad(block, member):
-    blocks = block[None]
-    for axis, later in (("ylo", member % 2 == 1), ("xl", member >= 2)):
-        other = lax.ppermute(blocks, axis, SWAP)
-        blocks = jnp.concatenate(
-            [jnp.where(later, other, blocks), jnp.where(later, blocks, other)]
-        )
-    return blocks
 
 
 def lon_halo(block, width, lon):
@@ -134,27 +124,26 @@
     own = features[0]
     height, breadth, width = own.shape
 
-    first = silu(own)
     block = copies_of(quarter(kernel_one, member, groups))
-    block, first = lax.optimization_barrier((block, first))
     mine = lax.all_to_all(block, "z", 0, 0)
-    ext = region(first, member, upper, lon)
-    block, ext = lax.optimization_barrier((copies_of(quarter(kernel_two, member, groups)), ext))
-    ext = lon_halo(ext, 2, lon)
+    ext = region(own, member, upper, lon)
+    rims = with_rims(silu(lon_halo(ext, 2, lon)), upper)
+    block, rims = lax.optimization_barrier((copies_of(quarter(kernel_two, member, groups)), rims))
+    mine_two = lax.all_to_all(block, "z", 0, 0)
     other = lax.ppermute(mine, "core", SWAP)
-    out = conv(with_rims(ext, upper), mine, other, core)
+    out = conv(rims, mine, other, core)
     out = jnp.concatenate([out[:1], out[3:-3], out[-1:]])
     rows, columns = out.shape[0], out.shape[1]
     count = rows * columns
     partial = folded(out.reshape(count, -1), half_of(count))
 
-    block, partial = lax.optimization_barrier((block, partial))
-    mine = lax.all_to_all(block, "z", 0, 0)
+    mine = mine_two
     bias = lax.dynamic_slice_in_dim(bias_one, member * SLICE, SLICE, 0)
     hidden = reduced(partial, "ch") + jnp.concatenate([bias, bias])
-    hidden, mine = lax.optimization_barrier((hidden, mine))
+    acts = jnp.broadcast_to(silu(hidden), (4,) + hidden.shape)
+    acts, mine = lax.optimization_barrier((acts, mine))
     other = lax.ppermute(mine, "core", SWAP)
-    acts = unfolded(from_quad(silu(hidden), member), count)
+    acts = unfolded(lax.all_to_all(acts, QUAD, 0, 0), count)
     acts = jnp.concatenate([acts[k] for k in range(4)], axis=1)
     out = conv(acts.reshape(rows, columns, -1), mine, other, core)
     count = height * breadth

time: 111 us -> 110 us (level)
  the two profiles are of different devices: /device:TPU:14 before, /device:TPU:10 now
where the time goes in v6:
time: 110 us; the launch traced here: 109 us
  starting transfers between devices  50 us (45%)
  waiting for transfers between devices  23.4 us (21%)
  blocking collectives  19.1 us (17%)
  local copies, waits for them, and re-layouts  7.88 us (7%)
  other arithmetic  4.45 us (4%)
  matrix products  3.39 us (3%)
    all_to_all x1, blocking collectives, body(): lax.all_to_all(partial.reshape(4 * groups, -1, LANES), QUAD + ('ch',), 0, 0)  19.1 us
    ppermute x3, starting transfers between devices, reduced(): lax.ppermute(sent, axis, [(i, (i + d) % count) for i in range(count)])  14.5 us
    all_to_all x1, starting transfers between devices, body(): mine = lax.all_to_all(block, 'z', 0, 0)  10.3 us
    all_to_all x1, starting transfers between devices, body(): acts = unfolded(lax.all_to_all(acts, QUAD, 0, 0), count)  5.89 us
    all_to_all x1, waiting for transfers between devices, body(): acts = unfolded(lax.all_to_all(acts, QUAD, 0, 0), count)  5.79 us
    ppermute x3, waiting for transfers between devices, reduced(): lax.ppermute(sent, axis, [(i, (i + d) % count) for i in range(count)])  5.68 us
    all_to_all x1, starting transfers between devices, body(): mine_two = lax.all_to_all(block, 'z', 0, 0)  5.37 us
    ppermute x2, starting transfers between devices, region(): lax.ppermute(sent, LAT + LON, edge_pairs(8, lon, f))  4.56 us
  transfers between devices with their start and end apart: 14, of which 6 were waited for; matrix products, arithmetic and copies ran while one was open for 7% of the time, Pallas kernels for 0%

profile of v6, /device:TPU:10, one launch (start us, length us, event | category | flops | bytes accessed | tf_op | source)
XLA Modules:
  0.0 109.0 jit_solution(4803031195052232013)
XLA Ops:
  0.0 0.8 select_bitcast_fusion.4
  0.8 3.3 %collective-permute-start.1 = (bf16[2,24,256]{2,1,0:T(8,128)(2,1)S(1)}, bf16[2,24,256]{2,1,0:T(8,128)(2,1)S(1)}, u32[]{:S(2)}, u32[]{:S(2)}) collective-permute-start(bf16[2,24,256]{2,1,0:T(8,128)(2,1)S(1)} %select_bitcast_fusion.4), channel_id=1, source_target_pairs={{0,32},{4,36},{8,40},{12,44},{16,48},{20,52},{24,56},{28,60},{32,0... | collective-permute-start | bytes 73736 | tf_op jit(solution)/shard_map/ppermute | solution.py:65
  4.1 1.3 %collective-permute-start.2 = (bf16[2,24,256]{2,1,0:T(8,128)(2,1)S(1)}, bf16[2,24,256]{2,1,0:T(8,128)(2,1)S(1)}, u32[]{:S(2)}, u32[]{:S(2)}) collective-permute-start(bf16[2,24,256]{2,1,0:T(8,128)(2,1)S(1)} %select_bitcast_fusion.4), channel_id=1, source_target_pairs={{0,96},{4,100},{8,104},{12,108},{16,112},{20,116},{24,120},{28,124... | collective-permute-start | bytes 73736 | tf_op jit(solution)/shard_map/ppermute | solution.py:65
  5.4 0.3 convolution_convert_fusion
  5.8 0.9 broadcast_in_dim.27
  6.7 10.3 %all-to-all-start = ((bf16[8,9,16,256]{3,2,1,0:T(8,128)(2,1)}), bf16[8,9,16,256]{3,2,1,0:T(8,128)(2,1)S(1)}, u32[]{:S(2)}, u32[]{:S(2)}) async-start(bf16[8,9,16,256]{3,2,1,0:T(8,128)(2,1)} %broadcast_in_dim.27), calls=%async_computation | async-start | bytes 1179648 | tf_op jit(solution)/shard_map/all_to_all | solution.py:128
  17.0 1.9 %collective-permute-start = (bf16[7,24,256]{2,1,0:T(8,128)(2,1)S(1)}, bf16[7,24,256]{2,1,0:T(8,128)(2,1)S(1)}, u32[]{:S(2)}, u32[]{:S(2)}) collective-permute-start(bf16[7,24,256]{2,1,0:T(8,128)(2,1)S(1)} %bitcast.105), channel_id=1, source_target_pairs={{0,64},{64,0},{1,65},{65,1},{2,66},{66,2},{3,67},{67,3},{4,68},{68... | collective-permute-start | bytes 258056 | tf_op jit(solution)/shard_map/ppermute | solution.py:68
  19.0 4.3 %collective-permute-done = bf16[7,24,256]{2,1,0:T(8,128)(2,1)S(1)} collective-permute-done((bf16[7,24,256]{2,1,0:T(8,128)(2,1)S(1)}, bf16[7,24,256]{2,1,0:T(8,128)(2,1)S(1)}, u32[]{:S(2)}, u32[]{:S(2)}) %collective-permute-start) | collective-permute-done | bytes 86048 | tf_op jit(solution)/shard_map/ppermute | solution.py:68
  23.4 3.1 %collective-permute-start.3 = (bf16[16,24,256]{2,1,0:T(8,128)(2,1)S(1)}, bf16[16,24,256]{2,1,0:T(8,128)(2,1)S(1)}, u32[]{:S(2)}, u32[]{:S(2)}) collective-permute-start(bf16[16,24,256]{2,1,0:T(8,128)(2,1)S(1)} %pad_maximum_fusion.5), channel_id=1, source_target_pairs={{0,128},{128,0},{1,129},{129,1},{2,130},{130,2},{3,131},{131,3},{4... | collective-permute-start | bytes 589832 | tf_op jit(solution)/shard_map/ppermute | solution.py:72
  26.6 4.4 %collective-permute-done.3 = bf16[16,24,256]{2,1,0:T(8,128)(2,1)S(1)} collective-permute-done((bf16[16,24,256]{2,1,0:T(8,128)(2,1)S(1)}, bf16[16,24,256]{2,1,0:T(8,128)(2,1)S(1)}, u32[]{:S(2)}, u32[]{:S(2)}) %collective-permute-start.3) | collective-permute-done | bytes 196640 | tf_op jit(solution)/shard_map/ppermute | solution.py:72
  31.1 0.1 collective-permute-start.5
  31.3 0.4 collective-permute-start.4
  31.7 0.3 convolution_convert_fusion.1
  32.0 0.3 copy-done.5
  32.4 3.2 %all-to-all-done = bf16[8,9,16,256]{3,2,1,0:T(8,128)(2,1)S(1)} async-done(((bf16[8,9,16,256]{3,2,1,0:T(8,128)(2,1)}), bf16[8,9,16,256]{3,2,1,0:T(8,128)(2,1)S(1)}, u32[]{:S(2)}, u32[]{:S(2)}) %all-to-all-start) | async-done | bytes 589856 | tf_op jit(solution)/shard_map/all_to_all | solution.py:128
  35.6 1.9 %collective-permute-start.6 = (bf16[8,9,16,256]{3,2,1,0:T(8,128)(2,1)S(1)}, bf16[8,9,16,256]{3,2,1,0:T(8,128)(2,1)S(1)}, u32[]{:S(2)}, u32[]{:S(2)}) collective-permute-start(bf16[8,9,16,256]{3,2,1,0:T(8,128)(2,1)S(1)} %all-to-all-done), channel_id=1, source_target_pairs={{0,4},{4,0},{1,5},{5,1},{2,6},{6,2},{3,7},{7,3},{8,12},{12,8},{9,1... | collective-permute-start | bytes 1769480 | tf_op jit(solution)/shard_map/ppermute | solution.py:133
  37.5 0.4 fusion.7
  38.2 0.9 broadcast_in_dim.24
  39.1 0.1 reshape.132
  39.4 0.8 slice.206
  40.2 5.4 %all-to-all-start.1 = ((bf16[8,9,16,256]{3,2,1,0:T(8,128)(2,1)}), bf16[8,9,16,256]{3,2,1,0:T(8,128)(2,1)S(1)}, u32[]{:S(2)}, u32[]{:S(2)}) async-start(bf16[8,9,16,256]{3,2,1,0:T(8,128)(2,1)} %broadcast_in_dim.24), calls=%async_computation.1 | async-start | bytes 1179648 | tf_op jit(solution)/shard_map/all_to_all | solution.py:132
  45.8 0.2 copy.23
  45.9 0.8 copy-done.2
  46.7 1.5 %fusion.2 = bf16[34,8,4,256]{3,1,2,0:T(8,128)(2,1)S(1)} fusion(bf16[3,3,256,256]{3,2,1,0:T(8,128)(2,1)S(1)} %bitcast.104, bf16[36,1,7,2,256]{4,2,3,0,1:T(8,128)(2,1)S(1)} %copy-done.2, bf16[36,1,8,4,256]{4,2,3,0,1:T(8,128)(2,1)S(1)} %copy.22, pred[8,4]{0,1:T(4,128)(4,1)S(1)} %copy-done.7), kind=kOutput, calls=%fused_computation.5 | convolution fusion | flops 1286668288 | bytes 2584608 | tf_op jit(solution)/shard_map/conv_general_dilated | solution.py:89
  48.3 0.2 copy.25
  48.8 0.1 reshape.125
  48.9 0.1 fusion.44
  49.1 0.1 pad_slice_fusion.19
  49.7 6.2 %collective-permute-start.9 = (bf16[392,128]{1,0:T(8,128)(2,1)S(1)}, bf16[392,128]{1,0:T(8,128)(2,1)S(1)}, u32[]{:S(2)}, u32[]{:S(2)}) collective-permute-start(bf16[392,128]{1,0:T(8,128)(2,1)S(1)} %get-tuple-element.26), channel_id=1, source_target_pairs={{0,3},{1,0},{2,1},{3,2},{4,7},{5,4},{6,5},{7,6},{8,11},{9,8},{10,9... | collective-permute-start | bytes 301064 | tf_op jit(solution)/shard_map/ppermute | solution.py:37
  55.9 3.8 %collective-permute-start.8 = (bf16[392,128]{1,0:T(8,128)(2,1)S(1)}, bf16[392,128]{1,0:T(8,128)(2,1)S(1)}, u32[]{:S(2)}, u32[]{:S(2)}) collective-permute-start(bf16[392,128]{1,0:T(8,128)(2,1)S(1)} %get-tuple-element.27), channel_id=1, source_target_pairs={{0,2},{1,3},{2,0},{3,1},{4,6},{5,7},{6,4},{7,5},{8,10},{9,11},{10,... | collective-permute-start | bytes 301064 | tf_op jit(solution)/shard_map/ppermute | solution.py:37
  59.7 4.5 %collective-permute-start.7 = (bf16[392,128]{1,0:T(8,128)(2,1)S(1)}, bf16[392,128]{1,0:T(8,128)(2,1)S(1)}, u32[]{:S(2)}, u32[]{:S(2)}) collective-permute-start(bf16[392,128]{1,0:T(8,128)(2,1)S(1)} %get-tuple-element.25), channel_id=1, source_target_pairs={{0,1},{1,2},{2,3},{3,0},{4,5},{5,6},{6,7},{7,4},{8,9},{9,10},{10,1... | collective-permute-start | bytes 301064 | tf_op jit(solution)/shard_map/ppermute | solution.py:37
  64.3 3.2 %collective-permute-done.8 = bf16[392,128]{1,0:T(8,128)(2,1)S(1)} collective-permute-done((bf16[392,128]{1,0:T(8,128)(2,1)S(1)}, bf16[392,128]{1,0:T(8,128)(2,1)S(1)}, u32[]{:S(2)}, u32[]{:S(2)}) %collective-permute-start.8) | collective-permute-done | bytes 100384 | tf_op jit(solution)/shard_map/ppermute | solution.py:37
  67.5 2.5 %collective-permute-done.7 = bf16[392,128]{1,0:T(8,128)(2,1)S(1)} collective-permute-done((bf16[392,128]{1,0:T(8,128)(2,1)S(1)}, bf16[392,128]{1,0:T(8,128)(2,1)S(1)}, u32[]{:S(2)}, u32[]{:S(2)}) %collective-permute-start.7) | collective-permute-done | bytes 100384 | tf_op jit(solution)/shard_map/ppermute | solution.py:37
  70.1 0.8 broadcast_in_dim.28
  70.9 1.9 %collective-permute-start.10 = (bf16[8,9,16,256]{3,2,1,0:T(8,128)(2,1)S(1)}, bf16[8,9,16,256]{3,2,1,0:T(8,128)(2,1)S(1)}, u32[]{:S(2)}, u32[]{:S(2)}) collective-permute-start(bf16[8,9,16,256]{3,2,1,0:T(8,128)(2,1)S(1)} %all-to-all-done.1), channel_id=1, source_target_pairs={{0,4},{4,0},{1,5},{5,1},{2,6},{6,2},{3,7},{7,3},{8,12},{12,8},{9,1... | collective-permute-start | bytes 1769480 | tf_op jit(solution)/shard_map/ppermute | solution.py:145
  72.8 5.9 %all-to-all-start.2 = ((bf16[4,392,128]{2,1,0:T(8,128)(2,1)}), bf16[4,392,128]{2,1,0:T(8,128)(2,1)S(1)}, u32[]{:S(2)}, u32[]{:S(2)}) async-start(bf16[4,392,128]{2,1,0:T(8,128)(2,1)} %broadcast_in_dim.28), calls=%async_computation.2 | async-start | bytes 802816 | tf_op jit(solution)/shard_map/all_to_all | solution.py:146
  78.9 0.1 copy.29
  79.1 5.8 %all-to-all-done.2 = bf16[4,392,128]{2,1,0:T(8,128)(2,1)S(1)} async-done(((bf16[4,392,128]{2,1,0:T(8,128)(2,1)}), bf16[4,392,128]{2,1,0:T(8,128)(2,1)S(1)}, u32[]{:S(2)}, u32[]{:S(2)}) %all-to-all-start.2) | async-done | bytes 401440 | tf_op jit(solution)/shard_map/all_to_all | solution.py:146
  84.8 0.2 slice.219
  85.0 0.2 fusion.23
  85.5 0.3 maximum_bitcast_fusion.2
  85.9 0.1 reshape.143
  86.2 0.4 copy-done.6
  86.5 1.2 %fusion.3 = bf16[28,8,4,256]{3,1,2,0:T(8,128)(2,1)S(1)} fusion(bf16[3,3,256,256]{3,2,1,0:T(8,128)(2,1)S(1)} %bitcast.103, bf16[30,1,7,2,256]{4,2,3,0,1:T(8,128)(2,1)S(1)} %slice.226, bf16[30,1,8,4,256]{4,2,3,0,1:T(8,128)(2,1)S(1)} %copy.28, pred[8,4]{0,1:T(4,128)(4,1)S(1)} %copy-done.6), kind=kOutput, calls=%fused_computation.9 | convolution fusion | flops 1059635200 | bytes 2344992 | tf_op jit(solution)/shard_map/conv_general_dilated | solution.py:89
  87.8 0.2 copy.30
  88.2 0.1 fusion.45
  88.9 19.1 %all_to_all.20 = bf16[16,88,128]{2,1,0:T(8,128)(2,1)S(1)} all-to-all(bf16[16,88,128]{2,1,0:T(8,128)(2,1)S(1)} %bitcast.102), channel_id=1, replica_groups=mesh['xh'=2,'xl'=2,'ylo'=2,'z'=8,'core'=2,'ch'=4] {'xl','ylo','ch'}, dimensions={0} | all-to-all | bytes 720896 | tf_op jit(solution)/shard_map/all_to_all | solution.py:151
  108.2 0.8 fusion.30
  (82 shorter events, 3.4 us)
Async XLA Ops:
  0.0 5.4 %copy-start = (bf16[3,3,1,16,1024]{4,3,2,1,0:T(8,128)(2,1)S(1)}, bf16[3,3,1,16,1024]{4,3,2,1,0:T(8,128)(2,1)}, u32[]{:S(2)}) copy-start(bf16[3,3,1,16,1024]{4,3,2,1,0:T(8,128)(2,1)} %param.6) | copy-start | bytes 884740
  0.8 18.2 %collective-permute-start.1 = (bf16[2,24,256]{2,1,0:T(8,128)(2,1)S(1)}, bf16[2,24,256]{2,1,0:T(8,128)(2,1)S(1)}, u32[]{:S(2)}, u32[]{:S(2)}) collective-permute-start(bf16[2,24,256]{2,1,0:T(8,128)(2,1)S(1)} %select_bitcast_fusion.4), channel_id=1, source_target_pairs={{0,32},{4,36},{8,40},{12,44},{16,48},{20,52},{24,56},{28,60},{32,0... | collective-permute-start | bytes 73736 | tf_op jit(solution)/shard_map/ppermute | solution.py:65
  4.1 14.9 %collective-permute-start.2 = (bf16[2,24,256]{2,1,0:T(8,128)(2,1)S(1)}, bf16[2,24,256]{2,1,0:T(8,128)(2,1)S(1)}, u32[]{:S(2)}, u32[]{:S(2)}) collective-permute-start(bf16[2,24,256]{2,1,0:T(8,128)(2,1)S(1)} %select_bitcast_fusion.4), channel_id=1, source_target_pairs={{0,96},{4,100},{8,104},{12,108},{16,112},{20,116},{24,120},{28,124... | collective-permute-start | bytes 73736 | tf_op jit(solution)/shard_map/ppermute | solution.py:65
  5.8 11.2 %copy-start.1 = (bf16[1,7,24,256]{3,2,1,0:T(8,128)(2,1)S(1)}, bf16[1,7,24,256]{3,2,1,0:T(8,128)(2,1)}, u32[]{:S(2)}) copy-start(bf16[1,7,24,256]{3,2,1,0:T(8,128)(2,1)} %param.5) | copy-start | bytes 258052
  6.7 28.9 %all-to-all-start = ((bf16[8,9,16,256]{3,2,1,0:T(8,128)(2,1)}), bf16[8,9,16,256]{3,2,1,0:T(8,128)(2,1)S(1)}, u32[]{:S(2)}, u32[]{:S(2)}) async-start(bf16[8,9,16,256]{3,2,1,0:T(8,128)(2,1)} %broadcast_in_dim.27), calls=%async_computation | async-start | bytes 1179648 | tf_op jit(solution)/shard_map/all_to_all | solution.py:128
  17.0 6.4 %collective-permute-start = (bf16[7,24,256]{2,1,0:T(8,128)(2,1)S(1)}, bf16[7,24,256]{2,1,0:T(8,128)(2,1)S(1)}, u32[]{:S(2)}, u32[]{:S(2)}) collective-permute-start(bf16[7,24,256]{2,1,0:T(8,128)(2,1)S(1)} %bitcast.105), channel_id=1, source_target_pairs={{0,64},{64,0},{1,65},{65,1},{2,66},{66,2},{3,67},{67,3},{4,68},{68... | collective-permute-start | bytes 258056 | tf_op jit(solution)/shard_map/ppermute | solution.py:68
  19.0 12.7 %copy-start.4 = (bf16[3,3,1,16,1024]{4,3,2,1,0:T(8,128)(2,1)S(1)}, bf16[3,3,1,16,1024]{4,3,2,1,0:T(8,128)(2,1)}, u32[]{:S(2)}) copy-start(bf16[3,3,1,16,1024]{4,3,2,1,0:T(8,128)(2,1)} %param.8) | copy-start | bytes 884740
  23.4 7.6 %collective-permute-start.3 = (bf16[16,24,256]{2,1,0:T(8,128)(2,1)S(1)}, bf16[16,24,256]{2,1,0:T(8,128)(2,1)S(1)}, u32[]{:S(2)}, u32[]{:S(2)}) collective-permute-start(bf16[16,24,256]{2,1,0:T(8,128)(2,1)S(1)} %pad_maximum_fusion.5), channel_id=1, source_target_pairs={{0,128},{128,0},{1,129},{129,1},{2,130},{130,2},{3,131},{131,3},{4... | collective-permute-start | bytes 589832 | tf_op jit(solution)/shard_map/ppermute | solution.py:72
  31.1 6.4 %collective-permute-start.5 = (bf16[32,2,256]{2,1,0:T(2,128)(2,1)S(1)}, bf16[32,2,256]{2,1,0:T(2,128)(2,1)S(1)}, u32[]{:S(2)}, u32[]{:S(2)}) collective-permute-start(bf16[32,2,256]{2,1,0:T(2,128)(2,1)S(1)} %get-tuple-element.33), channel_id=1, source_target_pairs={{4,0},{8,4},{12,8},{16,12},{20,16},{24,20},{28,24},{32,28},{36,32}... | collective-permute-start | bytes 98312 | tf_op jit(solution)/shard_map/ppermute | solution.py:46
  31.3 6.3 %collective-permute-start.4 = (bf16[32,2,256]{2,1,0:T(2,128)(2,1)S(1)}, bf16[32,2,256]{2,1,0:T(2,128)(2,1)S(1)}, u32[]{:S(2)}, u32[]{:S(2)}) collective-permute-start(bf16[32,2,256]{2,1,0:T(2,128)(2,1)S(1)} %get-tuple-element.32), channel_id=1, source_target_pairs={{0,4},{4,8},{8,12},{12,16},{16,20},{20,24},{24,28},{28,32},{32,36}... | collective-permute-start | bytes 98312 | tf_op jit(solution)/shard_map/ppermute | solution.py:45
  31.7 0.7 copy-start.5
  35.6 9.9 %collective-permute-start.6 = (bf16[8,9,16,256]{3,2,1,0:T(8,128)(2,1)S(1)}, bf16[8,9,16,256]{3,2,1,0:T(8,128)(2,1)S(1)}, u32[]{:S(2)}, u32[]{:S(2)}) collective-permute-start(bf16[8,9,16,256]{3,2,1,0:T(8,128)(2,1)S(1)} %all-to-all-done), channel_id=1, source_target_pairs={{0,4},{4,0},{1,5},{5,1},{2,6},{6,2},{3,7},{7,3},{8,12},{12,8},{9,1... | collective-permute-start | bytes 1769480 | tf_op jit(solution)/shard_map/ppermute | solution.py:133
  40.2 29.9 %all-to-all-start.1 = ((bf16[8,9,16,256]{3,2,1,0:T(8,128)(2,1)}), bf16[8,9,16,256]{3,2,1,0:T(8,128)(2,1)S(1)}, u32[]{:S(2)}, u32[]{:S(2)}) async-start(bf16[8,9,16,256]{3,2,1,0:T(8,128)(2,1)} %broadcast_in_dim.24), calls=%async_computation.1 | async-start | bytes 1179648 | tf_op jit(solution)/shard_map/all_to_all | solution.py:132
  45.7 1.0 copy-start.2
  45.8 1.0 copy-start.7
  49.7 14.6 %collective-permute-start.9 = (bf16[392,128]{1,0:T(8,128)(2,1)S(1)}, bf16[392,128]{1,0:T(8,128)(2,1)S(1)}, u32[]{:S(2)}, u32[]{:S(2)}) collective-permute-start(bf16[392,128]{1,0:T(8,128)(2,1)S(1)} %get-tuple-element.26), channel_id=1, source_target_pairs={{0,3},{1,0},{2,1},{3,2},{4,7},{5,4},{6,5},{7,6},{8,11},{9,8},{10,9... | collective-permute-start | bytes 301064 | tf_op jit(solution)/shard_map/ppermute | solution.py:37
  55.9 11.6 %collective-permute-start.8 = (bf16[392,128]{1,0:T(8,128)(2,1)S(1)}, bf16[392,128]{1,0:T(8,128)(2,1)S(1)}, u32[]{:S(2)}, u32[]{:S(2)}) collective-permute-start(bf16[392,128]{1,0:T(8,128)(2,1)S(1)} %get-tuple-element.27), channel_id=1, source_target_pairs={{0,2},{1,3},{2,0},{3,1},{4,6},{5,7},{6,4},{7,5},{8,10},{9,11},{10,... | collective-permute-start | bytes 301064 | tf_op jit(solution)/shard_map/ppermute | solution.py:37
  59.7 10.3 %collective-permute-start.7 = (bf16[392,128]{1,0:T(8,128)(2,1)S(1)}, bf16[392,128]{1,0:T(8,128)(2,1)S(1)}, u32[]{:S(2)}, u32[]{:S(2)}) collective-permute-start(bf16[392,128]{1,0:T(8,128)(2,1)S(1)} %get-tuple-element.25), channel_id=1, source_target_pairs={{0,1},{1,2},{2,3},{3,0},{4,5},{5,6},{6,7},{7,4},{8,9},{9,10},{10,1... | collective-permute-start | bytes 301064 | tf_op jit(solution)/shard_map/ppermute | solution.py:37
  70.9 7.8 %collective-permute-start.10 = (bf16[8,9,16,256]{3,2,1,0:T(8,128)(2,1)S(1)}, bf16[8,9,16,256]{3,2,1,0:T(8,128)(2,1)S(1)}, u32[]{:S(2)}, u32[]{:S(2)}) collective-permute-start(bf16[8,9,16,256]{3,2,1,0:T(8,128)(2,1)S(1)} %all-to-all-done.1), channel_id=1, source_target_pairs={{0,4},{4,0},{1,5},{5,1},{2,6},{6,2},{3,7},{7,3},{8,12},{12,8},{9,1... | collective-permute-start | bytes 1769480 | tf_op jit(solution)/shard_map/ppermute | solution.py:145
  72.8 12.0 %all-to-all-start.2 = ((bf16[4,392,128]{2,1,0:T(8,128)(2,1)}), bf16[4,392,128]{2,1,0:T(8,128)(2,1)S(1)}, u32[]{:S(2)}, u32[]{:S(2)}) async-start(bf16[4,392,128]{2,1,0:T(8,128)(2,1)} %broadcast_in_dim.28), calls=%async_computation.2 | async-start | bytes 802816 | tf_op jit(solution)/shard_map/all_to_all | solution.py:146
  85.9 0.7 copy-start.6
  88.9 19.3 %copy-start.3 = (f32[256]{0:T(256)S(1)}, f32[256]{0:T(256)}, u32[]{:S(2)}) copy-start(f32[256]{0:T(256)} %param.9) | copy-start | bytes 3076

commit v7 on v5

--- a/solution.py
+++ b/solution.py
@@ -29,14 +29,13 @@
     return jnp.broadcast_to(block[None], (lax.axis_size("z"),) + block.shape)
 
 
-def reduced(blocks, axis):
+def traded(blocks, axis):
     me, count = lax.axis_index(axis), blocks.shape[0]
-    total = lax.dynamic_index_in_dim(blocks, me, 0, keepdims=False).astype(jnp.float32)
+    came = [lax.dynamic_index_in_dim(blocks, me, 0, keepdims=False)]
     for d in range(1, count):
         sent = lax.dynamic_index_in_dim(blocks, lax.rem(me + d, count), 0, keepdims=False)
-        came = lax.ppermute(sent, axis, [(i, (i + d) % count) for i in range(count)])
-        total = total + came.astype(jnp.float32)
-    return total
+        came.append(lax.ppermute(sent, axis, [(i, (i + d) % count) for i in range(count)]))
+    return came
 
 
 def from_quad(block, member):
@@ -134,13 +133,10 @@
     own = features[0]
     height, breadth, width = own.shape
 
-    first = silu(own)
     block = copies_of(quarter(kernel_one, member, groups))
-    block, first = lax.optimization_barrier((block, first))
     mine = lax.all_to_all(block, "z", 0, 0)
-    ext = region(first, member, upper, lon)
-    block, ext = lax.optimization_barrier((copies_of(quarter(kernel_two, member, groups)), ext))
-    ext = lon_halo(ext, 2, lon)
+    ext = region(own, member, upper, lon)
+    ext = silu(lon_halo(ext, 2, lon))
     other = lax.ppermute(mine, "core", SWAP)
     out = conv(with_rims(ext, upper), mine, other, core)
     out = jnp.concatenate([out[:1], out[3:-3], out[-1:]])
@@ -148,13 +144,15 @@
     count = rows * columns
     partial = folded(out.reshape(count, -1), half_of(count))
 
-    block, partial = lax.optimization_barrier((block, partial))
+    came = traded(partial, "ch")
+    block = copies_of(quarter(kernel_two, member, groups))
+    block, came[3] = lax.optimization_barrier((block, came[3]))
     mine = lax.all_to_all(block, "z", 0, 0)
     bias = lax.dynamic_slice_in_dim(bias_one, member * SLICE, SLICE, 0)
-    hidden = reduced(partial, "ch") + jnp.concatenate([bias, bias])
-    hidden, mine = lax.optimization_barrier((hidden, mine))
+    hidden = sum(part.astype(jnp.float32) for part in came) + jnp.concatenate([bias, bias])
+    acts, mine = lax.optimization_barrier((from_quad(silu(hidden), member), mine))
     other = lax.ppermute(mine, "core", SWAP)
-    acts = unfolded(from_quad(silu(hidden), member), count)
+    acts = unfolded(acts, count)
     acts = jnp.concatenate([acts[k] for k in range(4)], axis=1)
     out = conv(acts.reshape(rows, columns, -1), mine, other, core)
     count = height * breadth

time: 111 us -> 109 us (0.982)
  the two profiles are of different devices: /device:TPU:14 before, /device:TPU:10 now
where the time goes in v7:
time: 109 us
  starting transfers between devices  49.2 us (45%)
  waiting for transfers between devices  25.2 us (23%)
  blocking collectives  19.4 us (18%)
  local copies, waits for them, and re-layouts  6.15 us (6%)
  other arithmetic  4.58 us (4%)
  matrix products  3.4 us (3%)
    all_to_all x1, blocking collectives, body(): lax.all_to_all(partial.reshape(4 * groups, -1, LANES), QUAD + ('ch',), 0, 0)  19.4 us
    all_to_all x2, starting transfers between devices, body(): mine = lax.all_to_all(block, 'z', 0, 0)  14.8 us
    ppermute x3, starting transfers between devices, traded(): lax.ppermute(sent, axis, [(i, (i + d) % count) for i in range(count)])  14.5 us
    ppermute x2, waiting for transfers between devices, from_quad(): other = lax.ppermute(blocks, axis, SWAP)  8.36 us
    all_to_all x2, waiting for transfers between devices, body(): mine = lax.all_to_all(block, 'z', 0, 0)  6.44 us
    ppermute x2, starting transfers between devices, from_quad(): other = lax.ppermute(blocks, axis, SWAP)  6.03 us
    ppermute x2, starting transfers between devices, region(): lax.ppermute(sent, LAT + LON, edge_pairs(8, lon, f))  4.56 us
    ppermute x1, waiting for transfers between devices, region(): other = lax.ppermute(both, 'xl', SWAP)  4.41 us
  transfers between devices with their start and end apart: 15, of which 8 were waited for; matrix products, arithmetic and copies ran while one was open for 5% of the time, Pallas kernels for 0%

profile of v7, /device:TPU:10, one launch (start us, length us, event | category | flops | bytes accessed | tf_op | source)
XLA Modules:
  0.0 108.7 jit_solution(4091402479217729858)
XLA Ops:
  0.0 0.8 select_bitcast_fusion.4
  0.8 3.3 %collective-permute-start.1 = (bf16[2,24,256]{2,1,0:T(8,128)(2,1)S(1)}, bf16[2,24,256]{2,1,0:T(8,128)(2,1)S(1)}, u32[]{:S(2)}, u32[]{:S(2)}) collective-permute-start(bf16[2,24,256]{2,1,0:T(8,128)(2,1)S(1)} %select_bitcast_fusion.4), channel_id=1, source_target_pairs={{0,32},{4,36},{8,40},{12,44},{16,48},{20,52},{24,56},{28,60},{32,0... | collective-permute-start | bytes 73736 | tf_op jit(solution)/shard_map/ppermute | solution.py:74
  4.1 1.3 %collective-permute-start.2 = (bf16[2,24,256]{2,1,0:T(8,128)(2,1)S(1)}, bf16[2,24,256]{2,1,0:T(8,128)(2,1)S(1)}, u32[]{:S(2)}, u32[]{:S(2)}) collective-permute-start(bf16[2,24,256]{2,1,0:T(8,128)(2,1)S(1)} %select_bitcast_fusion.4), channel_id=1, source_target_pairs={{0,96},{4,100},{8,104},{12,108},{16,112},{20,116},{24,120},{28,124... | collective-permute-start | bytes 73736 | tf_op jit(solution)/shard_map/ppermute | solution.py:74
  5.4 0.3 convolution_convert_fusion.1
  5.8 0.9 broadcast_in_dim.25
  6.7 10.3 %all-to-all-start = ((bf16[8,9,16,256]{3,2,1,0:T(8,128)(2,1)}), bf16[8,9,16,256]{3,2,1,0:T(8,128)(2,1)S(1)}, u32[]{:S(2)}, u32[]{:S(2)}) async-start(bf16[8,9,16,256]{3,2,1,0:T(8,128)(2,1)} %broadcast_in_dim.25), calls=%async_computation | async-start | bytes 1179648 | tf_op jit(solution)/shard_map/all_to_all | solution.py:137
  17.0 1.9 %collective-permute-start = (bf16[7,24,256]{2,1,0:T(8,128)(2,1)S(1)}, bf16[7,24,256]{2,1,0:T(8,128)(2,1)S(1)}, u32[]{:S(2)}, u32[]{:S(2)}) collective-permute-start(bf16[7,24,256]{2,1,0:T(8,128)(2,1)S(1)} %bitcast.109), channel_id=1, source_target_pairs={{0,64},{64,0},{1,65},{65,1},{2,66},{66,2},{3,67},{67,3},{4,68},{68... | collective-permute-start | bytes 258056 | tf_op jit(solution)/shard_map/ppermute | solution.py:77
  19.0 4.3 %collective-permute-done = bf16[7,24,256]{2,1,0:T(8,128)(2,1)S(1)} collective-permute-done((bf16[7,24,256]{2,1,0:T(8,128)(2,1)S(1)}, bf16[7,24,256]{2,1,0:T(8,128)(2,1)S(1)}, u32[]{:S(2)}, u32[]{:S(2)}) %collective-permute-start) | collective-permute-done | bytes 86048 | tf_op jit(solution)/shard_map/ppermute | solution.py:77
  23.4 3.1 %collective-permute-start.3 = (bf16[16,24,256]{2,1,0:T(8,128)(2,1)S(1)}, bf16[16,24,256]{2,1,0:T(8,128)(2,1)S(1)}, u32[]{:S(2)}, u32[]{:S(2)}) collective-permute-start(bf16[16,24,256]{2,1,0:T(8,128)(2,1)S(1)} %pad_maximum_fusion.6), channel_id=1, source_target_pairs={{0,128},{128,0},{1,129},{129,1},{2,130},{130,2},{3,131},{131,3},{4... | collective-permute-start | bytes 589832 | tf_op jit(solution)/shard_map/ppermute | solution.py:81
  26.6 4.4 %collective-permute-done.3 = bf16[16,24,256]{2,1,0:T(8,128)(2,1)S(1)} collective-permute-done((bf16[16,24,256]{2,1,0:T(8,128)(2,1)S(1)}, bf16[16,24,256]{2,1,0:T(8,128)(2,1)S(1)}, u32[]{:S(2)}, u32[]{:S(2)}) %collective-permute-start.3) | collective-permute-done | bytes 196640 | tf_op jit(solution)/shard_map/ppermute | solution.py:81
  31.1 0.1 collective-permute-start.5
  31.2 0.4 collective-permute-start.4
  31.6 0.3 convolution_convert_fusion
  32.0 0.3 copy-done.4
  32.4 3.2 %all-to-all-done = bf16[8,9,16,256]{3,2,1,0:T(8,128)(2,1)S(1)} async-done(((bf16[8,9,16,256]{3,2,1,0:T(8,128)(2,1)}), bf16[8,9,16,256]{3,2,1,0:T(8,128)(2,1)S(1)}, u32[]{:S(2)}, u32[]{:S(2)}) %all-to-all-start) | async-done | bytes 589856 | tf_op jit(solution)/shard_map/all_to_all | solution.py:137
  35.6 1.9 %collective-permute-start.6 = (bf16[8,9,16,256]{3,2,1,0:T(8,128)(2,1)S(1)}, bf16[8,9,16,256]{3,2,1,0:T(8,128)(2,1)S(1)}, u32[]{:S(2)}, u32[]{:S(2)}) collective-permute-start(bf16[8,9,16,256]{3,2,1,0:T(8,128)(2,1)S(1)} %all-to-all-done), channel_id=1, source_target_pairs={{0,4},{4,0},{1,5},{5,1},{2,6},{6,2},{3,7},{7,3},{8,12},{12,8},{9,1... | collective-permute-start | bytes 1769480 | tf_op jit(solution)/shard_map/ppermute | solution.py:140
  37.5 0.4 fusion.7
  38.2 0.1 reshape.132
  38.5 0.9 collective-permute-done.6
  39.7 0.2 copy.23
  39.9 0.5 copy-done.6
  40.3 1.5 %fusion.2 = bf16[34,8,4,256]{3,1,2,0:T(8,128)(2,1)S(1)} fusion(bf16[3,3,256,256]{3,2,1,0:T(8,128)(2,1)S(1)} %bitcast.107, bf16[36,1,7,2,256]{4,2,3,0,1:T(8,128)(2,1)S(1)} %slice.206, bf16[36,1,8,4,256]{4,2,3,0,1:T(8,128)(2,1)S(1)} %copy.22, pred[8,4]{0,1:T(4,128)(4,1)S(1)} %copy-done.6), kind=kOutput, calls=%fused_computation.5 | convolution fusion | flops 1286668288 | bytes 2584608 | tf_op jit(solution)/shard_map/conv_general_dilated | solution.py:98
  41.9 0.2 copy.25
  42.4 0.1 reshape.124
  42.6 0.1 fusion.45
  42.7 0.1 pad_slice_fusion.19
  43.4 6.2 %collective-permute-start.9 = (bf16[392,128]{1,0:T(8,128)(2,1)S(1)}, bf16[392,128]{1,0:T(8,128)(2,1)S(1)}, u32[]{:S(2)}, u32[]{:S(2)}) collective-permute-start(bf16[392,128]{1,0:T(8,128)(2,1)S(1)} %get-tuple-element.28), channel_id=1, source_target_pairs={{0,3},{1,0},{2,1},{3,2},{4,7},{5,4},{6,5},{7,6},{8,11},{9,8},{10,9... | collective-permute-start | bytes 301064 | tf_op jit(solution)/shard_map/ppermute | solution.py:37
  49.5 3.8 %collective-permute-start.8 = (bf16[392,128]{1,0:T(8,128)(2,1)S(1)}, bf16[392,128]{1,0:T(8,128)(2,1)S(1)}, u32[]{:S(2)}, u32[]{:S(2)}) collective-permute-start(bf16[392,128]{1,0:T(8,128)(2,1)S(1)} %get-tuple-element.29), channel_id=1, source_target_pairs={{0,2},{1,3},{2,0},{3,1},{4,6},{5,7},{6,4},{7,5},{8,10},{9,11},{10,... | collective-permute-start | bytes 301064 | tf_op jit(solution)/shard_map/ppermute | solution.py:37
  53.3 4.5 %collective-permute-start.7 = (bf16[392,128]{1,0:T(8,128)(2,1)S(1)}, bf16[392,128]{1,0:T(8,128)(2,1)S(1)}, u32[]{:S(2)}, u32[]{:S(2)}) collective-permute-start(bf16[392,128]{1,0:T(8,128)(2,1)S(1)} %get-tuple-element.27), channel_id=1, source_target_pairs={{0,1},{1,2},{2,3},{3,0},{4,5},{5,6},{6,7},{7,4},{8,9},{9,10},{10,1... | collective-permute-start | bytes 301064 | tf_op jit(solution)/shard_map/ppermute | solution.py:37
  57.9 0.9 broadcast_in_dim.27
  58.8 4.5 %all-to-all-start.1 = ((bf16[8,9,16,256]{3,2,1,0:T(8,128)(2,1)}), bf16[8,9,16,256]{3,2,1,0:T(8,128)(2,1)S(1)}, u32[]{:S(2)}, u32[]{:S(2)}) async-start(bf16[8,9,16,256]{3,2,1,0:T(8,128)(2,1)} %broadcast_in_dim.27), calls=%async_computation.1 | async-start | bytes 1179648 | tf_op jit(solution)/shard_map/all_to_all | solution.py:150
  63.4 2.7 %collective-permute-start.10 = (bf16[1,392,128]{2,1,0:T(8,128)(2,1)S(1)}, bf16[1,392,128]{2,1,0:T(8,128)(2,1)S(1)}, u32[]{:S(2)}, u32[]{:S(2)}) collective-permute-start(bf16[1,392,128]{2,1,0:T(8,128)(2,1)S(1)} %fusion.31), channel_id=1, source_target_pairs={{0,64},{64,0},{1,65},{65,1},{2,66},{66,2},{3,67},{67,3},{4,68},{68... | collective-permute-start | bytes 301064 | tf_op jit(solution)/shard_map/ppermute | solution.py:44
  66.1 3.8 %collective-permute-done.10 = bf16[1,392,128]{2,1,0:T(8,128)(2,1)S(1)} collective-permute-done((bf16[1,392,128]{2,1,0:T(8,128)(2,1)S(1)}, bf16[1,392,128]{2,1,0:T(8,128)(2,1)S(1)}, u32[]{:S(2)}, u32[]{:S(2)}) %collective-permute-start.10) | collective-permute-done | bytes 100384 | tf_op jit(solution)/shard_map/ppermute | solution.py:44
  70.0 3.3 %collective-permute-start.11 = (bf16[2,392,128]{2,1,0:T(8,128)(2,1)S(1)}, bf16[2,392,128]{2,1,0:T(8,128)(2,1)S(1)}, u32[]{:S(2)}, u32[]{:S(2)}) collective-permute-start(bf16[2,392,128]{2,1,0:T(8,128)(2,1)S(1)} %pad_maximum_fusion.5), channel_id=1, source_target_pairs={{0,128},{128,0},{1,129},{129,1},{2,130},{130,2},{3,131},{131,3},{4... | collective-permute-start | bytes 602120 | tf_op jit(solution)/shard_map/ppermute | solution.py:44
  73.3 4.6 %collective-permute-done.11 = bf16[2,392,128]{2,1,0:T(8,128)(2,1)S(1)} collective-permute-done((bf16[2,392,128]{2,1,0:T(8,128)(2,1)S(1)}, bf16[2,392,128]{2,1,0:T(8,128)(2,1)S(1)}, u32[]{:S(2)}, u32[]{:S(2)}) %collective-permute-start.11) | collective-permute-done | bytes 200736 | tf_op jit(solution)/shard_map/ppermute | solution.py:44
  78.0 3.2 %all-to-all-done.1 = bf16[8,9,16,256]{3,2,1,0:T(8,128)(2,1)S(1)} async-done(((bf16[8,9,16,256]{3,2,1,0:T(8,128)(2,1)}), bf16[8,9,16,256]{3,2,1,0:T(8,128)(2,1)S(1)}, u32[]{:S(2)}, u32[]{:S(2)}) %all-to-all-start.1) | async-done | bytes 589856 | tf_op jit(solution)/shard_map/all_to_all | solution.py:150
  81.2 1.9 %collective-permute-start.12 = (bf16[8,9,16,256]{3,2,1,0:T(8,128)(2,1)S(1)}, bf16[8,9,16,256]{3,2,1,0:T(8,128)(2,1)S(1)}, u32[]{:S(2)}, u32[]{:S(2)}) collective-permute-start(bf16[8,9,16,256]{3,2,1,0:T(8,128)(2,1)S(1)} %all-to-all-done.1), channel_id=1, source_target_pairs={{0,4},{4,0},{1,5},{5,1},{2,6},{6,2},{3,7},{7,3},{8,12},{12,8},{9,1... | collective-permute-start | bytes 1769480 | tf_op jit(solution)/shard_map/ppermute | solution.py:154
  83.1 0.2 slice.172
  83.3 0.2 fusion.23
  83.8 0.3 maximum_bitcast_fusion.3
  84.4 0.7 collective-permute-done.12
  85.3 0.2 copy.29
  85.5 0.5 copy-done.5
  86.0 1.2 %fusion.3 = bf16[28,8,4,256]{3,1,2,0:T(8,128)(2,1)S(1)} fusion(bf16[3,3,256,256]{3,2,1,0:T(8,128)(2,1)S(1)} %bitcast.108, bf16[30,1,7,2,256]{4,2,3,0,1:T(8,128)(2,1)S(1)} %slice.224, bf16[30,1,8,4,256]{4,2,3,0,1:T(8,128)(2,1)S(1)} %copy.28, pred[8,4]{0,1:T(4,128)(4,1)S(1)} %copy-done.5), kind=kOutput, calls=%fused_computation.9 | convolution fusion | flops 1059635200 | bytes 2344992 | tf_op jit(solution)/shard_map/conv_general_dilated | solution.py:98
  87.2 0.2 copy.30
  87.6 0.1 fusion.46
  88.3 19.4 %all_to_all.15 = bf16[16,88,128]{2,1,0:T(8,128)(2,1)S(1)} all-to-all(bf16[16,88,128]{2,1,0:T(8,128)(2,1)S(1)} %bitcast.106), channel_id=1, replica_groups=mesh['xh'=2,'xl'=2,'ylo'=2,'z'=8,'core'=2,'ch'=4] {'xl','ylo','ch'}, dimensions={0} | all-to-all | bytes 720896 | tf_op jit(solution)/shard_map/all_to_all | solution.py:160
  107.9 0.8 fusion.30
  (85 shorter events, 3.7 us)
Async XLA Ops:
  0.0 5.4 %copy-start = (bf16[3,3,1,16,1024]{4,3,2,1,0:T(8,128)(2,1)S(1)}, bf16[3,3,1,16,1024]{4,3,2,1,0:T(8,128)(2,1)}, u32[]{:S(2)}) copy-start(bf16[3,3,1,16,1024]{4,3,2,1,0:T(8,128)(2,1)} %param.6) | copy-start | bytes 884740
  0.8 18.1 %collective-permute-start.1 = (bf16[2,24,256]{2,1,0:T(8,128)(2,1)S(1)}, bf16[2,24,256]{2,1,0:T(8,128)(2,1)S(1)}, u32[]{:S(2)}, u32[]{:S(2)}) collective-permute-start(bf16[2,24,256]{2,1,0:T(8,128)(2,1)S(1)} %select_bitcast_fusion.4), channel_id=1, source_target_pairs={{0,32},{4,36},{8,40},{12,44},{16,48},{20,52},{24,56},{28,60},{32,0... | collective-permute-start | bytes 73736 | tf_op jit(solution)/shard_map/ppermute | solution.py:74
  4.1 14.9 %collective-permute-start.2 = (bf16[2,24,256]{2,1,0:T(8,128)(2,1)S(1)}, bf16[2,24,256]{2,1,0:T(8,128)(2,1)S(1)}, u32[]{:S(2)}, u32[]{:S(2)}) collective-permute-start(bf16[2,24,256]{2,1,0:T(8,128)(2,1)S(1)} %select_bitcast_fusion.4), channel_id=1, source_target_pairs={{0,96},{4,100},{8,104},{12,108},{16,112},{20,116},{24,120},{28,124... | collective-permute-start | bytes 73736 | tf_op jit(solution)/shard_map/ppermute | solution.py:74
  5.8 11.2 %copy-start.1 = (bf16[1,7,24,256]{3,2,1,0:T(8,128)(2,1)S(1)}, bf16[1,7,24,256]{3,2,1,0:T(8,128)(2,1)}, u32[]{:S(2)}) copy-start(bf16[1,7,24,256]{3,2,1,0:T(8,128)(2,1)} %param.5) | copy-start | bytes 258052
  6.7 28.9 %all-to-all-start = ((bf16[8,9,16,256]{3,2,1,0:T(8,128)(2,1)}), bf16[8,9,16,256]{3,2,1,0:T(8,128)(2,1)S(1)}, u32[]{:S(2)}, u32[]{:S(2)}) async-start(bf16[8,9,16,256]{3,2,1,0:T(8,128)(2,1)} %broadcast_in_dim.25), calls=%async_computation | async-start | bytes 1179648 | tf_op jit(solution)/shard_map/all_to_all | solution.py:137
  17.0 6.4 %collective-permute-start = (bf16[7,24,256]{2,1,0:T(8,128)(2,1)S(1)}, bf16[7,24,256]{2,1,0:T(8,128)(2,1)S(1)}, u32[]{:S(2)}, u32[]{:S(2)}) collective-permute-start(bf16[7,24,256]{2,1,0:T(8,128)(2,1)S(1)} %bitcast.109), channel_id=1, source_target_pairs={{0,64},{64,0},{1,65},{65,1},{2,66},{66,2},{3,67},{67,3},{4,68},{68... | collective-permute-start | bytes 258056 | tf_op jit(solution)/shard_map/ppermute | solution.py:77
  19.0 12.7 %copy-start.3 = (bf16[3,3,1,16,1024]{4,3,2,1,0:T(8,128)(2,1)S(1)}, bf16[3,3,1,16,1024]{4,3,2,1,0:T(8,128)(2,1)}, u32[]{:S(2)}) copy-start(bf16[3,3,1,16,1024]{4,3,2,1,0:T(8,128)(2,1)} %param.8) | copy-start | bytes 884740
  23.4 7.6 %collective-permute-start.3 = (bf16[16,24,256]{2,1,0:T(8,128)(2,1)S(1)}, bf16[16,24,256]{2,1,0:T(8,128)(2,1)S(1)}, u32[]{:S(2)}, u32[]{:S(2)}) collective-permute-start(bf16[16,24,256]{2,1,0:T(8,128)(2,1)S(1)} %pad_maximum_fusion.6), channel_id=1, source_target_pairs={{0,128},{128,0},{1,129},{129,1},{2,130},{130,2},{3,131},{131,3},{4... | collective-permute-start | bytes 589832 | tf_op jit(solution)/shard_map/ppermute | solution.py:81
  31.1 6.4 %collective-permute-start.5 = (bf16[32,2,256]{2,1,0:T(2,128)(2,1)S(1)}, bf16[32,2,256]{2,1,0:T(2,128)(2,1)S(1)}, u32[]{:S(2)}, u32[]{:S(2)}) collective-permute-start(bf16[32,2,256]{2,1,0:T(2,128)(2,1)S(1)} %get-tuple-element.35), channel_id=1, source_target_pairs={{4,0},{8,4},{12,8},{16,12},{20,16},{24,20},{28,24},{32,28},{36,32}... | collective-permute-start | bytes 98312 | tf_op jit(solution)/shard_map/ppermute | solution.py:55
  31.2 6.3 %collective-permute-start.4 = (bf16[32,2,256]{2,1,0:T(2,128)(2,1)S(1)}, bf16[32,2,256]{2,1,0:T(2,128)(2,1)S(1)}, u32[]{:S(2)}, u32[]{:S(2)}) collective-permute-start(bf16[32,2,256]{2,1,0:T(2,128)(2,1)S(1)} %get-tuple-element.34), channel_id=1, source_target_pairs={{0,4},{4,8},{8,12},{12,16},{16,20},{20,24},{24,28},{28,32},{32,36}... | collective-permute-start | bytes 98312 | tf_op jit(solution)/shard_map/ppermute | solution.py:54
  31.6 0.7 copy-start.4
  35.6 3.9 %collective-permute-start.6 = (bf16[8,9,16,256]{3,2,1,0:T(8,128)(2,1)S(1)}, bf16[8,9,16,256]{3,2,1,0:T(8,128)(2,1)S(1)}, u32[]{:S(2)}, u32[]{:S(2)}) collective-permute-start(bf16[8,9,16,256]{3,2,1,0:T(8,128)(2,1)S(1)} %all-to-all-done), channel_id=1, source_target_pairs={{0,4},{4,0},{1,5},{5,1},{2,6},{6,2},{3,7},{7,3},{8,12},{12,8},{9,1... | collective-permute-start | bytes 1769480 | tf_op jit(solution)/shard_map/ppermute | solution.py:140
  39.7 0.7 copy-start.6
  43.4 14.6 %collective-permute-start.9 = (bf16[392,128]{1,0:T(8,128)(2,1)S(1)}, bf16[392,128]{1,0:T(8,128)(2,1)S(1)}, u32[]{:S(2)}, u32[]{:S(2)}) collective-permute-start(bf16[392,128]{1,0:T(8,128)(2,1)S(1)} %get-tuple-element.28), channel_id=1, source_target_pairs={{0,3},{1,0},{2,1},{3,2},{4,7},{5,4},{6,5},{7,6},{8,11},{9,8},{10,9... | collective-permute-start | bytes 301064 | tf_op jit(solution)/shard_map/ppermute | solution.py:37
  49.5 13.7 %collective-permute-start.8 = (bf16[392,128]{1,0:T(8,128)(2,1)S(1)}, bf16[392,128]{1,0:T(8,128)(2,1)S(1)}, u32[]{:S(2)}, u32[]{:S(2)}) collective-permute-start(bf16[392,128]{1,0:T(8,128)(2,1)S(1)} %get-tuple-element.29), channel_id=1, source_target_pairs={{0,2},{1,3},{2,0},{3,1},{4,6},{5,7},{6,4},{7,5},{8,10},{9,11},{10,... | collective-permute-start | bytes 301064 | tf_op jit(solution)/shard_map/ppermute | solution.py:37
  53.3 9.9 %collective-permute-start.7 = (bf16[392,128]{1,0:T(8,128)(2,1)S(1)}, bf16[392,128]{1,0:T(8,128)(2,1)S(1)}, u32[]{:S(2)}, u32[]{:S(2)}) collective-permute-start(bf16[392,128]{1,0:T(8,128)(2,1)S(1)} %get-tuple-element.27), channel_id=1, source_target_pairs={{0,1},{1,2},{2,3},{3,0},{4,5},{5,6},{6,7},{7,4},{8,9},{9,10},{10,1... | collective-permute-start | bytes 301064 | tf_op jit(solution)/shard_map/ppermute | solution.py:37
  58.8 22.4 %all-to-all-start.1 = ((bf16[8,9,16,256]{3,2,1,0:T(8,128)(2,1)}), bf16[8,9,16,256]{3,2,1,0:T(8,128)(2,1)S(1)}, u32[]{:S(2)}, u32[]{:S(2)}) async-start(bf16[8,9,16,256]{3,2,1,0:T(8,128)(2,1)} %broadcast_in_dim.27), calls=%async_computation.1 | async-start | bytes 1179648 | tf_op jit(solution)/shard_map/all_to_all | solution.py:150
  63.4 6.6 %collective-permute-start.10 = (bf16[1,392,128]{2,1,0:T(8,128)(2,1)S(1)}, bf16[1,392,128]{2,1,0:T(8,128)(2,1)S(1)}, u32[]{:S(2)}, u32[]{:S(2)}) collective-permute-start(bf16[1,392,128]{2,1,0:T(8,128)(2,1)S(1)} %fusion.31), channel_id=1, source_target_pairs={{0,64},{64,0},{1,65},{65,1},{2,66},{66,2},{3,67},{67,3},{4,68},{68... | collective-permute-start | bytes 301064 | tf_op jit(solution)/shard_map/ppermute | solution.py:44
  70.0 7.8 %collective-permute-start.11 = (bf16[2,392,128]{2,1,0:T(8,128)(2,1)S(1)}, bf16[2,392,128]{2,1,0:T(8,128)(2,1)S(1)}, u32[]{:S(2)}, u32[]{:S(2)}) collective-permute-start(bf16[2,392,128]{2,1,0:T(8,128)(2,1)S(1)} %pad_maximum_fusion.5), channel_id=1, source_target_pairs={{0,128},{128,0},{1,129},{129,1},{2,130},{130,2},{3,131},{131,3},{4... | collective-permute-start | bytes 602120 | tf_op jit(solution)/shard_map/ppermute | solution.py:44
  81.2 3.9 %collective-permute-start.12 = (bf16[8,9,16,256]{3,2,1,0:T(8,128)(2,1)S(1)}, bf16[8,9,16,256]{3,2,1,0:T(8,128)(2,1)S(1)}, u32[]{:S(2)}, u32[]{:S(2)}) collective-permute-start(bf16[8,9,16,256]{3,2,1,0:T(8,128)(2,1)S(1)} %all-to-all-done.1), channel_id=1, source_target_pairs={{0,4},{4,0},{1,5},{5,1},{2,6},{6,2},{3,7},{7,3},{8,12},{12,8},{9,1... | collective-permute-start | bytes 1769480 | tf_op jit(solution)/shard_map/ppermute | solution.py:154
  85.3 0.7 copy-start.5
  88.3 19.6 %copy-start.2 = (f32[256]{0:T(256)S(1)}, f32[256]{0:T(256)}, u32[]{:S(2)}) copy-start(f32[256]{0:T(256)} %param.9) | copy-start | bytes 3076

commit v8 on v7

--- a/solution.py
+++ b/solution.py
@@ -144,8 +144,9 @@
     count = rows * columns
     partial = folded(out.reshape(count, -1), half_of(count))
 
+    block = copies_of(quarter(kernel_two, member, groups))
+    block, partial = lax.optimization_barrier((block, partial))
     came = traded(partial, "ch")
-    block = copies_of(quarter(kernel_two, member, groups))
     block, came[3] = lax.optimization_barrier((block, came[3]))
     mine = lax.all_to_all(block, "z", 0, 0)
     bias = lax.dynamic_slice_in_dim(bias_one, member * SLICE, SLICE, 0)
@@ -156,9 +157,9 @@
     acts = jnp.concatenate([acts[k] for k in range(4)], axis=1)
     out = conv(acts.reshape(rows, columns, -1), mine, other, core)
     count = height * breadth
-    partial = folded(out.reshape(4, count, -1), half_of(count))
-    parts = lax.all_to_all(partial.reshape(4 * groups, -1, LANES), QUAD + ("ch",), 0, 0)
-    parts = parts.astype(jnp.float32).reshape(4, groups, -1, LANES).sum(1)
+    partial = folded(out.reshape(4, count, -1), half_of(count)).swapaxes(0, 1)
+    parts = lax.all_to_all(partial.reshape(4 * groups, -1, LANES), ("ch",) + QUAD, 0, 0)
+    parts = parts.astype(jnp.float32).reshape(groups, 4, -1, LANES).sum(0)
     second = unfolded(parts, count)
     second = jnp.concatenate([second[k] for k in range(4)], axis=1) + bias_two
     second = second.reshape(height, breadth, width)

time: 109 us -> 109 us (level)
  transfers between devices with their start and end apart: 15 -> 15, of which waited for: 8 -> 9; matrix products, arithmetic and copies ran while one was open for 5% -> 4% of each run, Pallas kernels for 0% -> 0%
where the time goes in v8:
time: 109 us
  starting transfers between devices  48.4 us (44%)
  waiting for transfers between devices  26 us (24%)
  blocking collectives  19.5 us (18%)
  local copies, waits for them, and re-layouts  6.14 us (6%)
  other arithmetic  4.58 us (4%)
  matrix products  3.4 us (3%)
    all_to_all x1, blocking collectives, body(): lax.all_to_all(partial.reshape(4 * groups, -1, LANES), ('ch',) + QUAD, 0, 0)  19.5 us
    all_to_all x2, starting transfers between devices, body(): mine = lax.all_to_all(block, 'z', 0, 0)  14.8 us
    ppermute x3, starting transfers between devices, traded(): lax.ppermute(sent, axis, [(i, (i + d) % count) for i in range(count)])  14.5 us
    ppermute x2, waiting for transfers between devices, from_quad(): other = lax.ppermute(blocks, axis, SWAP)  9.19 us
    all_to_all x2, waiting for transfers between devices, body(): mine = lax.all_to_all(block, 'z', 0, 0)  5.58 us
    ppermute x2, starting transfers between devices, from_quad(): other = lax.ppermute(blocks, axis, SWAP)  5.2 us
    ppermute x2, starting transfers between devices, region(): lax.ppermute(sent, LAT + LON, edge_pairs(8, lon, f))  4.56 us
    ppermute x1, waiting for transfers between devices, region(): other = lax.ppermute(both, 'xl', SWAP)  4.41 us
  transfers between devices with their start and end apart: 15, of which 9 were waited for; matrix products, arithmetic and copies ran while one was open for 4% of the time, Pallas kernels for 0%

profile of v8, /device:TPU:10, one launch (start us, length us, event | category | flops | bytes accessed | tf_op | source)
XLA Modules:
  0.0 108.8 jit_solution(8037774796406083213)
XLA Ops:
  0.0 0.8 select_bitcast_fusion.4
  0.8 3.3 %collective-permute-start.1 = (bf16[2,24,256]{2,1,0:T(8,128)(2,1)S(1)}, bf16[2,24,256]{2,1,0:T(8,128)(2,1)S(1)}, u32[]{:S(2)}, u32[]{:S(2)}) collective-permute-start(bf16[2,24,256]{2,1,0:T(8,128)(2,1)S(1)} %select_bitcast_fusion.4), channel_id=1, source_target_pairs={{0,32},{4,36},{8,40},{12,44},{16,48},{20,52},{24,56},{28,60},{32,0... | collective-permute-start | bytes 73736 | tf_op jit(solution)/shard_map/ppermute | solution.py:74
  4.1 1.3 %collective-permute-start.2 = (bf16[2,24,256]{2,1,0:T(8,128)(2,1)S(1)}, bf16[2,24,256]{2,1,0:T(8,128)(2,1)S(1)}, u32[]{:S(2)}, u32[]{:S(2)}) collective-permute-start(bf16[2,24,256]{2,1,0:T(8,128)(2,1)S(1)} %select_bitcast_fusion.4), channel_id=1, source_target_pairs={{0,96},{4,100},{8,104},{12,108},{16,112},{20,116},{24,120},{28,124... | collective-permute-start | bytes 73736 | tf_op jit(solution)/shard_map/ppermute | solution.py:74
  5.4 0.3 convolution_convert_fusion
  5.8 0.9 broadcast_in_dim.27
  6.7 10.3 %all-to-all-start = ((bf16[8,9,16,256]{3,2,1,0:T(8,128)(2,1)}), bf16[8,9,16,256]{3,2,1,0:T(8,128)(2,1)S(1)}, u32[]{:S(2)}, u32[]{:S(2)}) async-start(bf16[8,9,16,256]{3,2,1,0:T(8,128)(2,1)} %broadcast_in_dim.27), calls=%async_computation | async-start | bytes 1179648 | tf_op jit(solution)/shard_map/all_to_all | solution.py:137
  17.0 1.9 %collective-permute-start = (bf16[7,24,256]{2,1,0:T(8,128)(2,1)S(1)}, bf16[7,24,256]{2,1,0:T(8,128)(2,1)S(1)}, u32[]{:S(2)}, u32[]{:S(2)}) collective-permute-start(bf16[7,24,256]{2,1,0:T(8,128)(2,1)S(1)} %bitcast.105), channel_id=1, source_target_pairs={{0,64},{64,0},{1,65},{65,1},{2,66},{66,2},{3,67},{67,3},{4,68},{68... | collective-permute-start | bytes 258056 | tf_op jit(solution)/shard_map/ppermute | solution.py:77
  19.0 4.3 %collective-permute-done = bf16[7,24,256]{2,1,0:T(8,128)(2,1)S(1)} collective-permute-done((bf16[7,24,256]{2,1,0:T(8,128)(2,1)S(1)}, bf16[7,24,256]{2,1,0:T(8,128)(2,1)S(1)}, u32[]{:S(2)}, u32[]{:S(2)}) %collective-permute-start) | collective-permute-done | bytes 86048 | tf_op jit(solution)/shard_map/ppermute | solution.py:77
  23.4 3.1 %collective-permute-start.3 = (bf16[16,24,256]{2,1,0:T(8,128)(2,1)S(1)}, bf16[16,24,256]{2,1,0:T(8,128)(2,1)S(1)}, u32[]{:S(2)}, u32[]{:S(2)}) collective-permute-start(bf16[16,24,256]{2,1,0:T(8,128)(2,1)S(1)} %pad_maximum_fusion.6), channel_id=1, source_target_pairs={{0,128},{128,0},{1,129},{129,1},{2,130},{130,2},{3,131},{131,3},{4... | collective-permute-start | bytes 589832 | tf_op jit(solution)/shard_map/ppermute | solution.py:81
  26.6 4.4 %collective-permute-done.3 = bf16[16,24,256]{2,1,0:T(8,128)(2,1)S(1)} collective-permute-done((bf16[16,24,256]{2,1,0:T(8,128)(2,1)S(1)}, bf16[16,24,256]{2,1,0:T(8,128)(2,1)S(1)}, u32[]{:S(2)}, u32[]{:S(2)}) %collective-permute-start.3) | collective-permute-done | bytes 196640 | tf_op jit(solution)/shard_map/ppermute | solution.py:81
  31.1 0.1 collective-permute-start.5
  31.2 0.4 collective-permute-start.4
  31.6 0.3 convolution_convert_fusion.1
  32.0 0.3 copy-done.4
  32.4 3.2 %all-to-all-done = bf16[8,9,16,256]{3,2,1,0:T(8,128)(2,1)S(1)} async-done(((bf16[8,9,16,256]{3,2,1,0:T(8,128)(2,1)}), bf16[8,9,16,256]{3,2,1,0:T(8,128)(2,1)S(1)}, u32[]{:S(2)}, u32[]{:S(2)}) %all-to-all-start) | async-done | bytes 589856 | tf_op jit(solution)/shard_map/all_to_all | solution.py:137
  35.6 1.9 %collective-permute-start.6 = (bf16[8,9,16,256]{3,2,1,0:T(8,128)(2,1)S(1)}, bf16[8,9,16,256]{3,2,1,0:T(8,128)(2,1)S(1)}, u32[]{:S(2)}, u32[]{:S(2)}) collective-permute-start(bf16[8,9,16,256]{3,2,1,0:T(8,128)(2,1)S(1)} %all-to-all-done), channel_id=1, source_target_pairs={{0,4},{4,0},{1,5},{5,1},{2,6},{6,2},{3,7},{7,3},{8,12},{12,8},{9,1... | collective-permute-start | bytes 1769480 | tf_op jit(solution)/shard_map/ppermute | solution.py:140
  37.5 0.4 fusion.7
  38.2 0.1 reshape.132
  38.5 0.9 collective-permute-done.6
  39.7 0.2 copy.20
  39.9 0.5 copy-done.6
  40.3 1.5 %fusion.2 = bf16[34,8,4,256]{3,1,2,0:T(8,128)(2,1)S(1)} fusion(bf16[3,3,256,256]{3,2,1,0:T(8,128)(2,1)S(1)} %bitcast.103, bf16[36,1,7,2,256]{4,2,3,0,1:T(8,128)(2,1)S(1)} %slice.206, bf16[36,1,8,4,256]{4,2,3,0,1:T(8,128)(2,1)S(1)} %copy.19, pred[8,4]{0,1:T(4,128)(4,1)S(1)} %copy-done.6), kind=kOutput, calls=%fused_computation.5 | convolution fusion | flops 1286668288 | bytes 2584608 | tf_op jit(solution)/shard_map/conv_general_dilated | solution.py:98
  41.9 0.2 copy.22
  42.6 0.1 fusion.45
  42.7 0.1 pad_slice_fusion.19
  43.3 0.9 broadcast_in_dim.24
  44.2 6.2 %collective-permute-start.9 = (bf16[392,128]{1,0:T(8,128)(2,1)S(1)}, bf16[392,128]{1,0:T(8,128)(2,1)S(1)}, u32[]{:S(2)}, u32[]{:S(2)}) collective-permute-start(bf16[392,128]{1,0:T(8,128)(2,1)S(1)} %get-tuple-element.32), channel_id=1, source_target_pairs={{0,3},{1,0},{2,1},{3,2},{4,7},{5,4},{6,5},{7,6},{8,11},{9,8},{10,9... | collective-permute-start | bytes 301064 | tf_op jit(solution)/shard_map/ppermute | solution.py:37
  50.4 3.8 %collective-permute-start.8 = (bf16[392,128]{1,0:T(8,128)(2,1)S(1)}, bf16[392,128]{1,0:T(8,128)(2,1)S(1)}, u32[]{:S(2)}, u32[]{:S(2)}) collective-permute-start(bf16[392,128]{1,0:T(8,128)(2,1)S(1)} %get-tuple-element.33), channel_id=1, source_target_pairs={{0,2},{1,3},{2,0},{3,1},{4,6},{5,7},{6,4},{7,5},{8,10},{9,11},{10,... | collective-permute-start | bytes 301064 | tf_op jit(solution)/shard_map/ppermute | solution.py:37
  54.2 4.5 %collective-permute-start.7 = (bf16[392,128]{1,0:T(8,128)(2,1)S(1)}, bf16[392,128]{1,0:T(8,128)(2,1)S(1)}, u32[]{:S(2)}, u32[]{:S(2)}) collective-permute-start(bf16[392,128]{1,0:T(8,128)(2,1)S(1)} %get-tuple-element.31), channel_id=1, source_target_pairs={{0,1},{1,2},{2,3},{3,0},{4,5},{5,6},{6,7},{7,4},{8,9},{9,10},{10,1... | collective-permute-start | bytes 301064 | tf_op jit(solution)/shard_map/ppermute | solution.py:37
  58.8 4.5 %all-to-all-start.1 = ((bf16[8,9,16,256]{3,2,1,0:T(8,128)(2,1)}), bf16[8,9,16,256]{3,2,1,0:T(8,128)(2,1)S(1)}, u32[]{:S(2)}, u32[]{:S(2)}) async-start(bf16[8,9,16,256]{3,2,1,0:T(8,128)(2,1)} %broadcast_in_dim.24), calls=%async_computation.1 | async-start | bytes 1179648 | tf_op jit(solution)/shard_map/all_to_all | solution.py:151
  63.2 0.9 collective-permute-done.7
  64.2 1.9 %collective-permute-start.10 = (bf16[1,392,128]{2,1,0:T(8,128)(2,1)S(1)}, bf16[1,392,128]{2,1,0:T(8,128)(2,1)S(1)}, u32[]{:S(2)}, u32[]{:S(2)}) collective-permute-start(bf16[1,392,128]{2,1,0:T(8,128)(2,1)S(1)} %fusion.31), channel_id=1, source_target_pairs={{0,64},{64,0},{1,65},{65,1},{2,66},{66,2},{3,67},{67,3},{4,68},{68... | collective-permute-start | bytes 301064 | tf_op jit(solution)/shard_map/ppermute | solution.py:44
  66.2 4.6 %collective-permute-done.10 = bf16[1,392,128]{2,1,0:T(8,128)(2,1)S(1)} collective-permute-done((bf16[1,392,128]{2,1,0:T(8,128)(2,1)S(1)}, bf16[1,392,128]{2,1,0:T(8,128)(2,1)S(1)}, u32[]{:S(2)}, u32[]{:S(2)}) %collective-permute-start.10) | collective-permute-done | bytes 100384 | tf_op jit(solution)/shard_map/ppermute | solution.py:44
  70.9 3.3 %collective-permute-start.11 = (bf16[2,392,128]{2,1,0:T(8,128)(2,1)S(1)}, bf16[2,392,128]{2,1,0:T(8,128)(2,1)S(1)}, u32[]{:S(2)}, u32[]{:S(2)}) collective-permute-start(bf16[2,392,128]{2,1,0:T(8,128)(2,1)S(1)} %pad_maximum_fusion.5), channel_id=1, source_target_pairs={{0,128},{128,0},{1,129},{129,1},{2,130},{130,2},{3,131},{131,3},{4... | collective-permute-start | bytes 602120 | tf_op jit(solution)/shard_map/ppermute | solution.py:44
  74.2 4.6 %collective-permute-done.11 = bf16[2,392,128]{2,1,0:T(8,128)(2,1)S(1)} collective-permute-done((bf16[2,392,128]{2,1,0:T(8,128)(2,1)S(1)}, bf16[2,392,128]{2,1,0:T(8,128)(2,1)S(1)}, u32[]{:S(2)}, u32[]{:S(2)}) %collective-permute-start.11) | collective-permute-done | bytes 200736 | tf_op jit(solution)/shard_map/ppermute | solution.py:44
  78.8 2.4 %all-to-all-done.1 = bf16[8,9,16,256]{3,2,1,0:T(8,128)(2,1)S(1)} async-done(((bf16[8,9,16,256]{3,2,1,0:T(8,128)(2,1)}), bf16[8,9,16,256]{3,2,1,0:T(8,128)(2,1)S(1)}, u32[]{:S(2)}, u32[]{:S(2)}) %all-to-all-start.1) | async-done | bytes 589856 | tf_op jit(solution)/shard_map/all_to_all | solution.py:151
  81.2 1.9 %collective-permute-start.12 = (bf16[8,9,16,256]{3,2,1,0:T(8,128)(2,1)S(1)}, bf16[8,9,16,256]{3,2,1,0:T(8,128)(2,1)S(1)}, u32[]{:S(2)}, u32[]{:S(2)}) collective-permute-start(bf16[8,9,16,256]{3,2,1,0:T(8,128)(2,1)S(1)} %all-to-all-done.1), channel_id=1, source_target_pairs={{0,4},{4,0},{1,5},{5,1},{2,6},{6,2},{3,7},{7,3},{8,12},{12,8},{9,1... | collective-permute-start | bytes 1769480 | tf_op jit(solution)/shard_map/ppermute | solution.py:155
  83.1 0.2 slice.172
  83.3 0.2 fusion.23
  83.7 0.3 maximum_bitcast_fusion.3
  84.4 0.7 collective-permute-done.12
  85.3 0.2 copy.26
  85.5 0.5 copy-done.5
  85.9 1.2 %fusion.3 = bf16[28,8,4,256]{3,1,2,0:T(8,128)(2,1)S(1)} fusion(bf16[3,3,256,256]{3,2,1,0:T(8,128)(2,1)S(1)} %bitcast.104, bf16[30,1,7,2,256]{4,2,3,0,1:T(8,128)(2,1)S(1)} %slice.224, bf16[30,1,8,4,256]{4,2,3,0,1:T(8,128)(2,1)S(1)} %copy.25, pred[8,4]{0,1:T(4,128)(4,1)S(1)} %copy-done.5), kind=kOutput, calls=%fused_computation.9 | convolution fusion | flops 1059635200 | bytes 2344992 | tf_op jit(solution)/shard_map/conv_general_dilated | solution.py:98
  87.2 0.2 copy.27
  87.6 0.1 fusion.46
  88.3 19.5 %all_to_all.15 = bf16[16,88,128]{2,1,0:T(8,128)(2,1)S(1)} all-to-all(bf16[16,88,128]{2,1,0:T(8,128)(2,1)S(1)} %bitcast.101), channel_id=1, replica_groups=mesh['xh'=2,'xl'=2,'ylo'=2,'z'=8,'core'=2,'ch'=4] {'ch','xl','ylo'}, dimensions={0} | all-to-all | bytes 720896 | tf_op jit(solution)/shard_map/all_to_all | solution.py:161
  108.0 0.8 fusion.30
  (85 shorter events, 3.8 us)
Async XLA Ops:
  0.0 5.4 %copy-start = (bf16[3,3,1,16,1024]{4,3,2,1,0:T(8,128)(2,1)S(1)}, bf16[3,3,1,16,1024]{4,3,2,1,0:T(8,128)(2,1)}, u32[]{:S(2)}) copy-start(bf16[3,3,1,16,1024]{4,3,2,1,0:T(8,128)(2,1)} %param.6) | copy-start | bytes 884740
  0.8 18.1 %collective-permute-start.1 = (bf16[2,24,256]{2,1,0:T(8,128)(2,1)S(1)}, bf16[2,24,256]{2,1,0:T(8,128)(2,1)S(1)}, u32[]{:S(2)}, u32[]{:S(2)}) collective-permute-start(bf16[2,24,256]{2,1,0:T(8,128)(2,1)S(1)} %select_bitcast_fusion.4), channel_id=1, source_target_pairs={{0,32},{4,36},{8,40},{12,44},{16,48},{20,52},{24,56},{28,60},{32,0... | collective-permute-start | bytes 73736 | tf_op jit(solution)/shard_map/ppermute | solution.py:74
  4.1 14.9 %collective-permute-start.2 = (bf16[2,24,256]{2,1,0:T(8,128)(2,1)S(1)}, bf16[2,24,256]{2,1,0:T(8,128)(2,1)S(1)}, u32[]{:S(2)}, u32[]{:S(2)}) collective-permute-start(bf16[2,24,256]{2,1,0:T(8,128)(2,1)S(1)} %select_bitcast_fusion.4), channel_id=1, source_target_pairs={{0,96},{4,100},{8,104},{12,108},{16,112},{20,116},{24,120},{28,124... | collective-permute-start | bytes 73736 | tf_op jit(solution)/shard_map/ppermute | solution.py:74
  5.8 11.2 %copy-start.1 = (bf16[1,7,24,256]{3,2,1,0:T(8,128)(2,1)S(1)}, bf16[1,7,24,256]{3,2,1,0:T(8,128)(2,1)}, u32[]{:S(2)}) copy-start(bf16[1,7,24,256]{3,2,1,0:T(8,128)(2,1)} %param.5) | copy-start | bytes 258052
  6.7 28.9 %all-to-all-start = ((bf16[8,9,16,256]{3,2,1,0:T(8,128)(2,1)}), bf16[8,9,16,256]{3,2,1,0:T(8,128)(2,1)S(1)}, u32[]{:S(2)}, u32[]{:S(2)}) async-start(bf16[8,9,16,256]{3,2,1,0:T(8,128)(2,1)} %broadcast_in_dim.27), calls=%async_computation | async-start | bytes 1179648 | tf_op jit(solution)/shard_map/all_to_all | solution.py:137
  17.0 6.4 %collective-permute-start = (bf16[7,24,256]{2,1,0:T(8,128)(2,1)S(1)}, bf16[7,24,256]{2,1,0:T(8,128)(2,1)S(1)}, u32[]{:S(2)}, u32[]{:S(2)}) collective-permute-start(bf16[7,24,256]{2,1,0:T(8,128)(2,1)S(1)} %bitcast.105), channel_id=1, source_target_pairs={{0,64},{64,0},{1,65},{65,1},{2,66},{66,2},{3,67},{67,3},{4,68},{68... | collective-permute-start | bytes 258056 | tf_op jit(solution)/shard_map/ppermute | solution.py:77
  19.0 12.7 %copy-start.3 = (bf16[3,3,1,16,1024]{4,3,2,1,0:T(8,128)(2,1)S(1)}, bf16[3,3,1,16,1024]{4,3,2,1,0:T(8,128)(2,1)}, u32[]{:S(2)}) copy-start(bf16[3,3,1,16,1024]{4,3,2,1,0:T(8,128)(2,1)} %param.8) | copy-start | bytes 884740
  23.4 7.6 %collective-permute-start.3 = (bf16[16,24,256]{2,1,0:T(8,128)(2,1)S(1)}, bf16[16,24,256]{2,1,0:T(8,128)(2,1)S(1)}, u32[]{:S(2)}, u32[]{:S(2)}) collective-permute-start(bf16[16,24,256]{2,1,0:T(8,128)(2,1)S(1)} %pad_maximum_fusion.6), channel_id=1, source_target_pairs={{0,128},{128,0},{1,129},{129,1},{2,130},{130,2},{3,131},{131,3},{4... | collective-permute-start | bytes 589832 | tf_op jit(solution)/shard_map/ppermute | solution.py:81
  31.1 6.4 %collective-permute-start.5 = (bf16[32,2,256]{2,1,0:T(2,128)(2,1)S(1)}, bf16[32,2,256]{2,1,0:T(2,128)(2,1)S(1)}, u32[]{:S(2)}, u32[]{:S(2)}) collective-permute-start(bf16[32,2,256]{2,1,0:T(2,128)(2,1)S(1)} %get-tuple-element.39), channel_id=1, source_target_pairs={{4,0},{8,4},{12,8},{16,12},{20,16},{24,20},{28,24},{32,28},{36,32}... | collective-permute-start | bytes 98312 | tf_op jit(solution)/shard_map/ppermute | solution.py:55
  31.2 6.3 %collective-permute-start.4 = (bf16[32,2,256]{2,1,0:T(2,128)(2,1)S(1)}, bf16[32,2,256]{2,1,0:T(2,128)(2,1)S(1)}, u32[]{:S(2)}, u32[]{:S(2)}) collective-permute-start(bf16[32,2,256]{2,1,0:T(2,128)(2,1)S(1)} %get-tuple-element.38), channel_id=1, source_target_pairs={{0,4},{4,8},{8,12},{12,16},{16,20},{20,24},{24,28},{28,32},{32,36}... | collective-permute-start | bytes 98312 | tf_op jit(solution)/shard_map/ppermute | solution.py:54
  31.6 0.7 copy-start.4
  35.6 3.9 %collective-permute-start.6 = (bf16[8,9,16,256]{3,2,1,0:T(8,128)(2,1)S(1)}, bf16[8,9,16,256]{3,2,1,0:T(8,128)(2,1)S(1)}, u32[]{:S(2)}, u32[]{:S(2)}) collective-permute-start(bf16[8,9,16,256]{3,2,1,0:T(8,128)(2,1)S(1)} %all-to-all-done), channel_id=1, source_target_pairs={{0,4},{4,0},{1,5},{5,1},{2,6},{6,2},{3,7},{7,3},{8,12},{12,8},{9,1... | collective-permute-start | bytes 1769480 | tf_op jit(solution)/shard_map/ppermute | solution.py:140
  39.7 0.7 copy-start.6
  44.2 14.6 %collective-permute-start.9 = (bf16[392,128]{1,0:T(8,128)(2,1)S(1)}, bf16[392,128]{1,0:T(8,128)(2,1)S(1)}, u32[]{:S(2)}, u32[]{:S(2)}) collective-permute-start(bf16[392,128]{1,0:T(8,128)(2,1)S(1)} %get-tuple-element.32), channel_id=1, source_target_pairs={{0,3},{1,0},{2,1},{3,2},{4,7},{5,4},{6,5},{7,6},{8,11},{9,8},{10,9... | collective-permute-start | bytes 301064 | tf_op jit(solution)/shard_map/ppermute | solution.py:37
  50.4 12.9 %collective-permute-start.8 = (bf16[392,128]{1,0:T(8,128)(2,1)S(1)}, bf16[392,128]{1,0:T(8,128)(2,1)S(1)}, u32[]{:S(2)}, u32[]{:S(2)}) collective-permute-start(bf16[392,128]{1,0:T(8,128)(2,1)S(1)} %get-tuple-element.33), channel_id=1, source_target_pairs={{0,2},{1,3},{2,0},{3,1},{4,6},{5,7},{6,4},{7,5},{8,10},{9,11},{10,... | collective-permute-start | bytes 301064 | tf_op jit(solution)/shard_map/ppermute | solution.py:37
  54.2 9.9 %collective-permute-start.7 = (bf16[392,128]{1,0:T(8,128)(2,1)S(1)}, bf16[392,128]{1,0:T(8,128)(2,1)S(1)}, u32[]{:S(2)}, u32[]{:S(2)}) collective-permute-start(bf16[392,128]{1,0:T(8,128)(2,1)S(1)} %get-tuple-element.31), channel_id=1, source_target_pairs={{0,1},{1,2},{2,3},{3,0},{4,5},{5,6},{6,7},{7,4},{8,9},{9,10},{10,1... | collective-permute-start | bytes 301064 | tf_op jit(solution)/shard_map/ppermute | solution.py:37
  58.8 22.4 %all-to-all-start.1 = ((bf16[8,9,16,256]{3,2,1,0:T(8,128)(2,1)}), bf16[8,9,16,256]{3,2,1,0:T(8,128)(2,1)S(1)}, u32[]{:S(2)}, u32[]{:S(2)}) async-start(bf16[8,9,16,256]{3,2,1,0:T(8,128)(2,1)} %broadcast_in_dim.24), calls=%async_computation.1 | async-start | bytes 1179648 | tf_op jit(solution)/shard_map/all_to_all | solution.py:151
  64.2 6.6 %collective-permute-start.10 = (bf16[1,392,128]{2,1,0:T(8,128)(2,1)S(1)}, bf16[1,392,128]{2,1,0:T(8,128)(2,1)S(1)}, u32[]{:S(2)}, u32[]{:S(2)}) collective-permute-start(bf16[1,392,128]{2,1,0:T(8,128)(2,1)S(1)} %fusion.31), channel_id=1, source_target_pairs={{0,64},{64,0},{1,65},{65,1},{2,66},{66,2},{3,67},{67,3},{4,68},{68... | collective-permute-start | bytes 301064 | tf_op jit(solution)/shard_map/ppermute | solution.py:44
  70.9 7.8 %collective-permute-start.11 = (bf16[2,392,128]{2,1,0:T(8,128)(2,1)S(1)}, bf16[2,392,128]{2,1,0:T(8,128)(2,1)S(1)}, u32[]{:S(2)}, u32[]{:S(2)}) collective-permute-start(bf16[2,392,128]{2,1,0:T(8,128)(2,1)S(1)} %pad_maximum_fusion.5), channel_id=1, source_target_pairs={{0,128},{128,0},{1,129},{129,1},{2,130},{130,2},{3,131},{131,3},{4... | collective-permute-start | bytes 602120 | tf_op jit(solution)/shard_map/ppermute | solution.py:44
  81.2 3.9 %collective-permute-start.12 = (bf16[8,9,16,256]{3,2,1,0:T(8,128)(2,1)S(1)}, bf16[8,9,16,256]{3,2,1,0:T(8,128)(2,1)S(1)}, u32[]{:S(2)}, u32[]{:S(2)}) collective-permute-start(bf16[8,9,16,256]{3,2,1,0:T(8,128)(2,1)S(1)} %all-to-all-done.1), channel_id=1, source_target_pairs={{0,4},{4,0},{1,5},{5,1},{2,6},{6,2},{3,7},{7,3},{8,12},{12,8},{9,1... | collective-permute-start | bytes 1769480 | tf_op jit(solution)/shard_map/ppermute | solution.py:155
  85.3 0.7 copy-start.5
  88.3 19.7 %copy-start.2 = (f32[256]{0:T(256)S(1)}, f32[256]{0:T(256)}, u32[]{:S(2)}) copy-start(f32[256]{0:T(256)} %param.9) | copy-start | bytes 3076

commit v9 on v8

--- a/solution.py
+++ b/solution.py
@@ -147,7 +147,7 @@
     block = copies_of(quarter(kernel_two, member, groups))
     block, partial = lax.optimization_barrier((block, partial))
     came = traded(partial, "ch")
-    block, came[3] = lax.optimization_barrier((block, came[3]))
+    block, came[1] = lax.optimization_barrier((block, came[1]))
     mine = lax.all_to_all(block, "z", 0, 0)
     bias = lax.dynamic_slice_in_dim(bias_one, member * SLICE, SLICE, 0)
     hidden = sum(part.astype(jnp.float32) for part in came) + jnp.concatenate([bias, bias])

time: 109 us -> 117 us (1.073)
  the two profiles are of different devices: /device:TPU:10 before, /device:TPU:14 now
where the time goes in v9:
time: 117 us; the launch traced here: 116 us
  starting transfers between devices  48.6 us (42%)
  waiting for transfers between devices  34.5 us (29%)
  blocking collectives  18.3 us (16%)
  local copies, waits for them, and re-layouts  6.14 us (5%)
  other arithmetic  4.59 us (4%)
  matrix products  3.39 us (3%)
    all_to_all x1, blocking collectives, body(): lax.all_to_all(partial.reshape(4 * groups, -1, LANES), ('ch',) + QUAD, 0, 0)  18.3 us
    ppermute x3, starting transfers between devices, traded(): lax.ppermute(sent, axis, [(i, (i + d) % count) for i in range(count)])  13.7 us
    ppermute x2, starting transfers between devices, region(): lax.ppermute(sent, LAT + LON, edge_pairs(8, lon, f))  12.2 us
    all_to_all x2, starting transfers between devices, body(): mine = lax.all_to_all(block, 'z', 0, 0)  10.7 us
    ppermute x2, waiting for transfers between devices, from_quad(): other = lax.ppermute(blocks, axis, SWAP)  10.3 us
    all_to_all x2, waiting for transfers between devices, body(): mine = lax.all_to_all(block, 'z', 0, 0)  7.59 us
    ppermute x1, waiting for transfers between devices, region(): other = lax.ppermute(both, 'xl', SWAP)  5.64 us
    ppermute x3, waiting for transfers between devices, traded(): lax.ppermute(sent, axis, [(i, (i + d) % count) for i in range(count)])  5.04 us
  transfers between devices with their start and end apart: 15, of which 9 were waited for; matrix products, arithmetic and copies ran while one was open for 4% of the time, Pallas kernels for 0%

profile of v9, /device:TPU:14, one launch (start us, length us, event | category | flops | bytes accessed | tf_op | source)
XLA Modules:
  0.0 116.3 jit_solution(5038501100837463671)
XLA Ops:
  0.0 0.8 select_bitcast_fusion.4
  0.8 10.9 %collective-permute-start.1 = (bf16[2,24,256]{2,1,0:T(8,128)(2,1)S(1)}, bf16[2,24,256]{2,1,0:T(8,128)(2,1)S(1)}, u32[]{:S(2)}, u32[]{:S(2)}) collective-permute-start(bf16[2,24,256]{2,1,0:T(8,128)(2,1)S(1)} %select_bitcast_fusion.4), channel_id=1, source_target_pairs={{0,32},{4,36},{8,40},{12,44},{16,48},{20,52},{24,56},{28,60},{32,0... | collective-permute-start | bytes 73736 | tf_op jit(solution)/shard_map/ppermute | solution.py:74
  11.7 1.3 %collective-permute-start.2 = (bf16[2,24,256]{2,1,0:T(8,128)(2,1)S(1)}, bf16[2,24,256]{2,1,0:T(8,128)(2,1)S(1)}, u32[]{:S(2)}, u32[]{:S(2)}) collective-permute-start(bf16[2,24,256]{2,1,0:T(8,128)(2,1)S(1)} %select_bitcast_fusion.4), channel_id=1, source_target_pairs={{0,96},{4,100},{8,104},{12,108},{16,112},{20,116},{24,120},{28,124... | collective-permute-start | bytes 73736 | tf_op jit(solution)/shard_map/ppermute | solution.py:74
  13.1 0.3 convolution_convert_fusion
  13.4 0.9 broadcast_in_dim.27
  14.3 4.6 %all-to-all-start = ((bf16[8,9,16,256]{3,2,1,0:T(8,128)(2,1)}), bf16[8,9,16,256]{3,2,1,0:T(8,128)(2,1)S(1)}, u32[]{:S(2)}, u32[]{:S(2)}) async-start(bf16[8,9,16,256]{3,2,1,0:T(8,128)(2,1)} %broadcast_in_dim.27), calls=%async_computation | async-start | bytes 1179648 | tf_op jit(solution)/shard_map/all_to_all | solution.py:137
  18.9 1.9 %collective-permute-start = (bf16[7,24,256]{2,1,0:T(8,128)(2,1)S(1)}, bf16[7,24,256]{2,1,0:T(8,128)(2,1)S(1)}, u32[]{:S(2)}, u32[]{:S(2)}) collective-permute-start(bf16[7,24,256]{2,1,0:T(8,128)(2,1)S(1)} %bitcast.105), channel_id=1, source_target_pairs={{0,64},{64,0},{1,65},{65,1},{2,66},{66,2},{3,67},{67,3},{4,68},{68... | collective-permute-start | bytes 258056 | tf_op jit(solution)/shard_map/ppermute | solution.py:77
  20.9 4.3 %collective-permute-done = bf16[7,24,256]{2,1,0:T(8,128)(2,1)S(1)} collective-permute-done((bf16[7,24,256]{2,1,0:T(8,128)(2,1)S(1)}, bf16[7,24,256]{2,1,0:T(8,128)(2,1)S(1)}, u32[]{:S(2)}, u32[]{:S(2)}) %collective-permute-start) | collective-permute-done | bytes 86048 | tf_op jit(solution)/shard_map/ppermute | solution.py:77
  25.3 1.9 %collective-permute-start.3 = (bf16[16,24,256]{2,1,0:T(8,128)(2,1)S(1)}, bf16[16,24,256]{2,1,0:T(8,128)(2,1)S(1)}, u32[]{:S(2)}, u32[]{:S(2)}) collective-permute-start(bf16[16,24,256]{2,1,0:T(8,128)(2,1)S(1)} %pad_maximum_fusion.6), channel_id=1, source_target_pairs={{0,128},{128,0},{1,129},{129,1},{2,130},{130,2},{3,131},{131,3},{4... | collective-permute-start | bytes 589832 | tf_op jit(solution)/shard_map/ppermute | solution.py:81
  27.2 5.6 %collective-permute-done.3 = bf16[16,24,256]{2,1,0:T(8,128)(2,1)S(1)} collective-permute-done((bf16[16,24,256]{2,1,0:T(8,128)(2,1)S(1)}, bf16[16,24,256]{2,1,0:T(8,128)(2,1)S(1)}, u32[]{:S(2)}, u32[]{:S(2)}) %collective-permute-start.3) | collective-permute-done | bytes 196640 | tf_op jit(solution)/shard_map/ppermute | solution.py:81
  33.0 0.1 collective-permute-start.5
  33.1 0.4 collective-permute-start.4
  33.5 0.3 convolution_convert_fusion.1
  33.9 0.3 copy-done.4
  34.3 3.2 %all-to-all-done = bf16[8,9,16,256]{3,2,1,0:T(8,128)(2,1)S(1)} async-done(((bf16[8,9,16,256]{3,2,1,0:T(8,128)(2,1)}), bf16[8,9,16,256]{3,2,1,0:T(8,128)(2,1)S(1)}, u32[]{:S(2)}, u32[]{:S(2)}) %all-to-all-start) | async-done | bytes 589856 | tf_op jit(solution)/shard_map/all_to_all | solution.py:137
  37.5 1.9 %collective-permute-start.6 = (bf16[8,9,16,256]{3,2,1,0:T(8,128)(2,1)S(1)}, bf16[8,9,16,256]{3,2,1,0:T(8,128)(2,1)S(1)}, u32[]{:S(2)}, u32[]{:S(2)}) collective-permute-start(bf16[8,9,16,256]{3,2,1,0:T(8,128)(2,1)S(1)} %all-to-all-done), channel_id=1, source_target_pairs={{0,4},{4,0},{1,5},{5,1},{2,6},{6,2},{3,7},{7,3},{8,12},{12,8},{9,1... | collective-permute-start | bytes 1769480 | tf_op jit(solution)/shard_map/ppermute | solution.py:140
  39.4 0.4 fusion.7
  40.1 0.1 reshape.132
  40.4 0.9 collective-permute-done.6
  41.6 0.2 copy.20
  41.7 0.5 copy-done.6
  42.2 1.5 %fusion.2 = bf16[34,8,4,256]{3,1,2,0:T(8,128)(2,1)S(1)} fusion(bf16[3,3,256,256]{3,2,1,0:T(8,128)(2,1)S(1)} %bitcast.103, bf16[36,1,7,2,256]{4,2,3,0,1:T(8,128)(2,1)S(1)} %slice.206, bf16[36,1,8,4,256]{4,2,3,0,1:T(8,128)(2,1)S(1)} %copy.19, pred[8,4]{0,1:T(4,128)(4,1)S(1)} %copy-done.6), kind=kOutput, calls=%fused_computation.5 | convolution fusion | flops 1286668288 | bytes 2584608 | tf_op jit(solution)/shard_map/conv_general_dilated | solution.py:98
  43.8 0.2 copy.22
  44.5 0.1 fusion.45
  44.6 0.1 pad_slice_fusion.19
  45.2 0.9 broadcast_in_dim.24
  46.1 5.4 %collective-permute-start.9 = (bf16[392,128]{1,0:T(8,128)(2,1)S(1)}, bf16[392,128]{1,0:T(8,128)(2,1)S(1)}, u32[]{:S(2)}, u32[]{:S(2)}) collective-permute-start(bf16[392,128]{1,0:T(8,128)(2,1)S(1)} %get-tuple-element.32), channel_id=1, source_target_pairs={{0,3},{1,0},{2,1},{3,2},{4,7},{5,4},{6,5},{7,6},{8,11},{9,8},{10,9... | collective-permute-start | bytes 301064 | tf_op jit(solution)/shard_map/ppermute | solution.py:37
  51.5 4.6 %collective-permute-start.8 = (bf16[392,128]{1,0:T(8,128)(2,1)S(1)}, bf16[392,128]{1,0:T(8,128)(2,1)S(1)}, u32[]{:S(2)}, u32[]{:S(2)}) collective-permute-start(bf16[392,128]{1,0:T(8,128)(2,1)S(1)} %get-tuple-element.33), channel_id=1, source_target_pairs={{0,2},{1,3},{2,0},{3,1},{4,6},{5,7},{6,4},{7,5},{8,10},{9,11},{10,... | collective-permute-start | bytes 301064 | tf_op jit(solution)/shard_map/ppermute | solution.py:37
  56.1 3.7 %collective-permute-start.7 = (bf16[392,128]{1,0:T(8,128)(2,1)S(1)}, bf16[392,128]{1,0:T(8,128)(2,1)S(1)}, u32[]{:S(2)}, u32[]{:S(2)}) collective-permute-start(bf16[392,128]{1,0:T(8,128)(2,1)S(1)} %get-tuple-element.31), channel_id=1, source_target_pairs={{0,1},{1,2},{2,3},{3,0},{4,5},{5,6},{6,7},{7,4},{8,9},{9,10},{10,1... | collective-permute-start | bytes 301064 | tf_op jit(solution)/shard_map/ppermute | solution.py:37
  59.9 5.0 %collective-permute-done.7 = bf16[392,128]{1,0:T(8,128)(2,1)S(1)} collective-permute-done((bf16[392,128]{1,0:T(8,128)(2,1)S(1)}, bf16[392,128]{1,0:T(8,128)(2,1)S(1)}, u32[]{:S(2)}, u32[]{:S(2)}) %collective-permute-start.7) | collective-permute-done | bytes 100384 | tf_op jit(solution)/shard_map/ppermute | solution.py:37
  64.9 6.1 %all-to-all-start.1 = ((bf16[8,9,16,256]{3,2,1,0:T(8,128)(2,1)}), bf16[8,9,16,256]{3,2,1,0:T(8,128)(2,1)S(1)}, u32[]{:S(2)}, u32[]{:S(2)}) async-start(bf16[8,9,16,256]{3,2,1,0:T(8,128)(2,1)} %broadcast_in_dim.24), calls=%async_computation.1 | async-start | bytes 1179648 | tf_op jit(solution)/shard_map/all_to_all | solution.py:151
  71.2 1.9 %collective-permute-start.10 = (bf16[1,392,128]{2,1,0:T(8,128)(2,1)S(1)}, bf16[1,392,128]{2,1,0:T(8,128)(2,1)S(1)}, u32[]{:S(2)}, u32[]{:S(2)}) collective-permute-start(bf16[1,392,128]{2,1,0:T(8,128)(2,1)S(1)} %fusion.31), channel_id=1, source_target_pairs={{0,64},{64,0},{1,65},{65,1},{2,66},{66,2},{3,67},{67,3},{4,68},{68... | collective-permute-start | bytes 301064 | tf_op jit(solution)/shard_map/ppermute | solution.py:44
  73.1 4.6 %collective-permute-done.10 = bf16[1,392,128]{2,1,0:T(8,128)(2,1)S(1)} collective-permute-done((bf16[1,392,128]{2,1,0:T(8,128)(2,1)S(1)}, bf16[1,392,128]{2,1,0:T(8,128)(2,1)S(1)}, u32[]{:S(2)}, u32[]{:S(2)}) %collective-permute-start.10) | collective-permute-done | bytes 100384 | tf_op jit(solution)/shard_map/ppermute | solution.py:44
  77.8 1.9 %collective-permute-start.11 = (bf16[2,392,128]{2,1,0:T(8,128)(2,1)S(1)}, bf16[2,392,128]{2,1,0:T(8,128)(2,1)S(1)}, u32[]{:S(2)}, u32[]{:S(2)}) collective-permute-start(bf16[2,392,128]{2,1,0:T(8,128)(2,1)S(1)} %pad_maximum_fusion.5), channel_id=1, source_target_pairs={{0,128},{128,0},{1,129},{129,1},{2,130},{130,2},{3,131},{131,3},{4... | collective-permute-start | bytes 602120 | tf_op jit(solution)/shard_map/ppermute | solution.py:44
  79.7 5.7 %collective-permute-done.11 = bf16[2,392,128]{2,1,0:T(8,128)(2,1)S(1)} collective-permute-done((bf16[2,392,128]{2,1,0:T(8,128)(2,1)S(1)}, bf16[2,392,128]{2,1,0:T(8,128)(2,1)S(1)}, u32[]{:S(2)}, u32[]{:S(2)}) %collective-permute-start.11) | collective-permute-done | bytes 200736 | tf_op jit(solution)/shard_map/ppermute | solution.py:44
  85.5 4.4 %all-to-all-done.1 = bf16[8,9,16,256]{3,2,1,0:T(8,128)(2,1)S(1)} async-done(((bf16[8,9,16,256]{3,2,1,0:T(8,128)(2,1)}), bf16[8,9,16,256]{3,2,1,0:T(8,128)(2,1)S(1)}, u32[]{:S(2)}, u32[]{:S(2)}) %all-to-all-start.1) | async-done | bytes 589856 | tf_op jit(solution)/shard_map/all_to_all | solution.py:151
  89.9 1.9 %collective-permute-start.12 = (bf16[8,9,16,256]{3,2,1,0:T(8,128)(2,1)S(1)}, bf16[8,9,16,256]{3,2,1,0:T(8,128)(2,1)S(1)}, u32[]{:S(2)}, u32[]{:S(2)}) collective-permute-start(bf16[8,9,16,256]{3,2,1,0:T(8,128)(2,1)S(1)} %all-to-all-done.1), channel_id=1, source_target_pairs={{0,4},{4,0},{1,5},{5,1},{2,6},{6,2},{3,7},{7,3},{8,12},{12,8},{9,1... | collective-permute-start | bytes 1769480 | tf_op jit(solution)/shard_map/ppermute | solution.py:155
  91.8 0.2 slice.172
  92.0 0.2 fusion.23
  92.4 0.3 maximum_bitcast_fusion.3
  93.1 0.7 collective-permute-done.12
  94.0 0.2 copy.26
  94.1 0.5 copy-done.5
  94.6 1.2 %fusion.3 = bf16[28,8,4,256]{3,1,2,0:T(8,128)(2,1)S(1)} fusion(bf16[3,3,256,256]{3,2,1,0:T(8,128)(2,1)S(1)} %bitcast.104, bf16[30,1,7,2,256]{4,2,3,0,1:T(8,128)(2,1)S(1)} %slice.224, bf16[30,1,8,4,256]{4,2,3,0,1:T(8,128)(2,1)S(1)} %copy.25, pred[8,4]{0,1:T(4,128)(4,1)S(1)} %copy-done.5), kind=kOutput, calls=%fused_computation.9 | convolution fusion | flops 1059635200 | bytes 2344992 | tf_op jit(solution)/shard_map/conv_general_dilated | solution.py:98
  95.9 0.2 copy.27
  96.3 0.1 fusion.46
  97.0 18.3 %all_to_all.15 = bf16[16,88,128]{2,1,0:T(8,128)(2,1)S(1)} all-to-all(bf16[16,88,128]{2,1,0:T(8,128)(2,1)S(1)} %bitcast.101), channel_id=1, replica_groups=mesh['xh'=2,'xl'=2,'ylo'=2,'z'=8,'core'=2,'ch'=4] {'ch','xl','ylo'}, dimensions={0} | all-to-all | bytes 720896 | tf_op jit(solution)/shard_map/all_to_all | solution.py:161
  115.5 0.8 fusion.30
  (85 shorter events, 3.8 us)
Async XLA Ops:
  0.0 13.1 %copy-start = (bf16[3,3,1,16,1024]{4,3,2,1,0:T(8,128)(2,1)S(1)}, bf16[3,3,1,16,1024]{4,3,2,1,0:T(8,128)(2,1)}, u32[]{:S(2)}) copy-start(bf16[3,3,1,16,1024]{4,3,2,1,0:T(8,128)(2,1)} %param.6) | copy-start | bytes 884740
  0.8 20.0 %collective-permute-start.1 = (bf16[2,24,256]{2,1,0:T(8,128)(2,1)S(1)}, bf16[2,24,256]{2,1,0:T(8,128)(2,1)S(1)}, u32[]{:S(2)}, u32[]{:S(2)}) collective-permute-start(bf16[2,24,256]{2,1,0:T(8,128)(2,1)S(1)} %select_bitcast_fusion.4), channel_id=1, source_target_pairs={{0,32},{4,36},{8,40},{12,44},{16,48},{20,52},{24,56},{28,60},{32,0... | collective-permute-start | bytes 73736 | tf_op jit(solution)/shard_map/ppermute | solution.py:74
  11.7 9.1 %collective-permute-start.2 = (bf16[2,24,256]{2,1,0:T(8,128)(2,1)S(1)}, bf16[2,24,256]{2,1,0:T(8,128)(2,1)S(1)}, u32[]{:S(2)}, u32[]{:S(2)}) collective-permute-start(bf16[2,24,256]{2,1,0:T(8,128)(2,1)S(1)} %select_bitcast_fusion.4), channel_id=1, source_target_pairs={{0,96},{4,100},{8,104},{12,108},{16,112},{20,116},{24,120},{28,124... | collective-permute-start | bytes 73736 | tf_op jit(solution)/shard_map/ppermute | solution.py:74
  13.4 5.4 %copy-start.1 = (bf16[1,7,24,256]{3,2,1,0:T(8,128)(2,1)S(1)}, bf16[1,7,24,256]{3,2,1,0:T(8,128)(2,1)}, u32[]{:S(2)}) copy-start(bf16[1,7,24,256]{3,2,1,0:T(8,128)(2,1)} %param.5) | copy-start | bytes 258052
  14.3 23.2 %all-to-all-start = ((bf16[8,9,16,256]{3,2,1,0:T(8,128)(2,1)}), bf16[8,9,16,256]{3,2,1,0:T(8,128)(2,1)S(1)}, u32[]{:S(2)}, u32[]{:S(2)}) async-start(bf16[8,9,16,256]{3,2,1,0:T(8,128)(2,1)} %broadcast_in_dim.27), calls=%async_computation | async-start | bytes 1179648 | tf_op jit(solution)/shard_map/all_to_all | solution.py:137
  18.9 6.4 %collective-permute-start = (bf16[7,24,256]{2,1,0:T(8,128)(2,1)S(1)}, bf16[7,24,256]{2,1,0:T(8,128)(2,1)S(1)}, u32[]{:S(2)}, u32[]{:S(2)}) collective-permute-start(bf16[7,24,256]{2,1,0:T(8,128)(2,1)S(1)} %bitcast.105), channel_id=1, source_target_pairs={{0,64},{64,0},{1,65},{65,1},{2,66},{66,2},{3,67},{67,3},{4,68},{68... | collective-permute-start | bytes 258056 | tf_op jit(solution)/shard_map/ppermute | solution.py:77
  20.9 12.7 %copy-start.3 = (bf16[3,3,1,16,1024]{4,3,2,1,0:T(8,128)(2,1)S(1)}, bf16[3,3,1,16,1024]{4,3,2,1,0:T(8,128)(2,1)}, u32[]{:S(2)}) copy-start(bf16[3,3,1,16,1024]{4,3,2,1,0:T(8,128)(2,1)} %param.8) | copy-start | bytes 884740
  25.3 7.6 %collective-permute-start.3 = (bf16[16,24,256]{2,1,0:T(8,128)(2,1)S(1)}, bf16[16,24,256]{2,1,0:T(8,128)(2,1)S(1)}, u32[]{:S(2)}, u32[]{:S(2)}) collective-permute-start(bf16[16,24,256]{2,1,0:T(8,128)(2,1)S(1)} %pad_maximum_fusion.6), channel_id=1, source_target_pairs={{0,128},{128,0},{1,129},{129,1},{2,130},{130,2},{3,131},{131,3},{4... | collective-permute-start | bytes 589832 | tf_op jit(solution)/shard_map/ppermute | solution.py:81
  33.0 6.4 %collective-permute-start.5 = (bf16[32,2,256]{2,1,0:T(2,128)(2,1)S(1)}, bf16[32,2,256]{2,1,0:T(2,128)(2,1)S(1)}, u32[]{:S(2)}, u32[]{:S(2)}) collective-permute-start(bf16[32,2,256]{2,1,0:T(2,128)(2,1)S(1)} %get-tuple-element.39), channel_id=1, source_target_pairs={{4,0},{8,4},{12,8},{16,12},{20,16},{24,20},{28,24},{32,28},{36,32}... | collective-permute-start | bytes 98312 | tf_op jit(solution)/shard_map/ppermute | solution.py:55
  33.1 6.3 %collective-permute-start.4 = (bf16[32,2,256]{2,1,0:T(2,128)(2,1)S(1)}, bf16[32,2,256]{2,1,0:T(2,128)(2,1)S(1)}, u32[]{:S(2)}, u32[]{:S(2)}) collective-permute-start(bf16[32,2,256]{2,1,0:T(2,128)(2,1)S(1)} %get-tuple-element.38), channel_id=1, source_target_pairs={{0,4},{4,8},{8,12},{12,16},{16,20},{20,24},{24,28},{28,32},{32,36}... | collective-permute-start | bytes 98312 | tf_op jit(solution)/shard_map/ppermute | solution.py:54
  33.5 0.7 copy-start.4
  37.5 3.9 %collective-permute-start.6 = (bf16[8,9,16,256]{3,2,1,0:T(8,128)(2,1)S(1)}, bf16[8,9,16,256]{3,2,1,0:T(8,128)(2,1)S(1)}, u32[]{:S(2)}, u32[]{:S(2)}) collective-permute-start(bf16[8,9,16,256]{3,2,1,0:T(8,128)(2,1)S(1)} %all-to-all-done), channel_id=1, source_target_pairs={{0,4},{4,0},{1,5},{5,1},{2,6},{6,2},{3,7},{7,3},{8,12},{12,8},{9,1... | collective-permute-start | bytes 1769480 | tf_op jit(solution)/shard_map/ppermute | solution.py:140
  41.6 0.7 copy-start.6
  46.1 24.9 %collective-permute-start.9 = (bf16[392,128]{1,0:T(8,128)(2,1)S(1)}, bf16[392,128]{1,0:T(8,128)(2,1)S(1)}, u32[]{:S(2)}, u32[]{:S(2)}) collective-permute-start(bf16[392,128]{1,0:T(8,128)(2,1)S(1)} %get-tuple-element.32), channel_id=1, source_target_pairs={{0,3},{1,0},{2,1},{3,2},{4,7},{5,4},{6,5},{7,6},{8,11},{9,8},{10,9... | collective-permute-start | bytes 301064 | tf_op jit(solution)/shard_map/ppermute | solution.py:37
  51.5 19.5 %collective-permute-start.8 = (bf16[392,128]{1,0:T(8,128)(2,1)S(1)}, bf16[392,128]{1,0:T(8,128)(2,1)S(1)}, u32[]{:S(2)}, u32[]{:S(2)}) collective-permute-start(bf16[392,128]{1,0:T(8,128)(2,1)S(1)} %get-tuple-element.33), channel_id=1, source_target_pairs={{0,2},{1,3},{2,0},{3,1},{4,6},{5,7},{6,4},{7,5},{8,10},{9,11},{10,... | collective-permute-start | bytes 301064 | tf_op jit(solution)/shard_map/ppermute | solution.py:37
  56.1 8.9 %collective-permute-start.7 = (bf16[392,128]{1,0:T(8,128)(2,1)S(1)}, bf16[392,128]{1,0:T(8,128)(2,1)S(1)}, u32[]{:S(2)}, u32[]{:S(2)}) collective-permute-start(bf16[392,128]{1,0:T(8,128)(2,1)S(1)} %get-tuple-element.31), channel_id=1, source_target_pairs={{0,1},{1,2},{2,3},{3,0},{4,5},{5,6},{6,7},{7,4},{8,9},{9,10},{10,1... | collective-permute-start | bytes 301064 | tf_op jit(solution)/shard_map/ppermute | solution.py:37
  64.9 24.9 %all-to-all-start.1 = ((bf16[8,9,16,256]{3,2,1,0:T(8,128)(2,1)}), bf16[8,9,16,256]{3,2,1,0:T(8,128)(2,1)S(1)}, u32[]{:S(2)}, u32[]{:S(2)}) async-start(bf16[8,9,16,256]{3,2,1,0:T(8,128)(2,1)} %broadcast_in_dim.24), calls=%async_computation.1 | async-start | bytes 1179648 | tf_op jit(solution)/shard_map/all_to_all | solution.py:151
  71.2 6.5 %collective-permute-start.10 = (bf16[1,392,128]{2,1,0:T(8,128)(2,1)S(1)}, bf16[1,392,128]{2,1,0:T(8,128)(2,1)S(1)}, u32[]{:S(2)}, u32[]{:S(2)}) collective-permute-start(bf16[1,392,128]{2,1,0:T(8,128)(2,1)S(1)} %fusion.31), channel_id=1, source_target_pairs={{0,64},{64,0},{1,65},{65,1},{2,66},{66,2},{3,67},{67,3},{4,68},{68... | collective-permute-start | bytes 301064 | tf_op jit(solution)/shard_map/ppermute | solution.py:44
  77.8 7.6 %collective-permute-start.11 = (bf16[2,392,128]{2,1,0:T(8,128)(2,1)S(1)}, bf16[2,392,128]{2,1,0:T(8,128)(2,1)S(1)}, u32[]{:S(2)}, u32[]{:S(2)}) collective-permute-start(bf16[2,392,128]{2,1,0:T(8,128)(2,1)S(1)} %pad_maximum_fusion.5), channel_id=1, source_target_pairs={{0,128},{128,0},{1,129},{129,1},{2,130},{130,2},{3,131},{131,3},{4... | collective-permute-start | bytes 602120 | tf_op jit(solution)/shard_map/ppermute | solution.py:44
  89.9 3.9 %collective-permute-start.12 = (bf16[8,9,16,256]{3,2,1,0:T(8,128)(2,1)S(1)}, bf16[8,9,16,256]{3,2,1,0:T(8,128)(2,1)S(1)}, u32[]{:S(2)}, u32[]{:S(2)}) collective-permute-start(bf16[8,9,16,256]{3,2,1,0:T(8,128)(2,1)S(1)} %all-to-all-done.1), channel_id=1, source_target_pairs={{0,4},{4,0},{1,5},{5,1},{2,6},{6,2},{3,7},{7,3},{8,12},{12,8},{9,1... | collective-permute-start | bytes 1769480 | tf_op jit(solution)/shard_map/ppermute | solution.py:155
  94.0 0.7 copy-start.5
  97.0 18.5 %copy-start.2 = (f32[256]{0:T(256)S(1)}, f32[256]{0:T(256)}, u32[]{:S(2)}) copy-start(f32[256]{0:T(256)} %param.9) | copy-start | bytes 3076

commit v10 on v9

--- a/solution.py
+++ b/solution.py
@@ -31,10 +31,10 @@
 
 def traded(blocks, axis):
     me, count = lax.axis_index(axis), blocks.shape[0]
-    came = [lax.dynamic_index_in_dim(blocks, me, 0, keepdims=False)]
-    for d in range(1, count):
+    came = {0: lax.dynamic_index_in_dim(blocks, me, 0, keepdims=False)}
+    for d in (1, 3, 2):
         sent = lax.dynamic_index_in_dim(blocks, lax.rem(me + d, count), 0, keepdims=False)
-        came.append(lax.ppermute(sent, axis, [(i, (i + d) % count) for i in range(count)]))
+        came[d] = lax.ppermute(sent, axis, [(i, (i + d) % count) for i in range(count)])
     return came
 
 
@@ -147,10 +147,10 @@
     block = copies_of(quarter(kernel_two, member, groups))
     block, partial = lax.optimization_barrier((block, partial))
     came = traded(partial, "ch")
-    block, came[1] = lax.optimization_barrier((block, came[1]))
+    block, came[2] = lax.optimization_barrier((block, came[2]))
     mine = lax.all_to_all(block, "z", 0, 0)
     bias = lax.dynamic_slice_in_dim(bias_one, member * SLICE, SLICE, 0)
-    hidden = sum(part.astype(jnp.float32) for part in came) + jnp.concatenate([bias, bias])
+    hidden = sum(part.astype(jnp.float32) for part in came.values()) + jnp.concatenate([bias, bias])
     acts, mine = lax.optimization_barrier((from_quad(silu(hidden), member), mine))
     other = lax.ppermute(mine, "core", SWAP)
     acts = unfolded(acts, count)

time: 117 us -> 111 us (0.949)
  waiting for transfers between devices: 34.5 us -> 29.8 us
  starting transfers between devices: 48.6 us -> 46 us
    ppermute x3, waiting for transfers between devices: 5.04 us -> 1.63 us  [traded(): lax.ppermute(sent, axis, [(i, (i + d) % count) for i in range(count)])]
    all_to_all x2, starting transfers between devices: 10.7 us -> 8.11 us  [body(): mine = lax.all_to_all(block, 'z', 0, 0)]
    all_to_all x2, waiting for transfers between devices: 7.59 us -> 6.3 us  [body(): mine = lax.all_to_all(block, 'z', 0, 0)]
  transfers between devices with their start and end apart: 15 -> 15, of which waited for: 9 -> 10; matrix products, arithmetic and copies ran while one was open for 4% -> 4% of each run, Pallas kernels for 0% -> 0%
where the time goes in v10:
time: 111 us; the launch traced here: 110 us
  starting transfers between devices  46 us (41%)
  waiting for transfers between devices  29.8 us (27%)
  blocking collectives  19.2 us (17%)
  local copies, waits for them, and re-layouts  6.14 us (6%)
  other arithmetic  4.58 us (4%)
  matrix products  3.4 us (3%)
    all_to_all x1, blocking collectives, body(): lax.all_to_all(partial.reshape(4 * groups, -1, LANES), ('ch',) + QUAD, 0, 0)  19.2 us
    ppermute x3, starting transfers between devices, traded(): lax.ppermute(sent, axis, [(i, (i + d) % count) for i in range(count)])  13.7 us
    ppermute x2, starting transfers between devices, region(): lax.ppermute(sent, LAT + LON, edge_pairs(8, lon, f))  12.2 us
    ppermute x2, waiting for transfers between devices, from_quad(): other = lax.ppermute(blocks, axis, SWAP)  10.3 us
    all_to_all x2, starting transfers between devices, body(): mine = lax.all_to_all(block, 'z', 0, 0)  8.11 us
    all_to_all x2, waiting for transfers between devices, body(): mine = lax.all_to_all(block, 'z', 0, 0)  6.3 us
    ppermute x1, waiting for transfers between devices, region(): other = lax.ppermute(both, 'xl', SWAP)  5.64 us
    ppermute x1, waiting for transfers between devices, region(): other = lax.ppermute(block, 'ylo', SWAP)  4.35 us
  transfers between devices with their start and end apart: 15, of which 10 were waited for; matrix products, arithmetic and copies ran while one was open for 4% of the time, Pallas kernels for 0%

profile of v10, /device:TPU:14, one launch (start us, length us, event | category | flops | bytes accessed | tf_op | source)
XLA Modules:
  0.0 109.9 jit_solution(5693138007008927490)
XLA Ops:
  0.0 0.8 select_bitcast_fusion.4
  0.8 10.9 %collective-permute-start.1 = (bf16[2,24,256]{2,1,0:T(8,128)(2,1)S(1)}, bf16[2,24,256]{2,1,0:T(8,128)(2,1)S(1)}, u32[]{:S(2)}, u32[]{:S(2)}) collective-permute-start(bf16[2,24,256]{2,1,0:T(8,128)(2,1)S(1)} %select_bitcast_fusion.4), channel_id=1, source_target_pairs={{0,32},{4,36},{8,40},{12,44},{16,48},{20,52},{24,56},{28,60},{32,0... | collective-permute-start | bytes 73736 | tf_op jit(solution)/shard_map/ppermute | solution.py:74
  11.7 1.3 %collective-permute-start.2 = (bf16[2,24,256]{2,1,0:T(8,128)(2,1)S(1)}, bf16[2,24,256]{2,1,0:T(8,128)(2,1)S(1)}, u32[]{:S(2)}, u32[]{:S(2)}) collective-permute-start(bf16[2,24,256]{2,1,0:T(8,128)(2,1)S(1)} %select_bitcast_fusion.4), channel_id=1, source_target_pairs={{0,96},{4,100},{8,104},{12,108},{16,112},{20,116},{24,120},{28,124... | collective-permute-start | bytes 73736 | tf_op jit(solution)/shard_map/ppermute | solution.py:74
  13.1 0.3 convolution_convert_fusion
  13.4 0.9 broadcast_in_dim.27
  14.3 4.6 %all-to-all-start = ((bf16[8,9,16,256]{3,2,1,0:T(8,128)(2,1)}), bf16[8,9,16,256]{3,2,1,0:T(8,128)(2,1)S(1)}, u32[]{:S(2)}, u32[]{:S(2)}) async-start(bf16[8,9,16,256]{3,2,1,0:T(8,128)(2,1)} %broadcast_in_dim.27), calls=%async_computation | async-start | bytes 1179648 | tf_op jit(solution)/shard_map/all_to_all | solution.py:137
  18.9 1.9 %collective-permute-start = (bf16[7,24,256]{2,1,0:T(8,128)(2,1)S(1)}, bf16[7,24,256]{2,1,0:T(8,128)(2,1)S(1)}, u32[]{:S(2)}, u32[]{:S(2)}) collective-permute-start(bf16[7,24,256]{2,1,0:T(8,128)(2,1)S(1)} %bitcast.105), channel_id=1, source_target_pairs={{0,64},{64,0},{1,65},{65,1},{2,66},{66,2},{3,67},{67,3},{4,68},{68... | collective-permute-start | bytes 258056 | tf_op jit(solution)/shard_map/ppermute | solution.py:77
  20.9 4.3 %collective-permute-done = bf16[7,24,256]{2,1,0:T(8,128)(2,1)S(1)} collective-permute-done((bf16[7,24,256]{2,1,0:T(8,128)(2,1)S(1)}, bf16[7,24,256]{2,1,0:T(8,128)(2,1)S(1)}, u32[]{:S(2)}, u32[]{:S(2)}) %collective-permute-start) | collective-permute-done | bytes 86048 | tf_op jit(solution)/shard_map/ppermute | solution.py:77
  25.3 1.9 %collective-permute-start.3 = (bf16[16,24,256]{2,1,0:T(8,128)(2,1)S(1)}, bf16[16,24,256]{2,1,0:T(8,128)(2,1)S(1)}, u32[]{:S(2)}, u32[]{:S(2)}) collective-permute-start(bf16[16,24,256]{2,1,0:T(8,128)(2,1)S(1)} %pad_maximum_fusion.6), channel_id=1, source_target_pairs={{0,128},{128,0},{1,129},{129,1},{2,130},{130,2},{3,131},{131,3},{4... | collective-permute-start | bytes 589832 | tf_op jit(solution)/shard_map/ppermute | solution.py:81
  27.2 5.6 %collective-permute-done.3 = bf16[16,24,256]{2,1,0:T(8,128)(2,1)S(1)} collective-permute-done((bf16[16,24,256]{2,1,0:T(8,128)(2,1)S(1)}, bf16[16,24,256]{2,1,0:T(8,128)(2,1)S(1)}, u32[]{:S(2)}, u32[]{:S(2)}) %collective-permute-start.3) | collective-permute-done | bytes 196640 | tf_op jit(solution)/shard_map/ppermute | solution.py:81
  33.0 0.1 collective-permute-start.5
  33.1 0.4 collective-permute-start.4
  33.5 0.3 convolution_convert_fusion.1
  33.9 0.3 copy-done.4
  34.3 3.2 %all-to-all-done = bf16[8,9,16,256]{3,2,1,0:T(8,128)(2,1)S(1)} async-done(((bf16[8,9,16,256]{3,2,1,0:T(8,128)(2,1)}), bf16[8,9,16,256]{3,2,1,0:T(8,128)(2,1)S(1)}, u32[]{:S(2)}, u32[]{:S(2)}) %all-to-all-start) | async-done | bytes 589856 | tf_op jit(solution)/shard_map/all_to_all | solution.py:137
  37.5 1.9 %collective-permute-start.6 = (bf16[8,9,16,256]{3,2,1,0:T(8,128)(2,1)S(1)}, bf16[8,9,16,256]{3,2,1,0:T(8,128)(2,1)S(1)}, u32[]{:S(2)}, u32[]{:S(2)}) collective-permute-start(bf16[8,9,16,256]{3,2,1,0:T(8,128)(2,1)S(1)} %all-to-all-done), channel_id=1, source_target_pairs={{0,4},{4,0},{1,5},{5,1},{2,6},{6,2},{3,7},{7,3},{8,12},{12,8},{9,1... | collective-permute-start | bytes 1769480 | tf_op jit(solution)/shard_map/ppermute | solution.py:140
  39.4 0.4 fusion.7
  40.1 0.1 reshape.132
  40.4 0.9 collective-permute-done.6
  41.6 0.2 copy.20
  41.7 0.5 copy-done.6
  42.2 1.5 %fusion.2 = bf16[34,8,4,256]{3,1,2,0:T(8,128)(2,1)S(1)} fusion(bf16[3,3,256,256]{3,2,1,0:T(8,128)(2,1)S(1)} %bitcast.103, bf16[36,1,7,2,256]{4,2,3,0,1:T(8,128)(2,1)S(1)} %slice.206, bf16[36,1,8,4,256]{4,2,3,0,1:T(8,128)(2,1)S(1)} %copy.19, pred[8,4]{0,1:T(4,128)(4,1)S(1)} %copy-done.6), kind=kOutput, calls=%fused_computation.5 | convolution fusion | flops 1286668288 | bytes 2584608 | tf_op jit(solution)/shard_map/conv_general_dilated | solution.py:98
  43.8 0.2 copy.22
  44.5 0.1 fusion.45
  44.6 0.1 pad_slice_fusion.19
  45.2 0.9 broadcast_in_dim.24
  46.1 7.0 %collective-permute-start.9 = (bf16[392,128]{1,0:T(8,128)(2,1)S(1)}, bf16[392,128]{1,0:T(8,128)(2,1)S(1)}, u32[]{:S(2)}, u32[]{:S(2)}) collective-permute-start(bf16[392,128]{1,0:T(8,128)(2,1)S(1)} %get-tuple-element.32), channel_id=1, source_target_pairs={{0,2},{1,3},{2,0},{3,1},{4,6},{5,7},{6,4},{7,5},{8,10},{9,11},{10,... | collective-permute-start | bytes 301064 | tf_op jit(solution)/shard_map/ppermute | solution.py:37
  53.1 3.0 %collective-permute-start.8 = (bf16[392,128]{1,0:T(8,128)(2,1)S(1)}, bf16[392,128]{1,0:T(8,128)(2,1)S(1)}, u32[]{:S(2)}, u32[]{:S(2)}) collective-permute-start(bf16[392,128]{1,0:T(8,128)(2,1)S(1)} %get-tuple-element.33), channel_id=1, source_target_pairs={{0,3},{1,0},{2,1},{3,2},{4,7},{5,4},{6,5},{7,6},{8,11},{9,8},{10,9... | collective-permute-start | bytes 301064 | tf_op jit(solution)/shard_map/ppermute | solution.py:37
  56.1 3.8 %collective-permute-start.7 = (bf16[392,128]{1,0:T(8,128)(2,1)S(1)}, bf16[392,128]{1,0:T(8,128)(2,1)S(1)}, u32[]{:S(2)}, u32[]{:S(2)}) collective-permute-start(bf16[392,128]{1,0:T(8,128)(2,1)S(1)} %get-tuple-element.31), channel_id=1, source_target_pairs={{0,1},{1,2},{2,3},{3,0},{4,5},{5,6},{6,7},{7,4},{8,9},{9,10},{10,1... | collective-permute-start | bytes 301064 | tf_op jit(solution)/shard_map/ppermute | solution.py:37
  59.9 1.5 %collective-permute-done.9 = bf16[392,128]{1,0:T(8,128)(2,1)S(1)} collective-permute-done((bf16[392,128]{1,0:T(8,128)(2,1)S(1)}, bf16[392,128]{1,0:T(8,128)(2,1)S(1)}, u32[]{:S(2)}, u32[]{:S(2)}) %collective-permute-start.9) | collective-permute-done | bytes 100384 | tf_op jit(solution)/shard_map/ppermute | solution.py:37
  61.4 3.5 %all-to-all-start.1 = ((bf16[8,9,16,256]{3,2,1,0:T(8,128)(2,1)}), bf16[8,9,16,256]{3,2,1,0:T(8,128)(2,1)S(1)}, u32[]{:S(2)}, u32[]{:S(2)}) async-start(bf16[8,9,16,256]{3,2,1,0:T(8,128)(2,1)} %broadcast_in_dim.24), calls=%async_computation.1 | async-start | bytes 1179648 | tf_op jit(solution)/shard_map/all_to_all | solution.py:151
  65.0 0.1 collective-permute-done.7
  65.2 1.9 %collective-permute-start.10 = (bf16[1,392,128]{2,1,0:T(8,128)(2,1)S(1)}, bf16[1,392,128]{2,1,0:T(8,128)(2,1)S(1)}, u32[]{:S(2)}, u32[]{:S(2)}) collective-permute-start(bf16[1,392,128]{2,1,0:T(8,128)(2,1)S(1)} %fusion.31), channel_id=1, source_target_pairs={{0,64},{64,0},{1,65},{65,1},{2,66},{66,2},{3,67},{67,3},{4,68},{68... | collective-permute-start | bytes 301064 | tf_op jit(solution)/shard_map/ppermute | solution.py:44
  67.1 4.6 %collective-permute-done.10 = bf16[1,392,128]{2,1,0:T(8,128)(2,1)S(1)} collective-permute-done((bf16[1,392,128]{2,1,0:T(8,128)(2,1)S(1)}, bf16[1,392,128]{2,1,0:T(8,128)(2,1)S(1)}, u32[]{:S(2)}, u32[]{:S(2)}) %collective-permute-start.10) | collective-permute-done | bytes 100384 | tf_op jit(solution)/shard_map/ppermute | solution.py:44
  71.8 1.9 %collective-permute-start.11 = (bf16[2,392,128]{2,1,0:T(8,128)(2,1)S(1)}, bf16[2,392,128]{2,1,0:T(8,128)(2,1)S(1)}, u32[]{:S(2)}, u32[]{:S(2)}) collective-permute-start(bf16[2,392,128]{2,1,0:T(8,128)(2,1)S(1)} %pad_maximum_fusion.5), channel_id=1, source_target_pairs={{0,128},{128,0},{1,129},{129,1},{2,130},{130,2},{3,131},{131,3},{4... | collective-permute-start | bytes 602120 | tf_op jit(solution)/shard_map/ppermute | solution.py:44
  73.7 5.7 %collective-permute-done.11 = bf16[2,392,128]{2,1,0:T(8,128)(2,1)S(1)} collective-permute-done((bf16[2,392,128]{2,1,0:T(8,128)(2,1)S(1)}, bf16[2,392,128]{2,1,0:T(8,128)(2,1)S(1)}, u32[]{:S(2)}, u32[]{:S(2)}) %collective-permute-start.11) | collective-permute-done | bytes 200736 | tf_op jit(solution)/shard_map/ppermute | solution.py:44
  79.5 3.1 %all-to-all-done.1 = bf16[8,9,16,256]{3,2,1,0:T(8,128)(2,1)S(1)} async-done(((bf16[8,9,16,256]{3,2,1,0:T(8,128)(2,1)}), bf16[8,9,16,256]{3,2,1,0:T(8,128)(2,1)S(1)}, u32[]{:S(2)}, u32[]{:S(2)}) %all-to-all-start.1) | async-done | bytes 589856 | tf_op jit(solution)/shard_map/all_to_all | solution.py:151
  82.6 1.9 %collective-permute-start.12 = (bf16[8,9,16,256]{3,2,1,0:T(8,128)(2,1)S(1)}, bf16[8,9,16,256]{3,2,1,0:T(8,128)(2,1)S(1)}, u32[]{:S(2)}, u32[]{:S(2)}) collective-permute-start(bf16[8,9,16,256]{3,2,1,0:T(8,128)(2,1)S(1)} %all-to-all-done.1), channel_id=1, source_target_pairs={{0,4},{4,0},{1,5},{5,1},{2,6},{6,2},{3,7},{7,3},{8,12},{12,8},{9,1... | collective-permute-start | bytes 1769480 | tf_op jit(solution)/shard_map/ppermute | solution.py:155
  84.5 0.2 slice.172
  84.7 0.2 fusion.23
  85.2 0.3 maximum_bitcast_fusion.3
  85.8 0.7 collective-permute-done.12
  86.7 0.2 copy.26
  86.9 0.5 copy-done.5
  87.4 1.2 %fusion.3 = bf16[28,8,4,256]{3,1,2,0:T(8,128)(2,1)S(1)} fusion(bf16[3,3,256,256]{3,2,1,0:T(8,128)(2,1)S(1)} %bitcast.104, bf16[30,1,7,2,256]{4,2,3,0,1:T(8,128)(2,1)S(1)} %slice.224, bf16[30,1,8,4,256]{4,2,3,0,1:T(8,128)(2,1)S(1)} %copy.25, pred[8,4]{0,1:T(4,128)(4,1)S(1)} %copy-done.5), kind=kOutput, calls=%fused_computation.9 | convolution fusion | flops 1059635200 | bytes 2344992 | tf_op jit(solution)/shard_map/conv_general_dilated | solution.py:98
  88.6 0.2 copy.27
  89.7 19.2 %all_to_all.15 = bf16[16,88,128]{2,1,0:T(8,128)(2,1)S(1)} all-to-all(bf16[16,88,128]{2,1,0:T(8,128)(2,1)S(1)} %bitcast.101), channel_id=1, replica_groups=mesh['xh'=2,'xl'=2,'ylo'=2,'z'=8,'core'=2,'ch'=4] {'ch','xl','ylo'}, dimensions={0} | all-to-all | bytes 720896 | tf_op jit(solution)/shard_map/all_to_all | solution.py:161
  109.2 0.8 fusion.30
  (85 shorter events, 3.9 us)
Async XLA Ops:
  0.0 13.1 %copy-start = (bf16[3,3,1,16,1024]{4,3,2,1,0:T(8,128)(2,1)S(1)}, bf16[3,3,1,16,1024]{4,3,2,1,0:T(8,128)(2,1)}, u32[]{:S(2)}) copy-start(bf16[3,3,1,16,1024]{4,3,2,1,0:T(8,128)(2,1)} %param.6) | copy-start | bytes 884740
  0.8 20.0 %collective-permute-start.1 = (bf16[2,24,256]{2,1,0:T(8,128)(2,1)S(1)}, bf16[2,24,256]{2,1,0:T(8,128)(2,1)S(1)}, u32[]{:S(2)}, u32[]{:S(2)}) collective-permute-start(bf16[2,24,256]{2,1,0:T(8,128)(2,1)S(1)} %select_bitcast_fusion.4), channel_id=1, source_target_pairs={{0,32},{4,36},{8,40},{12,44},{16,48},{20,52},{24,56},{28,60},{32,0... | collective-permute-start | bytes 73736 | tf_op jit(solution)/shard_map/ppermute | solution.py:74
  11.7 9.1 %collective-permute-start.2 = (bf16[2,24,256]{2,1,0:T(8,128)(2,1)S(1)}, bf16[2,24,256]{2,1,0:T(8,128)(2,1)S(1)}, u32[]{:S(2)}, u32[]{:S(2)}) collective-permute-start(bf16[2,24,256]{2,1,0:T(8,128)(2,1)S(1)} %select_bitcast_fusion.4), channel_id=1, source_target_pairs={{0,96},{4,100},{8,104},{12,108},{16,112},{20,116},{24,120},{28,124... | collective-permute-start | bytes 73736 | tf_op jit(solution)/shard_map/ppermute | solution.py:74
  13.4 5.4 %copy-start.1 = (bf16[1,7,24,256]{3,2,1,0:T(8,128)(2,1)S(1)}, bf16[1,7,24,256]{3,2,1,0:T(8,128)(2,1)}, u32[]{:S(2)}) copy-start(bf16[1,7,24,256]{3,2,1,0:T(8,128)(2,1)} %param.5) | copy-start | bytes 258052
  14.3 23.2 %all-to-all-start = ((bf16[8,9,16,256]{3,2,1,0:T(8,128)(2,1)}), bf16[8,9,16,256]{3,2,1,0:T(8,128)(2,1)S(1)}, u32[]{:S(2)}, u32[]{:S(2)}) async-start(bf16[8,9,16,256]{3,2,1,0:T(8,128)(2,1)} %broadcast_in_dim.27), calls=%async_computation | async-start | bytes 1179648 | tf_op jit(solution)/shard_map/all_to_all | solution.py:137
  18.9 6.4 %collective-permute-start = (bf16[7,24,256]{2,1,0:T(8,128)(2,1)S(1)}, bf16[7,24,256]{2,1,0:T(8,128)(2,1)S(1)}, u32[]{:S(2)}, u32[]{:S(2)}) collective-permute-start(bf16[7,24,256]{2,1,0:T(8,128)(2,1)S(1)} %bitcast.105), channel_id=1, source_target_pairs={{0,64},{64,0},{1,65},{65,1},{2,66},{66,2},{3,67},{67,3},{4,68},{68... | collective-permute-start | bytes 258056 | tf_op jit(solution)/shard_map/ppermute | solution.py:77
  20.9 12.7 %copy-start.3 = (bf16[3,3,1,16,1024]{4,3,2,1,0:T(8,128)(2,1)S(1)}, bf16[3,3,1,16,1024]{4,3,2,1,0:T(8,128)(2,1)}, u32[]{:S(2)}) copy-start(bf16[3,3,1,16,1024]{4,3,2,1,0:T(8,128)(2,1)} %param.8) | copy-start | bytes 884740
  25.3 7.6 %collective-permute-start.3 = (bf16[16,24,256]{2,1,0:T(8,128)(2,1)S(1)}, bf16[16,24,256]{2,1,0:T(8,128)(2,1)S(1)}, u32[]{:S(2)}, u32[]{:S(2)}) collective-permute-start(bf16[16,24,256]{2,1,0:T(8,128)(2,1)S(1)} %pad_maximum_fusion.6), channel_id=1, source_target_pairs={{0,128},{128,0},{1,129},{129,1},{2,130},{130,2},{3,131},{131,3},{4... | collective-permute-start | bytes 589832 | tf_op jit(solution)/shard_map/ppermute | solution.py:81
  33.0 6.4 %collective-permute-start.5 = (bf16[32,2,256]{2,1,0:T(2,128)(2,1)S(1)}, bf16[32,2,256]{2,1,0:T(2,128)(2,1)S(1)}, u32[]{:S(2)}, u32[]{:S(2)}) collective-permute-start(bf16[32,2,256]{2,1,0:T(2,128)(2,1)S(1)} %get-tuple-element.39), channel_id=1, source_target_pairs={{4,0},{8,4},{12,8},{16,12},{20,16},{24,20},{28,24},{32,28},{36,32}... | collective-permute-start | bytes 98312 | tf_op jit(solution)/shard_map/ppermute | solution.py:55
  33.1 6.3 %collective-permute-start.4 = (bf16[32,2,256]{2,1,0:T(2,128)(2,1)S(1)}, bf16[32,2,256]{2,1,0:T(2,128)(2,1)S(1)}, u32[]{:S(2)}, u32[]{:S(2)}) collective-permute-start(bf16[32,2,256]{2,1,0:T(2,128)(2,1)S(1)} %get-tuple-element.38), channel_id=1, source_target_pairs={{0,4},{4,8},{8,12},{12,16},{16,20},{20,24},{24,28},{28,32},{32,36}... | collective-permute-start | bytes 98312 | tf_op jit(solution)/shard_map/ppermute | solution.py:54
  33.5 0.7 copy-start.4
  37.5 3.9 %collective-permute-start.6 = (bf16[8,9,16,256]{3,2,1,0:T(8,128)(2,1)S(1)}, bf16[8,9,16,256]{3,2,1,0:T(8,128)(2,1)S(1)}, u32[]{:S(2)}, u32[]{:S(2)}) collective-permute-start(bf16[8,9,16,256]{3,2,1,0:T(8,128)(2,1)S(1)} %all-to-all-done), channel_id=1, source_target_pairs={{0,4},{4,0},{1,5},{5,1},{2,6},{6,2},{3,7},{7,3},{8,12},{12,8},{9,1... | collective-permute-start | bytes 1769480 | tf_op jit(solution)/shard_map/ppermute | solution.py:140
  41.6 0.7 copy-start.6
  46.1 15.3 %collective-permute-start.9 = (bf16[392,128]{1,0:T(8,128)(2,1)S(1)}, bf16[392,128]{1,0:T(8,128)(2,1)S(1)}, u32[]{:S(2)}, u32[]{:S(2)}) collective-permute-start(bf16[392,128]{1,0:T(8,128)(2,1)S(1)} %get-tuple-element.32), channel_id=1, source_target_pairs={{0,2},{1,3},{2,0},{3,1},{4,6},{5,7},{6,4},{7,5},{8,10},{9,11},{10,... | collective-permute-start | bytes 301064 | tf_op jit(solution)/shard_map/ppermute | solution.py:37
  53.1 11.9 %collective-permute-start.8 = (bf16[392,128]{1,0:T(8,128)(2,1)S(1)}, bf16[392,128]{1,0:T(8,128)(2,1)S(1)}, u32[]{:S(2)}, u32[]{:S(2)}) collective-permute-start(bf16[392,128]{1,0:T(8,128)(2,1)S(1)} %get-tuple-element.33), channel_id=1, source_target_pairs={{0,3},{1,0},{2,1},{3,2},{4,7},{5,4},{6,5},{7,6},{8,11},{9,8},{10,9... | collective-permute-start | bytes 301064 | tf_op jit(solution)/shard_map/ppermute | solution.py:37
  56.1 9.0 %collective-permute-start.7 = (bf16[392,128]{1,0:T(8,128)(2,1)S(1)}, bf16[392,128]{1,0:T(8,128)(2,1)S(1)}, u32[]{:S(2)}, u32[]{:S(2)}) collective-permute-start(bf16[392,128]{1,0:T(8,128)(2,1)S(1)} %get-tuple-element.31), channel_id=1, source_target_pairs={{0,1},{1,2},{2,3},{3,0},{4,5},{5,6},{6,7},{7,4},{8,9},{9,10},{10,1... | collective-permute-start | bytes 301064 | tf_op jit(solution)/shard_map/ppermute | solution.py:37
  61.4 21.2 %all-to-all-start.1 = ((bf16[8,9,16,256]{3,2,1,0:T(8,128)(2,1)}), bf16[8,9,16,256]{3,2,1,0:T(8,128)(2,1)S(1)}, u32[]{:S(2)}, u32[]{:S(2)}) async-start(bf16[8,9,16,256]{3,2,1,0:T(8,128)(2,1)} %broadcast_in_dim.24), calls=%async_computation.1 | async-start | bytes 1179648 | tf_op jit(solution)/shard_map/all_to_all | solution.py:151
  65.2 6.5 %collective-permute-start.10 = (bf16[1,392,128]{2,1,0:T(8,128)(2,1)S(1)}, bf16[1,392,128]{2,1,0:T(8,128)(2,1)S(1)}, u32[]{:S(2)}, u32[]{:S(2)}) collective-permute-start(bf16[1,392,128]{2,1,0:T(8,128)(2,1)S(1)} %fusion.31), channel_id=1, source_target_pairs={{0,64},{64,0},{1,65},{65,1},{2,66},{66,2},{3,67},{67,3},{4,68},{68... | collective-permute-start | bytes 301064 | tf_op jit(solution)/shard_map/ppermute | solution.py:44
  71.8 7.6 %collective-permute-start.11 = (bf16[2,392,128]{2,1,0:T(8,128)(2,1)S(1)}, bf16[2,392,128]{2,1,0:T(8,128)(2,1)S(1)}, u32[]{:S(2)}, u32[]{:S(2)}) collective-permute-start(bf16[2,392,128]{2,1,0:T(8,128)(2,1)S(1)} %pad_maximum_fusion.5), channel_id=1, source_target_pairs={{0,128},{128,0},{1,129},{129,1},{2,130},{130,2},{3,131},{131,3},{4... | collective-permute-start | bytes 602120 | tf_op jit(solution)/shard_map/ppermute | solution.py:44
  82.6 3.9 %collective-permute-start.12 = (bf16[8,9,16,256]{3,2,1,0:T(8,128)(2,1)S(1)}, bf16[8,9,16,256]{3,2,1,0:T(8,128)(2,1)S(1)}, u32[]{:S(2)}, u32[]{:S(2)}) collective-permute-start(bf16[8,9,16,256]{3,2,1,0:T(8,128)(2,1)S(1)} %all-to-all-done.1), channel_id=1, source_target_pairs={{0,4},{4,0},{1,5},{5,1},{2,6},{6,2},{3,7},{7,3},{8,12},{12,8},{9,1... | collective-permute-start | bytes 1769480 | tf_op jit(solution)/shard_map/ppermute | solution.py:155
  86.7 0.7 copy-start.5
  89.7 19.4 %copy-start.2 = (f32[256]{0:T(256)S(1)}, f32[256]{0:T(256)}, u32[]{:S(2)}) copy-start(f32[256]{0:T(256)} %param.9) | copy-start | bytes 3076
